TPU v7x, 512 devices: a whole 4x8x8 slice. The times are simulated.
512 devices in a mesh: dp: 16 (over y, x_lo), seq: 32 (over x_hi, z, core).
Axes of the slice: x: 4 (x_hi: 2, x_lo: 2; x = x_hi * 2 + x_lo), y: 8, z: 8, core: 2. Of those that a mesh axis runs over, the one named last changes fastest.
Arguments:
- q_spatial: bfloat16 [16, 4096, 1536], P('dp', 'seq'), may hold values from -6 to 6
- k_spatial: bfloat16 [16, 4096, 1536], P('dp', 'seq'), may hold values from -6 to 6
- v_spatial: bfloat16 [16, 4096, 1536], P('dp', 'seq'), may hold values from -6 to 6
- q_temporal: bfloat16 [16, 4096, 1536], P('dp', 'seq'), may hold values from -6 to 6
- k_temporal: bfloat16 [16, 4096, 1536], P('dp', 'seq'), may hold values from -6 to 6
- v_temporal: bfloat16 [16, 4096, 1536], P('dp', 'seq'), may hold values from -6 to 6
- upstream: bfloat16 [16, 4096, 1536], P('dp', 'seq'), may hold values from -13.5 to 13.5
- norm_gains: float32 [4, 128], replicated, may hold values from 0.7 to 5
Outputs:
- grad_q_spatial: bfloat16 [16, 4096, 1536], P('dp', 'seq')
- grad_k_spatial: bfloat16 [16, 4096, 1536], P('dp', 'seq')
- grad_v_spatial: bfloat16 [16, 4096, 1536], P('dp', 'seq')
- grad_q_temporal: bfloat16 [16, 4096, 1536], P('dp', 'seq')
- grad_k_temporal: bfloat16 [16, 4096, 1536], P('dp', 'seq')
- grad_v_temporal: bfloat16 [16, 4096, 1536], P('dp', 'seq')
- gain_grads: float32 [4, 128], replicated
All inputs are finite; a program needn't handle non-finite values.
Results may differ from a plain program's by a relative error of at most 0.013.
The roundings to bfloat16 on the way count: a program that leaves them out, or rounds other values in their place, can miss the bound.
Values may be sent and summed in bfloat16 or wider, within the bound.
No kernel may reach another device: no remote copies, remote signals or barrier semaphores. Data moves between devices by JAX's collectives and lax.ppermute only.
A program may use at most 128 MiB of HBM per device.

v0:
```python
import math

import jax
import jax.numpy as jnp
from jax import lax
from jax.sharding import PartitionSpec as P

HEAD_DIM = 128
FRAMES = 4


EPS = 1e-06


def from_partner(block, axis, stride):
    count = lax.axis_size(axis)
    route = []
    for low in range(count):
        high = low | 1 << stride
        if high != low and high < count:
            route += [(low, high), (high, low)]
    return lax.ppermute(block, axis, route)


def norm_rows(raw, gain):
    full = raw.astype(jnp.float32)
    inv = lax.rsqrt(jnp.mean(full * full, axis=-1, keepdims=True) + EPS)
    return ((full * inv * gain).astype(jnp.bfloat16), inv)


def norm_back(raw, inv, gain, grad):
    full = raw.astype(jnp.float32)
    scaled = gain * grad
    result = inv * scaled - full * inv**3 * jnp.mean(full * scaled, axis=-1, keepdims=True)
    gain_term = jnp.sum((grad * full * inv).reshape(-1, raw.shape[-1]), axis=0)
    return (result.astype(jnp.bfloat16), gain_term)


def join(mine, other, upper, axis_dim):
    return jnp.where(
        upper, jnp.concatenate([other, mine], axis_dim), jnp.concatenate([mine, other], axis_dim)
    )


def attend_frames(normed_query_rows, normed_key_rows, value_rows, output_gradient, softmax_scale):
    logit_matrix = (
        jnp.einsum(
            "fphd,gphd->phfg",
            normed_query_rows,
            normed_key_rows,
            preferred_element_type=jnp.float32,
        )
        * softmax_scale
    )
    probs = jax.nn.softmax(logit_matrix, axis=-1)
    softmax_weights = probs.astype(jnp.bfloat16)
    probs_gradient = jnp.einsum(
        "fphd,gphd->phfg", output_gradient, value_rows, preferred_element_type=jnp.float32
    )
    delta = jnp.sum(probs * probs_gradient, axis=-1, keepdims=True)
    scores_gradient = (probs * (probs_gradient - delta) * softmax_scale).astype(jnp.bfloat16)
    normed_query_gradient = jnp.einsum(
        "phfg,gphd->fphd", scores_gradient, normed_key_rows, preferred_element_type=jnp.float32
    )
    normed_key_gradient = jnp.einsum(
        "phfg,fphd->gphd", scores_gradient, normed_query_rows, preferred_element_type=jnp.float32
    )
    value_gradient = jnp.einsum(
        "phfg,fphd->gphd", softmax_weights, output_gradient, preferred_element_type=jnp.float32
    )
    return (normed_query_gradient, normed_key_gradient, value_gradient.astype(jnp.bfloat16))


def local(
    q_spatial, k_spatial, v_spatial, q_temporal, k_temporal, v_temporal, upstream, norm_gains
):
    tok = q_spatial.shape[1]
    width = q_spatial.shape[2]
    heads = width // HEAD_DIM
    nseq = lax.axis_size("seq")
    group = nseq // FRAMES
    levels = group.bit_length() - 1
    position = lax.axis_index("seq")
    softmax_scale = HEAD_DIM ** (-0.5)

    def split(arr):
        return arr[0].reshape(tok, heads, HEAD_DIM)

    qs = split(q_spatial)
    ks = split(k_spatial)
    spatial_values = split(v_spatial)
    output_gradient = split(upstream)
    spatial_normed_queries, qs_inv = norm_rows(qs, norm_gains[0])
    spatial_normed_keys, ks_inv = norm_rows(ks, norm_gains[1])
    gathered_keys, gathered_values = (spatial_normed_keys, spatial_values)
    for bit in range(levels):
        other_keys, other_vals = from_partner((gathered_keys, gathered_values), "seq", bit)
        upper = position >> bit & 1 == 1
        gathered_keys = join(gathered_keys, other_keys, upper, 0)
        gathered_values = join(gathered_values, other_vals, upper, 0)
    logit_matrix = (
        jnp.einsum(
            "axe,sxe->xas",
            spatial_normed_queries,
            gathered_keys,
            preferred_element_type=jnp.float32,
        )
        * softmax_scale
    )
    top = jnp.max(logit_matrix, axis=-1, keepdims=True)
    expo = jnp.exp(logit_matrix - top)
    total = jnp.sum(expo, axis=-1, keepdims=True)
    probs = expo / total
    log_total = (top + jnp.log(total))[:, :, 0]
    probs_gradient = jnp.einsum(
        "axe,sxe->xas", output_gradient, gathered_values, preferred_element_type=jnp.float32
    )
    delta = jnp.sum(probs * probs_gradient, axis=-1, keepdims=True)
    scores_gradient = (probs * (probs_gradient - delta) * softmax_scale).astype(jnp.bfloat16)
    spatial_normed_query_gradient = jnp.einsum(
        "fjz,zfc->jfc", scores_gradient, gathered_keys, preferred_element_type=jnp.float32
    )
    gathered_queries, output_gradient_gathered, lse_all, delta_all = (
        spatial_normed_queries,
        output_gradient,
        log_total,
        delta[:, :, 0],
    )
    for bit in range(levels):
        other_q, other_cot, other_lse, other_delta = (
            from_partner(gathered_queries.astype(jnp.float32), "seq", bit).astype(
                gathered_queries.dtype
            ),
            from_partner(output_gradient_gathered.astype(jnp.float32), "seq", bit).astype(
                output_gradient_gathered.dtype
            ),
            from_partner(lse_all, "seq", bit),
            from_partner(delta_all, "seq", bit),
        )
        upper = position >> bit & 1 == 1
        gathered_queries = join(gathered_queries, other_q, upper, 0)
        output_gradient_gathered = join(output_gradient_gathered, other_cot, upper, 0)
        lse_all = join(lse_all, other_lse, upper, 1)
        delta_all = join(delta_all, other_delta, upper, 1)
    back_scores = (
        jnp.einsum(
            "axe,sxe->xas",
            gathered_queries,
            spatial_normed_keys,
            preferred_element_type=jnp.float32,
        )
        * softmax_scale
    )
    backward_softmax_probs = jnp.exp(back_scores - lse_all[:, :, None])
    backward_probs_gradient = jnp.einsum(
        "axe,sxe->xas", output_gradient_gathered, spatial_values, preferred_element_type=jnp.float32
    )
    backward_scores_gradient = (
        backward_softmax_probs * (backward_probs_gradient - delta_all[:, :, None]) * softmax_scale
    ).astype(jnp.bfloat16)
    spatial_normed_key_gradient = jnp.einsum(
        "roy,orj->yrj",
        backward_scores_gradient,
        gathered_queries,
        preferred_element_type=jnp.float32,
    )
    dvs = jnp.einsum(
        "roy,orj->yrj",
        backward_softmax_probs.astype(jnp.bfloat16),
        output_gradient_gathered,
        preferred_element_type=jnp.float32,
    )
    grad_qs, gain_qs = norm_back(qs, qs_inv, norm_gains[0], spatial_normed_query_gradient)
    grad_ks, gain_ks = norm_back(ks, ks_inv, norm_gains[1], spatial_normed_key_gradient)
    grad_vs = dvs.astype(jnp.bfloat16)
    pieces = tok // nseq

    def pack(arr):
        return arr[0].reshape(nseq, pieces, width)

    q_pos, k_pos, v_pos, c_pos = (
        lax.all_to_all(pack(q_temporal), "seq", split_axis=0, concat_axis=0, tiled=True),
        lax.all_to_all(pack(k_temporal), "seq", split_axis=0, concat_axis=0, tiled=True),
        lax.all_to_all(pack(v_temporal), "seq", split_axis=0, concat_axis=0, tiled=True),
        lax.all_to_all(pack(upstream), "seq", split_axis=0, concat_axis=0, tiled=True),
    )

    def framed(arr):
        return arr.reshape(FRAMES, group * pieces, heads, HEAD_DIM)

    qt = framed(q_pos)
    kt = framed(k_pos)
    qt_n, qt_inv = norm_rows(qt, norm_gains[2])
    kt_n, kt_inv = norm_rows(kt, norm_gains[3])
    dqt_n, dkt_n, dvt = attend_frames(qt_n, kt_n, framed(v_pos), framed(c_pos), softmax_scale)
    grad_qt, gain_qt = norm_back(qt, qt_inv, norm_gains[2], dqt_n)
    grad_kt, gain_kt = norm_back(kt, kt_inv, norm_gains[3], dkt_n)
    back_q, back_k, back_v = (
        lax.all_to_all(
            grad_qt.reshape(nseq, pieces, width), "seq", split_axis=0, concat_axis=0, tiled=True
        ),
        lax.all_to_all(
            grad_kt.reshape(nseq, pieces, width), "seq", split_axis=0, concat_axis=0, tiled=True
        ),
        lax.all_to_all(
            dvt.reshape(nseq, pieces, width), "seq", split_axis=0, concat_axis=0, tiled=True
        ),
    )
    grad_qt = back_q.reshape(tok, width)
    grad_kt = back_k.reshape(tok, width)
    grad_vt = back_v.reshape(tok, width)
    local_gains = jnp.stack([gain_qs, gain_ks, gain_qt, gain_kt], 0)
    summed = lax.psum(local_gains, ("dp", "seq"))
    count = lax.axis_size("dp") * nseq * tok * heads
    gains = summed / jnp.float32(math.sqrt(count))
    return (
        grad_qs.reshape(1, tok, width),
        grad_ks.reshape(1, tok, width),
        grad_vs.reshape(1, tok, width),
        grad_qt[None],
        grad_kt[None],
        grad_vt[None],
        gains,
    )


def solution(mesh):
    in_specs = (
        P("dp", "seq", None),
        P("dp", "seq", None),
        P("dp", "seq", None),
        P("dp", "seq", None),
        P("dp", "seq", None),
        P("dp", "seq", None),
        P("dp", "seq", None),
        P(),
    )
    out_specs = (
        P("dp", "seq", None),
        P("dp", "seq", None),
        P("dp", "seq", None),
        P("dp", "seq", None),
        P("dp", "seq", None),
        P("dp", "seq", None),
        P(),
    )
    return jax.shard_map(local, mesh=mesh, in_specs=in_specs, out_specs=out_specs, check_vma=False)
```

profile of v0, /device:TPU:56, one launch (start us, length us, event | category | flops | bytes accessed | tf_op | source)
XLA Modules:
  0.0 579.4 jit_solution(1528525451279784517)
XLA Ops:
  0.7 1.9 reshape_squeeze.22
  2.6 13.2 %all-to-all-start = ((bf16[32,4,1536]{2,1,0:T(4,128)(2,1)}), bf16[32,4,1536]{2,1,0:T(4,128)(2,1)S(1)}, u32[]{:S(2)}, u32[]{:S(2)}) async-start(bf16[32,4,1536]{2,1,0:T(4,128)(2,1)} %reshape_squeeze.22), calls=%async_computation | async-start | bytes 786432 | tf_op jit(solution)/shard_map/all_to_all | solution.py:182
  15.8 1.9 reshape_squeeze.25
  17.6 15.5 %all-to-all-done = bf16[32,4,1536]{2,1,0:T(4,128)(2,1)S(1)} async-done(((bf16[32,4,1536]{2,1,0:T(4,128)(2,1)}), bf16[32,4,1536]{2,1,0:T(4,128)(2,1)S(1)}, u32[]{:S(2)}, u32[]{:S(2)}) %all-to-all-start) | async-done | bytes 393248 | tf_op jit(solution)/shard_map/all_to_all | solution.py:182
  33.9 3.9 all-to-all-start.3
  40.0 15.1 %all-to-all-done.3 = bf16[32,4,1536]{2,1,0:T(4,128)(2,1)S(1)} async-done(((bf16[32,4,1536]{2,1,0:T(4,128)(2,1)}), bf16[32,4,1536]{2,1,0:T(4,128)(2,1)S(1)}, u32[]{:S(2)}, u32[]{:S(2)}) %all-to-all-start.3) | async-done | bytes 393248 | tf_op jit(solution)/shard_map/all_to_all | solution.py:184
  55.2 3.9 all-to-all-start.1
  59.2 2.1 collective-permute-start
  61.6 2.3 collective-permute-start.3
  65.8 1.5 multiply_convert_fusion.6
  67.3 2.1 collective-permute-start.6
  70.3 2.2 collective-permute-start.12
  73.4 2.3 maximum_select_fusion.9
  75.7 3.6 collective-permute-start.1
  79.3 8.8 %all-to-all-start.2 = ((bf16[32,4,1536]{2,1,0:T(4,128)(2,1)}), bf16[32,4,1536]{2,1,0:T(4,128)(2,1)}, u32[]{:S(2)}, u32[]{:S(2)}) async-start(bf16[32,4,1536]{2,1,0:T(4,128)(2,1)} %reshape_squeeze.24), calls=%async_computation.2 | async-start | bytes 786432 | tf_op jit(solution)/shard_map/all_to_all | solution.py:185
  88.2 2.3 maximum_select_fusion.10
  90.4 3.8 collective-permute-start.4
  98.9 1.5 copy.150
  100.5 1.3 multiply_multiply_fusion
  103.5 9.2 %all-to-all-done.2 = bf16[32,4,1536]{2,1,0:T(4,128)(2,1)} async-done(((bf16[32,4,1536]{2,1,0:T(4,128)(2,1)}), bf16[32,4,1536]{2,1,0:T(4,128)(2,1)}, u32[]{:S(2)}, u32[]{:S(2)}) %all-to-all-start.2) | async-done | bytes 393248 | tf_op jit(solution)/shard_map/all_to_all | solution.py:185
  112.6 2.0 reshape.231
  114.7 2.7 fusion.51
  117.4 2.0 multiply_convert_fusion.4
  120.5 4.1 fusion.80
  124.7 5.6 multiply_reduce_fusion.4
  131.3 1.6 copy.159
  132.9 3.1 subtract_convert_fusion.1
  137.0 3.9 all-to-all-start.4
  141.6 3.2 fusion.42
  145.7 3.5 maximum_select_fusion.5
  149.1 4.8 collective-permute-start.2
  155.8 2.4 all-to-all-done.4
  158.3 5.4 all-to-all-start.5
  163.7 1.6 maximum_select_fusion.11
  165.3 3.6 collective-permute-start.7
  169.0 1.7 maximum_select_fusion.12
  170.7 2.2 collective-permute-start.13
  172.9 1.8 fusion.41
  175.7 58.5 %all-to-all-done.5 = bf16[32,4,1536]{2,1,0:T(4,128)(2,1)} async-done(((bf16[32,4,1536]{2,1,0:T(4,128)(2,1)}), bf16[32,4,1536]{2,1,0:T(4,128)(2,1)}, u32[]{:S(2)}, u32[]{:S(2)}) %all-to-all-start.5) | async-done | bytes 393248 | tf_op jit(solution)/shard_map/all_to_all | solution.py:202
  234.2 6.5 %all-to-all-start.6 = ((bf16[32,4,1536]{2,1,0:T(4,128)(2,1)}), bf16[32,4,1536]{2,1,0:T(4,128)(2,1)S(1)}, u32[]{:S(2)}, u32[]{:S(2)}) async-start(bf16[32,4,1536]{2,1,0:T(4,128)(2,1)} %reshape.235), calls=%async_computation.6 | async-start | bytes 786432 | tf_op jit(solution)/shard_map/all_to_all | solution.py:205
  240.7 3.5 maximum_select_fusion.6
  244.1 4.6 collective-permute-start.5
  248.8 2.9 maximum_select_fusion.7
  251.7 2.1 collective-permute-start.8
  253.8 3.0 maximum_select_fusion.8
  256.8 4.6 collective-permute-start.14
  262.2 1.8 broadcast_in_dim_reshape.10
  264.9 4.6 multiply_reduce_fusion
  270.8 117.5 %collective-permute-done.5 = bf16[512,12,128]{0,2,1:T(8,128)(2,1)} collective-permute-done((bf16[512,12,128]{0,2,1:T(8,128)(2,1)}, bf16[512,12,128]{0,2,1:T(8,128)(2,1)}, u32[]{:S(2)}, u32[]{:S(2)}) %collective-permute-start.5) | collective-permute-done | bytes 1572896 | tf_op jit(solution)/shard_map/ppermute | solution.py:22
  388.3 8.2 %fusion.2 = (f32[12,128]{1,0:T(8,128)S(1)}, f32[12,1024,128]{1,2,0:T(8,128)}) fusion(f32[12,128]{1,0:T(8,128)S(1)} %fusion.7, f32[12,128]{1,0:T(8,128)S(1)} %get-tuple-element.62, f32[12,128,1024]{2,1,0:T(8,128)S(1)} %get-tuple-element.63, bf16[128,12,128]{0,2,1:T(8,128)(2,1)} %bitcast.5, bf16[512,12,128]{0,2,1:T(8,128)(2,1)} %maximum_select_fusion.6, ...), kind=kOutput, calls=%fused_computation.4 | convolution fusion | flops 424671744 | bytes 16140289 | tf_op jit(solution)/shard_map/axe,sxe->xas/dot_general | solution.py:115
  396.5 2.2 collective-permute-start.15
  398.7 6.3 %multiply_reduce_fusion.6 = (f32[128]{0:T(128)S(1)}, f32[128,12]{0,1:T(8,128)S(1)}, f32[128,12,128]{0,2,1:T(8,128)S(1)}) fusion(f32[128,12,128]{0,2,1:T(8,128)S(1)} %bitcast.68, f32[128,12]{0,1:T(8,128)S(1)} %get-tuple-element.57, f32[128]{0:T(128)S(1)} %copy-done.22, f32[12,1024,128]{1,2,0:T(8,128)} %get-tuple-element.65, ...), kind=kOutput, calls=%fused_computation.67 | convolution fusion | flops 428996992 | bytes 17333248 | tf_op jit(solution)/shard_map/fjz,zfc->jfc/dot_general | solution.py:120
  405.4 16.6 %collective-permute-done.8 = bf16[512,12,128]{0,2,1:T(8,128)(2,1)} collective-permute-done((bf16[512,12,128]{0,2,1:T(8,128)(2,1)}, bf16[512,12,128]{0,2,1:T(8,128)(2,1)}, u32[]{:S(2)}, u32[]{:S(2)}) %collective-permute-start.8) | collective-permute-done | bytes 1572896 | tf_op jit(solution)/shard_map/ppermute | solution.py:22
  422.0 6.8 %fusion.49 = f32[12,1024,128]{2,1,0:T(8,128)} fusion(bf16[128,12,128]{0,2,1:T(8,128)(2,1)S(1)} %copy-done.8, bf16[512,12,128]{0,2,1:T(8,128)(2,1)} %maximum_select_fusion.7, bf16[512,12,128]{0,2,1:T(8,128)(2,1)} %collective-permute-done.8, pred[]{:T(512)S(6)} %eq.12), kind=kOutput, calls=%fused_computation.82 | convolution fusion | flops 416808960 | bytes 9830401 | tf_op jit(solution)/shard_map/axe,sxe->xas/dot_general | solution.py:146
  429.8 1.9 collective-permute-start.9
  431.7 1.9 collective-permute-start.16
  433.6 3.9 collective-permute-start.10
  437.6 17.9 %collective-permute-done.16 = f32[12,256]{1,0:T(8,128)S(1)} collective-permute-done((f32[12,256]{1,0:T(8,128)S(1)}, f32[12,256]{1,0:T(8,128)S(1)}, u32[]{:S(2)}, u32[]{:S(2)}) %collective-permute-start.16) | collective-permute-done | bytes 12320 | tf_op jit(solution)/shard_map/ppermute | solution.py:22
  455.5 1.9 collective-permute-start.17
  457.4 4.8 collective-permute-start.11
  462.3 2.2 collective-permute-done.11
  464.6 9.9 %multiply_reduce_fusion.5 = (f32[128]{0:T(128)S(1)}, f32[128,12]{0,1:T(8,128)S(1)}, f32[128,12,128]{0,2,1:T(8,128)S(1)}) fusion(f32[128,12,128]{0,2,1:T(8,128)S(1)} %bitcast.64, f32[128,12]{0,1:T(8,128)S(1)} %get-tuple-element.55, f32[128]{0:T(128)S(1)} %copy-done.21, f32[12,1024,128]{2,1,0:T(8,128)} %fusion.49, f32[12,1024]{1,0:T(8,128)S(1)} %maximum_select_fusion.21, ...), kind=kOutput, calls=%fused_computation.66 | convolution fusion | flops 844233088 | bytes 14660609 | tf_op jit(solution)/shard_map/roy,orj->yrj/dot_general | solution.py:161
  475.6 6.1 %fusion.38 = bf16[12,128,128]{2,1,0:T(8,128)(2,1)S(1)} fusion(f32[12,1024,128]{2,1,0:T(8,128)} %fusion.49, f32[12,1024]{1,0:T(8,128)S(1)} %maximum_select_fusion.20, bf16[512,12,128]{0,2,1:T(8,128)(2,1)} %maximum_select_fusion.8, bf16[512,12,128]{0,2,1:T(8,128)(2,1)} %collective-permute-done.14, pred[]{:T(512)S(6)} %eq.12), kind=kOutput, calls=%fused_computation.48 | convolution fusion | flops 421724160 | bytes 9879553 | tf_op jit(solution)/shard_map/roy,orj->yrj/dot_general | solution.py:167
  482.7 96.1 %psum.7 = f32[4,128]{1,0:T(4,128)S(1)} all-reduce(f32[4,128]{1,0:T(4,128)S(1)} %pad_maximum_fusion), channel_id=1, replica_groups=mesh['dp'=16,'seq'=32] {'dp','seq'}, use_global_device_ids=true, to_apply=%region_18.19 | all-reduce | flops 512 | bytes 4096 | tf_op jit(solution)/shard_map/psum | solution.py:213
  (118 shorter events, 27.8 us)
Async XLA Ops:
  0.6 37.1 %copy-start.14 = (bf16[1,128,1536]{2,1,0:T(8,128)(2,1)S(1)}, bf16[1,128,1536]{2,1,0:T(8,128)(2,1)}, u32[]{:S(2)}) copy-start(bf16[1,128,1536]{2,1,0:T(8,128)(2,1)} %param.9) | copy-start | bytes 1179652
  0.6 37.3 %copy-start.12 = (bf16[1,128,1536]{2,1,0:T(8,128)(2,1)S(1)}, bf16[1,128,1536]{2,1,0:T(8,128)(2,1)}, u32[]{:S(2)}) copy-start(bf16[1,128,1536]{2,1,0:T(8,128)(2,1)} %param.12) | copy-start | bytes 1179652
  0.7 38.2 %copy-start.23 = (f32[4,128]{1,0:T(4,128)S(1)}, f32[4,128]{1,0:T(4,128)}, u32[]{:S(2)}) copy-start(f32[4,128]{1,0:T(4,128)} %param.15) | copy-start | bytes 6148
  2.6 30.6 %all-to-all-start = ((bf16[32,4,1536]{2,1,0:T(4,128)(2,1)}), bf16[32,4,1536]{2,1,0:T(4,128)(2,1)S(1)}, u32[]{:S(2)}, u32[]{:S(2)}) async-start(bf16[32,4,1536]{2,1,0:T(4,128)(2,1)} %reshape_squeeze.22), calls=%async_computation | async-start | bytes 786432 | tf_op jit(solution)/shard_map/all_to_all | solution.py:182
  15.7 45.6 %copy-start.13 = (bf16[1,128,1536]{2,1,0:T(8,128)(2,1)S(1)}, bf16[1,128,1536]{2,1,0:T(8,128)(2,1)}, u32[]{:S(2)}) copy-start(bf16[1,128,1536]{2,1,0:T(8,128)(2,1)} %param.10) | copy-start | bytes 1179652
  33.1 0.7 copy-start.5
  33.9 21.3 %all-to-all-start.3 = ((bf16[32,4,1536]{2,1,0:T(4,128)(2,1)}), bf16[32,4,1536]{2,1,0:T(4,128)(2,1)S(1)}, u32[]{:S(2)}, u32[]{:S(2)}) async-start(bf16[32,4,1536]{2,1,0:T(4,128)(2,1)} %reshape_squeeze.25), calls=%async_computation.3 | async-start | bytes 786432 | tf_op jit(solution)/shard_map/all_to_all | solution.py:184
  38.9 30.5 %copy-start.2 = (bf16[1,128,1536]{2,1,0:T(8,128)(2,1)S(1)}, bf16[1,128,1536]{2,1,0:T(8,128)(2,1)}, u32[]{:S(2)}) copy-start(bf16[1,128,1536]{2,1,0:T(8,128)(2,1)} %param.14) | copy-start | bytes 1179652
  39.4 19.8 %copy-start.20 = (f32[128]{0:T(128)}, f32[128]{0:T(128)S(1)}, u32[]{:S(2)}) copy-start(f32[128]{0:T(128)S(1)} %get-tuple-element.59) | copy-start | bytes 1540
  55.2 24.1 %all-to-all-start.1 = ((bf16[32,4,1536]{2,1,0:T(4,128)(2,1)}), bf16[32,4,1536]{2,1,0:T(4,128)(2,1)S(1)}, u32[]{:S(2)}, u32[]{:S(2)}) async-start(bf16[32,4,1536]{2,1,0:T(4,128)(2,1)} %reshape_squeeze.23), calls=%async_computation.1 | async-start | bytes 786432 | tf_op jit(solution)/shard_map/all_to_all | solution.py:183
  59.2 16.5 %copy-start.7 = (bf16[128,12,128]{0,2,1:T(8,128)(2,1)}, bf16[128,12,128]{0,2,1:T(8,128)(2,1)S(1)}, u32[]{:S(2)}) copy-start(bf16[128,12,128]{0,2,1:T(8,128)(2,1)S(1)} %multiply_convert_fusion.7) | copy-start | bytes 1179652
  59.2 14.2 %collective-permute-start = (bf16[128,12,128]{0,2,1:T(8,128)(2,1)S(1)}, bf16[128,12,128]{0,2,1:T(8,128)(2,1)}, u32[]{:S(2)}, u32[]{:S(2)}) collective-permute-start(bf16[128,12,128]{0,2,1:T(8,128)(2,1)S(1)} %multiply_convert_fusion.7), channel_id=1, source_target_pairs={{0,1},{1,0},{2,3},{3,2},{4,5},{5,4},{6,7},{7,6},{8,9},{9,8},{10,11... | collective-permute-start | bytes 1179656 | tf_op jit(solution)/shard_map/ppermute | solution.py:22
  61.5 26.6 %copy-start.3 = (bf16[1,128,1536]{1,2,0:T(8,128)(2,1)}, bf16[1,128,1536]{1,2,0:T(8,128)(2,1)S(1)}, u32[]{:S(2)}) copy-start(bf16[1,128,1536]{1,2,0:T(8,128)(2,1)S(1)} %copy.139) | copy-start | bytes 1179652
  61.6 26.6 %collective-permute-start.3 = (bf16[128,12,128]{0,2,1:T(8,128)(2,1)S(1)}, bf16[128,12,128]{0,2,1:T(8,128)(2,1)}, u32[]{:S(2)}, u32[]{:S(2)}) collective-permute-start(bf16[128,12,128]{0,2,1:T(8,128)(2,1)S(1)} %bitcast.70), channel_id=1, source_target_pairs={{0,1},{1,0},{2,3},{3,2},{4,5},{5,4},{6,7},{7,6},{8,9},{9,8},{10,11... | collective-permute-start | bytes 1179656 | tf_op jit(solution)/shard_map/ppermute | solution.py:22
  65.0 25.5 %copy-start = (f32[1,128,1536]{1,2,0:T(8,128)}, f32[1,128,1536]{1,2,0:T(8,128)S(1)}, u32[]{:S(2)}) copy-start(f32[1,128,1536]{1,2,0:T(8,128)S(1)} %copy.135) | copy-start | bytes 2359300
  67.3 96.4 %collective-permute-start.6 = (bf16[128,12,128]{0,2,1:T(8,128)(2,1)}, bf16[128,12,128]{0,2,1:T(8,128)(2,1)}, u32[]{:S(2)}, u32[]{:S(2)}) collective-permute-start(bf16[128,12,128]{0,2,1:T(8,128)(2,1)} %multiply_convert_fusion.6), channel_id=1, source_target_pairs={{0,1},{1,0},{2,3},{3,2},{4,5},{5,4},{6,7},{7,6},{8,9},{9,8},{10,11... | collective-permute-start | bytes 1179656 | tf_op jit(solution)/shard_map/ppermute | solution.py:22
  70.3 98.7 %collective-permute-start.12 = (bf16[128,12,128]{0,2,1:T(8,128)(2,1)}, bf16[128,12,128]{0,2,1:T(8,128)(2,1)}, u32[]{:S(2)}, u32[]{:S(2)}) collective-permute-start(bf16[128,12,128]{0,2,1:T(8,128)(2,1)} %bitcast.5), channel_id=1, source_target_pairs={{0,1},{1,0},{2,3},{3,2},{4,5},{5,4},{6,7},{7,6},{8,9},{9,8},{10,11... | collective-permute-start | bytes 1179656 | tf_op jit(solution)/shard_map/ppermute | solution.py:22
  75.7 70.0 %collective-permute-start.1 = (bf16[256,12,128]{0,2,1:T(8,128)(2,1)}, bf16[256,12,128]{0,2,1:T(8,128)(2,1)}, u32[]{:S(2)}, u32[]{:S(2)}) collective-permute-start(bf16[256,12,128]{0,2,1:T(8,128)(2,1)} %maximum_select_fusion.9), channel_id=1, source_target_pairs={{0,2},{2,0},{1,3},{3,1},{4,6},{6,4},{5,7},{7,5},{8,10},{10,8},{9,1... | collective-permute-start | bytes 2359304 | tf_op jit(solution)/shard_map/ppermute | solution.py:22
  79.3 11.2 %copy-start.6 = (bf16[32,4,1536]{2,1,0:T(4,128)(2,1)}, bf16[32,4,1536]{2,1,0:T(4,128)(2,1)S(1)}, u32[]{:S(2)}) copy-start(bf16[32,4,1536]{2,1,0:T(4,128)(2,1)S(1)} %all-to-all-done.1) | copy-start | bytes 1179652
  79.3 33.4 %all-to-all-start.2 = ((bf16[32,4,1536]{2,1,0:T(4,128)(2,1)}), bf16[32,4,1536]{2,1,0:T(4,128)(2,1)}, u32[]{:S(2)}, u32[]{:S(2)}) async-start(bf16[32,4,1536]{2,1,0:T(4,128)(2,1)} %reshape_squeeze.24), calls=%async_computation.2 | async-start | bytes 786432 | tf_op jit(solution)/shard_map/all_to_all | solution.py:185
  90.4 150.2 %collective-permute-start.4 = (bf16[256,12,128]{0,2,1:T(8,128)(2,1)}, bf16[256,12,128]{0,2,1:T(8,128)(2,1)}, u32[]{:S(2)}, u32[]{:S(2)}) collective-permute-start(bf16[256,12,128]{0,2,1:T(8,128)(2,1)} %maximum_select_fusion.10), channel_id=1, source_target_pairs={{0,2},{2,0},{1,3},{3,1},{4,6},{6,4},{5,7},{7,5},{8,10},{10,8},{9,1... | collective-permute-start | bytes 2359304 | tf_op jit(solution)/shard_map/ppermute | solution.py:22
  103.5 16.0 %copy-start.9 = (f32[4,32,12]{1,2,0:T(8,128)S(1)}, f32[4,32,12]{1,2,0:T(8,128)}, u32[]{:S(2)}) copy-start(f32[4,32,12]{1,2,0:T(8,128)} %copy.151) | copy-start | bytes 18436
  103.5 16.0 %copy-start.18 = (f32[128]{0:T(128)S(1)}, f32[128]{0:T(128)}, u32[]{:S(2)}) copy-start(f32[128]{0:T(128)} %get-tuple-element.61) | copy-start | bytes 1540
  120.5 4.1 copy-start.15
  137.0 21.3 %all-to-all-start.4 = ((bf16[32,4,1536]{2,1,0:T(4,128)(2,1)}), bf16[32,4,1536]{2,1,0:T(4,128)(2,1)S(1)}, u32[]{:S(2)}, u32[]{:S(2)}) async-start(bf16[32,4,1536]{2,1,0:T(4,128)(2,1)} %reshape.233), calls=%async_computation.4 | async-start | bytes 786432 | tf_op jit(solution)/shard_map/all_to_all | solution.py:199
  141.6 3.2 copy-start.10
  141.6 3.2 copy-start.19
  149.1 115.8 %collective-permute-start.2 = (bf16[512,12,128]{0,2,1:T(8,128)(2,1)}, bf16[512,12,128]{0,2,1:T(8,128)(2,1)}, u32[]{:S(2)}, u32[]{:S(2)}) collective-permute-start(bf16[512,12,128]{0,2,1:T(8,128)(2,1)} %maximum_select_fusion.5), channel_id=1, source_target_pairs={{0,4},{4,0},{1,5},{5,1},{2,6},{6,2},{3,7},{7,3},{8,12},{12,8},{9,1... | collective-permute-start | bytes 4718600 | tf_op jit(solution)/shard_map/ppermute | solution.py:22
  154.7 18.2 %copy-start.11 = (bf16[4,32,12,128]{3,2,1,0:T(8,128)(2,1)S(1)}, bf16[4,32,12,128]{3,2,1,0:T(8,128)(2,1)}, u32[]{:S(2)}) copy-start(bf16[4,32,12,128]{3,2,1,0:T(8,128)(2,1)} %reshape.231) | copy-start | bytes 1179652
  158.3 75.9 %all-to-all-start.5 = ((bf16[32,4,1536]{2,1,0:T(4,128)(2,1)}), bf16[32,4,1536]{2,1,0:T(4,128)(2,1)}, u32[]{:S(2)}, u32[]{:S(2)}) async-start(bf16[32,4,1536]{2,1,0:T(4,128)(2,1)} %reshape.234), calls=%async_computation.5 | async-start | bytes 786432 | tf_op jit(solution)/shard_map/all_to_all | solution.py:202
  165.3 83.4 %collective-permute-start.7 = (bf16[256,12,128]{0,2,1:T(8,128)(2,1)S(1)}, bf16[256,12,128]{0,2,1:T(8,128)(2,1)}, u32[]{:S(2)}, u32[]{:S(2)}) collective-permute-start(bf16[256,12,128]{0,2,1:T(8,128)(2,1)S(1)} %maximum_select_fusion.11), channel_id=1, source_target_pairs={{0,2},{2,0},{1,3},{3,1},{4,6},{6,4},{5,7},{7,5},{8,10},{10,8},{9,1... | collective-permute-start | bytes 2359304 | tf_op jit(solution)/shard_map/ppermute | solution.py:22
  170.7 83.2 %collective-permute-start.13 = (bf16[256,12,128]{0,2,1:T(8,128)(2,1)S(1)}, bf16[256,12,128]{0,2,1:T(8,128)(2,1)}, u32[]{:S(2)}, u32[]{:S(2)}) collective-permute-start(bf16[256,12,128]{0,2,1:T(8,128)(2,1)S(1)} %maximum_select_fusion.12), channel_id=1, source_target_pairs={{0,2},{2,0},{1,3},{3,1},{4,6},{6,4},{5,7},{7,5},{8,10},{10,8},{9,1... | collective-permute-start | bytes 2359304 | tf_op jit(solution)/shard_map/ppermute | solution.py:22
  234.2 29.9 %all-to-all-start.6 = ((bf16[32,4,1536]{2,1,0:T(4,128)(2,1)}), bf16[32,4,1536]{2,1,0:T(4,128)(2,1)S(1)}, u32[]{:S(2)}, u32[]{:S(2)}) async-start(bf16[32,4,1536]{2,1,0:T(4,128)(2,1)} %reshape.235), calls=%async_computation.6 | async-start | bytes 786432 | tf_op jit(solution)/shard_map/all_to_all | solution.py:205
  244.1 144.1 %collective-permute-start.5 = (bf16[512,12,128]{0,2,1:T(8,128)(2,1)}, bf16[512,12,128]{0,2,1:T(8,128)(2,1)}, u32[]{:S(2)}, u32[]{:S(2)}) collective-permute-start(bf16[512,12,128]{0,2,1:T(8,128)(2,1)} %maximum_select_fusion.6), channel_id=1, source_target_pairs={{0,4},{4,0},{1,5},{5,1},{2,6},{6,2},{3,7},{7,3},{8,12},{12,8},{9,1... | collective-permute-start | bytes 4718600 | tf_op jit(solution)/shard_map/ppermute | solution.py:22
  251.7 170.3 %collective-permute-start.8 = (bf16[512,12,128]{0,2,1:T(8,128)(2,1)}, bf16[512,12,128]{0,2,1:T(8,128)(2,1)}, u32[]{:S(2)}, u32[]{:S(2)}) collective-permute-start(bf16[512,12,128]{0,2,1:T(8,128)(2,1)} %maximum_select_fusion.7), channel_id=1, source_target_pairs={{0,4},{4,0},{1,5},{5,1},{2,6},{6,2},{3,7},{7,3},{8,12},{12,8},{9,1... | collective-permute-start | bytes 4718600 | tf_op jit(solution)/shard_map/ppermute | solution.py:22
  256.8 207.7 %collective-permute-start.14 = (bf16[512,12,128]{0,2,1:T(8,128)(2,1)}, bf16[512,12,128]{0,2,1:T(8,128)(2,1)}, u32[]{:S(2)}, u32[]{:S(2)}) collective-permute-start(bf16[512,12,128]{0,2,1:T(8,128)(2,1)} %maximum_select_fusion.8), channel_id=1, source_target_pairs={{0,4},{4,0},{1,5},{5,1},{2,6},{6,2},{3,7},{7,3},{8,12},{12,8},{9,1... | collective-permute-start | bytes 4718600 | tf_op jit(solution)/shard_map/ppermute | solution.py:22
  270.7 127.9 %copy-start.1 = (f32[1,128,1536]{1,2,0:T(8,128)S(1)}, f32[1,128,1536]{1,2,0:T(8,128)}, u32[]{:S(2)}) copy-start(f32[1,128,1536]{1,2,0:T(8,128)} %copy-done) | copy-start | bytes 2359300
  270.8 127.9 %copy-start.22 = (f32[128]{0:T(128)S(1)}, f32[128]{0:T(128)}, u32[]{:S(2)}) copy-start(f32[128]{0:T(128)} %get-tuple-element.60) | copy-start | bytes 1540
  396.5 35.2 %collective-permute-start.15 = (f32[12,128]{1,0:T(8,128)S(1)}, f32[12,128]{1,0:T(8,128)S(1)}, u32[]{:S(2)}, u32[]{:S(2)}) collective-permute-start(f32[12,128]{1,0:T(8,128)S(1)} %get-tuple-element.64), channel_id=1, source_target_pairs={{0,1},{1,0},{2,3},{3,2},{4,5},{5,4},{6,7},{7,6},{8,9},{9,8},{10,11... | collective-permute-start | bytes 18440 | tf_op jit(solution)/shard_map/ppermute | solution.py:22
  398.7 6.4 %copy-start.17 = (f32[128,12]{0,1:T(8,128)S(1)}, f32[128,12]{0,1:T(8,128)}, u32[]{:S(2)}) copy-start(f32[128,12]{0,1:T(8,128)} %get-tuple-element.56) | copy-start | bytes 18436
  398.7 23.3 %copy-start.8 = (bf16[128,12,128]{0,2,1:T(8,128)(2,1)S(1)}, bf16[128,12,128]{0,2,1:T(8,128)(2,1)}, u32[]{:S(2)}) copy-start(bf16[128,12,128]{0,2,1:T(8,128)(2,1)} %copy-done.7) | copy-start | bytes 1179652
  405.3 59.2 %copy-start.4 = (bf16[1,128,1536]{1,2,0:T(8,128)(2,1)S(1)}, bf16[1,128,1536]{1,2,0:T(8,128)(2,1)}, u32[]{:S(2)}) copy-start(bf16[1,128,1536]{1,2,0:T(8,128)(2,1)} %copy-done.3) | copy-start | bytes 1179652
  405.3 59.2 %copy-start.21 = (f32[128]{0:T(128)S(1)}, f32[128]{0:T(128)}, u32[]{:S(2)}) copy-start(f32[128]{0:T(128)} %copy-done.20) | copy-start | bytes 1540
  429.8 3.9 collective-permute-start.9
  431.7 23.8 %collective-permute-start.16 = (f32[12,256]{1,0:T(8,128)S(1)}, f32[12,256]{1,0:T(8,128)S(1)}, u32[]{:S(2)}, u32[]{:S(2)}) collective-permute-start(f32[12,256]{1,0:T(8,128)S(1)} %maximum_select_fusion.25), channel_id=1, source_target_pairs={{0,2},{2,0},{1,3},{3,1},{4,6},{6,4},{5,7},{7,5},{8,10},{10,8},{9,1... | collective-permute-start | bytes 36872 | tf_op jit(solution)/shard_map/ppermute | solution.py:22
  433.6 23.8 %collective-permute-start.10 = (f32[12,256]{1,0:T(8,128)S(1)}, f32[12,256]{1,0:T(8,128)S(1)}, u32[]{:S(2)}, u32[]{:S(2)}) collective-permute-start(f32[12,256]{1,0:T(8,128)S(1)} %maximum_select_fusion.24), channel_id=1, source_target_pairs={{0,2},{2,0},{1,3},{3,1},{4,6},{6,4},{5,7},{7,5},{8,10},{10,8},{9,1... | collective-permute-start | bytes 36872 | tf_op jit(solution)/shard_map/ppermute | solution.py:22
  455.5 6.8 %collective-permute-start.17 = (f32[12,512]{1,0:T(8,128)S(1)}, f32[12,512]{1,0:T(8,128)S(1)}, u32[]{:S(2)}, u32[]{:S(2)}) collective-permute-start(f32[12,512]{1,0:T(8,128)S(1)} %maximum_select_fusion.23), channel_id=1, source_target_pairs={{0,4},{4,0},{1,5},{5,1},{2,6},{6,2},{3,7},{7,3},{8,12},{12,8},{9,1... | collective-permute-start | bytes 73736 | tf_op jit(solution)/shard_map/ppermute | solution.py:22
  457.4 7.1 %collective-permute-start.11 = (f32[12,512]{1,0:T(8,128)S(1)}, f32[12,512]{1,0:T(8,128)S(1)}, u32[]{:S(2)}, u32[]{:S(2)}) collective-permute-start(f32[12,512]{1,0:T(8,128)S(1)} %maximum_select_fusion.22), channel_id=1, source_target_pairs={{0,4},{4,0},{1,5},{5,1},{2,6},{6,2},{3,7},{7,3},{8,12},{12,8},{9,1... | collective-permute-start | bytes 73736 | tf_op jit(solution)/shard_map/ppermute | solution.py:22
  464.5 10.0 %copy-start.16 = (f32[128,12]{0,1:T(8,128)S(1)}, f32[128,12]{0,1:T(8,128)}, u32[]{:S(2)}) copy-start(f32[128,12]{0,1:T(8,128)} %get-tuple-element.54) | copy-start | bytes 18436
  475.6 7.0 %copy-start.24 = (f32[128]{0:T(128)S(1)}, f32[128]{0:T(128)}, u32[]{:S(2)}) copy-start(f32[128]{0:T(128)} %get-tuple-element.42) | copy-start | bytes 1540
where the time goes:
time: 584 us; the launch traced here: 579 us
  waiting for transfers between devices  255 us (44%)
  starting transfers between devices  100 us (17%)
  blocking collectives  96.1 us (16%)
  matrix products  59.4 us (10%)
  other arithmetic  38.2 us (7%)
  local copies, waits for them, and re-layouts  29 us (5%)
    ppermute x18, waiting for transfers between devices, from_partner(): return lax.ppermute(block, axis, route)  154 us
    psum x1, blocking collectives, local(): summed = lax.psum(local_gains, ('dp', 'seq'))  96.1 us
    all_to_all x1, waiting for transfers between devices, local(): lax.all_to_all(grad_kt.reshape(nseq, pieces, width), 'seq', split_axis=0,...  58.5 us
    ppermute x18, starting transfers between devices, from_partner(): return lax.ppermute(block, axis, route)  54.6 us
    select_n x14, other arithmetic, join(): jnp.where(upper, jnp.concatenate([other, mine], axis_dim), jnp.concatenat...  20.7 us
    all_to_all x1, waiting for transfers between devices, local(): lax.all_to_all(pack(q_temporal), 'seq', split_axis=0, concat_axis=0, tile...  15.5 us
    all_to_all x1, waiting for transfers between devices, local(): lax.all_to_all(pack(v_temporal), 'seq', split_axis=0, concat_axis=0, tile...  15.1 us
    all_to_all x1, starting transfers between devices, local(): lax.all_to_all(pack(q_temporal), 'seq', split_axis=0, concat_axis=0, tile...  13.2 us
  transfers between devices with their start and end apart: 25, of which 9 were waited for; matrix products, arithmetic and copies ran while one was open for 18% of the time, Pallas kernels for 0%

commit v1 on v0

v1 whole, which is shorter than its diff:
```python
import functools
import math

import jax
import jax.numpy as jnp
from jax import lax
from jax.experimental import pallas as pl
from jax.experimental.pallas import tpu as pltpu
from jax.sharding import PartitionSpec as P

D = 128
FRAMES = 4
EPS = 1e-06
SCALE = D**-0.5
F32, BF16 = jnp.float32, jnp.bfloat16
CHIPS = 4
QBLK = 256

VMEM = pl.BlockSpec(memory_space=pltpu.VMEM)
SMEM = pl.BlockSpec(memory_space=pltpu.SMEM)


def params(mib=48):
    return pltpu.CompilerParams(vmem_limit_bytes=mib * 2**20)


def dot(a, b):
    return jnp.dot(a, b, preferred_element_type=F32)


def dot_t(a, b):
    return lax.dot_general(a, b, (((1,), (1,)), ((), ())), preferred_element_type=F32)


def inv_of(raw):
    full = raw.astype(F32)
    return lax.rsqrt(jnp.mean(full * full, axis=-1, keepdims=True) + EPS)


def norm_back(raw, inv, gain, grad):
    full = raw.astype(F32)
    scaled = gain * grad
    result = inv * scaled - full * (inv * inv * inv) * jnp.mean(full * scaled, axis=-1, keepdims=True)
    gain_term = jnp.sum(grad * full * inv, axis=0, keepdims=True)
    return result.astype(BF16), gain_term


def cols(head):
    return slice(head * D, (head + 1) * D)


def spatial_pack_kernel(q, k, v, g, out):
    for c in range(CHIPS):
        a, b, e = cols(3 * c), cols(3 * c + 1), cols(3 * c + 2)
        for i, (ref, h) in enumerate([(q, a), (k, a), (v, a), (g, a), (q, b), (g, b)]):
            out[2 * c, i] = ref[:, h]
        for i, (ref, h) in enumerate([(q, e), (k, e), (v, e), (g, e), (k, b), (v, b)]):
            out[2 * c + 1, i] = ref[:, h]


def spatial_kernel(core_ref, gains, mine, other, out, gain_out, qn, kn, knt, gg, vv, raw_q, raw_k, dq, dk, dv):
    core = core_ref[0]
    n = qn.shape[0]
    srcs = mine.shape[0]
    tok = n // srcs
    gain_q, gain_k = gains[0:1, :], gains[1:2, :]

    def flat(x):
        return x.reshape(n, D)

    def head():
        q, k = raw_q[...], raw_k[...]
        inv_q, inv_k = inv_of(q), inv_of(k)
        qn[...] = (q.astype(F32) * inv_q * gain_q).astype(BF16)
        k_n = (k.astype(F32) * inv_k * gain_k).astype(BF16)
        kn[...] = k_n
        knt[...] = k_n.astype(F32).T.astype(BF16)
        dk[...] = jnp.zeros_like(dk)
        dv[...] = jnp.zeros_like(dv)

        def step(i, carry):
            rows = pl.ds(pl.multiple_of(i * QBLK, QBLK), QBLK)
            qb, gb = qn[rows, :], gg[rows, :]
            s = dot_t(kn[...], qb) * SCALE
            e = jnp.exp(s - jnp.max(s, axis=0, keepdims=True))
            p = e * (1.0 / jnp.sum(e, axis=0, keepdims=True))
            dp = dot_t(vv[...], gb)
            delta = jnp.sum(p * dp, axis=0, keepdims=True)
            ds = (p * (dp - delta) * SCALE).astype(BF16)
            dv[...] += dot(p.astype(BF16), gb)
            dk[...] += dot(ds, qb)
            dq[rows, :] = dot(knt[...], ds).T
            return carry

        lax.fori_loop(0, n // QBLK, step, 0)
        grad_q, term_q = norm_back(q, inv_q, gain_q, dq[...])
        grad_k, term_k = norm_back(k, inv_k, gain_k, dk[...])
        return grad_q, grad_k, dv[...].astype(BF16), term_q, term_k

    def blocks(x):
        return x.reshape(srcs, tok, D)

    raw_q[...] = flat(mine[:, 0])
    raw_k[...] = flat(mine[:, 1])
    vv[...] = flat(mine[:, 2])
    gg[...] = flat(mine[:, 3])
    grad_q, grad_k, grad_v, term_q, term_k = head()
    out[:, 0:tok] = blocks(grad_q)
    out[:, tok : 2 * tok] = blocks(grad_k)
    out[:, 2 * tok : 3 * tok] = blocks(grad_v)
    gain_out[...] = jnp.zeros_like(gain_out)
    gain_out[0:1, :] = term_q
    gain_out[1:2, :] = term_k

    @pl.when(core == 0)
    def _():
        raw_q[...] = flat(mine[:, 4])
        gg[...] = flat(mine[:, 5])
        raw_k[...] = flat(other[:, 0])
        vv[...] = flat(other[:, 1])

    @pl.when(core == 1)
    def _():
        raw_k[...] = flat(mine[:, 4])
        vv[...] = flat(mine[:, 5])
        raw_q[...] = flat(other[:, 0])
        gg[...] = flat(other[:, 1])

    grad_q, grad_k, grad_v, term_q, term_k = head()
    half = tok // 2

    @pl.when(core == 0)
    def _():
        out[:, 3 * tok : 4 * tok] = blocks(grad_q)
        out[:, 4 * tok : 4 * tok + half] = blocks(grad_v)[:, :half]
        gain_out[0:1, :] += term_q

    @pl.when(core == 1)
    def _():
        out[:, 3 * tok : 4 * tok] = blocks(grad_k)
        out[:, 4 * tok : 4 * tok + half] = blocks(grad_v)[:, half:]
        gain_out[1:2, :] += term_k


def spatial_unpack_kernel(got, grad_q, grad_k, grad_v):
    tok = grad_q.shape[0]
    half = tok // 2
    for c in range(CHIPS):
        a, b, e = cols(3 * c), cols(3 * c + 1), cols(3 * c + 2)
        for core, h in ((0, a), (1, e)):
            src = 2 * c + core
            grad_q[:, h] = got[src, 0:tok]
            grad_k[:, h] = got[src, tok : 2 * tok]
            grad_v[:, h] = got[src, 2 * tok : 3 * tok]
        grad_q[:, b] = got[2 * c, 3 * tok : 4 * tok]
        grad_k[:, b] = got[2 * c + 1, 3 * tok : 4 * tok]
        grad_v[0:half, b] = got[2 * c, 4 * tok : 4 * tok + half]
        grad_v[half:tok, b] = got[2 * c + 1, 4 * tok : 4 * tok + half]


def temporal_kernel(gains, got, out, gain_out):
    frames, _, pos, width = got.shape
    n = frames * pos
    gain_q, gain_k = gains[2:3, :], gains[3:4, :]
    row = lax.broadcasted_iota(jnp.int32, (n, n), 0)
    col = lax.broadcasted_iota(jnp.int32, (n, n), 1)
    same = lax.rem(row, pos) == lax.rem(col, pos)
    sum_q, sum_k = jnp.zeros((1, D), F32), jnp.zeros((1, D), F32)
    for h in range(width // D):
        q, k, v, g = (got[:, i, :, cols(h)].reshape(n, D) for i in range(4))
        inv_q, inv_k = inv_of(q), inv_of(k)
        q_n = (q.astype(F32) * inv_q * gain_q).astype(BF16)
        k_n = (k.astype(F32) * inv_k * gain_k).astype(BF16)
        s = jnp.where(same, dot_t(k_n, q_n) * SCALE, -1e30)
        e = jnp.exp(s - jnp.max(s, axis=0, keepdims=True))
        p = e * (1.0 / jnp.sum(e, axis=0, keepdims=True))
        dp = dot_t(v, g)
        delta = jnp.sum(p * dp, axis=0, keepdims=True)
        ds = (p * (dp - delta) * SCALE).astype(BF16)
        dv = dot(p.astype(BF16), g)
        dk = dot(ds, q_n)
        dq = dot(ds.astype(F32).T.astype(BF16), k_n)
        grad_q, term_q = norm_back(q, inv_q, gain_q, dq)
        grad_k, term_k = norm_back(k, inv_k, gain_k, dk)
        sum_q += term_q
        sum_k += term_k
        for i, x in enumerate((grad_q, grad_k, dv.astype(BF16))):
            out[:, i, :, cols(h)] = x.reshape(frames, pos, D)
    gain_out[...] = jnp.zeros_like(gain_out)
    gain_out[2:3, :] = sum_q
    gain_out[3:4, :] = sum_k


def swap(x, axis, bit):
    count = lax.axis_size(axis)
    return lax.ppermute(x, axis, [(i, i ^ bit) for i in range(count)])


def sum_all(x):
    for axis in ("seq", "dp"):
        bit = 1
        while bit < lax.axis_size(axis):
            x = x + swap(x, axis, bit)
            bit *= 2
    return x


def local(q_spatial, k_spatial, v_spatial, q_temporal, k_temporal, v_temporal, upstream, norm_gains):
    tok, width = q_spatial.shape[1:]
    nseq = lax.axis_size("seq")
    group = nseq // FRAMES
    frame_groups = [[f * group + j for j in range(group)] for f in range(FRAMES)]
    place_groups = [[f * group + j for f in range(FRAMES)] for j in range(group)]
    core = (lax.axis_index("seq") & 1).astype(jnp.int32).reshape(1)

    packed = pl.pallas_call(
        spatial_pack_kernel,
        out_shape=jax.ShapeDtypeStruct((group, 6, tok, D), BF16),
        in_specs=[VMEM] * 4,
        out_specs=VMEM,
        compiler_params=params(),
        name="spatial_pack",
    )(q_spatial[0], k_spatial[0], v_spatial[0], upstream[0])
    mine = lax.all_to_all(
        packed.reshape(group, 6 * tok, D), "seq", 0, 0, axis_index_groups=frame_groups, tiled=True
    ).reshape(group, 6, tok, D)

    pos = tok // FRAMES
    shares = jnp.stack(
        [x[0].reshape(FRAMES, pos, width) for x in (q_temporal, k_temporal, v_temporal, upstream)], 1
    ).reshape(FRAMES, 4 * pos, width)
    mine, shares = lax.optimization_barrier((mine, shares))
    got = lax.all_to_all(shares, "seq", 0, 0, axis_index_groups=place_groups, tiled=True)

    other = swap(mine[:, 4:6], "seq", 1)
    n = group * tok
    spatial_grads, spatial_terms = pl.pallas_call(
        spatial_kernel,
        out_shape=(
            jax.ShapeDtypeStruct((group, 4 * tok + tok // 2, D), BF16),
            jax.ShapeDtypeStruct((8, D), F32),
        ),
        in_specs=[SMEM, VMEM, VMEM, VMEM],
        out_specs=(VMEM, VMEM),
        scratch_shapes=[
            pltpu.VMEM((n, D), BF16),
            pltpu.VMEM((n, D), BF16),
            pltpu.VMEM((D, n), BF16),
            pltpu.VMEM((n, D), BF16),
            pltpu.VMEM((n, D), BF16),
            pltpu.VMEM((n, D), BF16),
            pltpu.VMEM((n, D), BF16),
            pltpu.VMEM((n, D), F32),
            pltpu.VMEM((n, D), F32),
            pltpu.VMEM((n, D), F32),
        ],
        compiler_params=params(),
        cost_estimate=pl.CostEstimate(
            flops=20 * n * n * D, bytes_accessed=30 * n * D, transcendentals=2 * n * n
        ),
        name="spatial_backward",
    )(core, norm_gains, mine, other)
    spatial_back = lax.all_to_all(
        spatial_grads, "seq", 0, 0, axis_index_groups=frame_groups, tiled=True
    )

    temporal_grads, temporal_terms = pl.pallas_call(
        temporal_kernel,
        out_shape=(
            jax.ShapeDtypeStruct((FRAMES, 3, pos, width), BF16),
            jax.ShapeDtypeStruct((8, D), F32),
        ),
        in_specs=[VMEM, VMEM],
        out_specs=(VMEM, VMEM),
        compiler_params=params(),
        cost_estimate=pl.CostEstimate(
            flops=10 * tok * tok * width, bytes_accessed=14 * tok * width, transcendentals=tok * tok * 12
        ),
        name="temporal_backward",
    )(norm_gains, got.reshape(FRAMES, 4, pos, width))
    temporal_back = lax.all_to_all(
        temporal_grads.reshape(FRAMES, 3 * pos, width), "seq", 0, 0, axis_index_groups=place_groups, tiled=True
    ).reshape(FRAMES, 3, pos, width)

    gains = sum_all(spatial_terms + temporal_terms)[:4]
    count = lax.axis_size("dp") * nseq * tok * (width // D)
    gains = gains / jnp.float32(math.sqrt(count))

    shape = jax.ShapeDtypeStruct((tok, width), BF16)
    grad_qs, grad_ks, grad_vs = pl.pallas_call(
        spatial_unpack_kernel,
        out_shape=(shape,) * 3,
        in_specs=[VMEM],
        out_specs=(VMEM,) * 3,
        compiler_params=params(),
        name="spatial_unpack",
    )(spatial_back)
    grad_qt, grad_kt, grad_vt = (temporal_back[:, i].reshape(1, tok, width) for i in range(3))
    return (grad_qs[None], grad_ks[None], grad_vs[None], grad_qt, grad_kt, grad_vt, gains)


def solution(mesh):
    rows = P("dp", "seq", None)
    return jax.shard_map(
        local, mesh=mesh, in_specs=(rows,) * 7 + (P(),), out_specs=(rows,) * 6 + (P(),), check_vma=False
    )
```

time: 584 us -> 218 us (0.37)
  waiting for transfers between devices: 255 us -> 123 us
  blocking collectives: 96.1 us -> 0 us
  matrix products: 59.4 us -> 0 us
  starting transfers between devices: 100 us -> 62.5 us
  other arithmetic: 38.2 us -> 0.81 us
  Pallas kernels: 0 us -> 20.4 us
  local copies, waits for them, and re-layouts: 29 us -> 9.19 us
    ppermute x18 -> x10, waiting for transfers between devices: 154 us -> 44.6 us  [swap(): return lax.ppermute(x, axis, [(i, i ^ bit) for i in range(count)])]
    psum x1 -> x0, blocking collectives: 96.1 us -> none  [local(): summed = lax.psum(local_gains, ('dp', 'seq'))]
    dot_general x10 -> x0, matrix products: 55.3 us -> none  [the longest x1 9.9 us: local(): jnp.einsum('roy,orj->yrj', backward_scores_gradient, gathered_queries, pr...]
    all_to_all x7 -> x4, waiting for transfers between devices: 101 us -> 78.1 us  [the longest x1 36.3 us: local(): lax.all_to_all(packed.reshape(group, 6 * tok, D), 'seq', 0, 0, axis_index...]
    select_n x14 -> x0, other arithmetic: 20.7 us -> none  [join(): jnp.where(upper, jnp.concatenate([other, mine], axis_dim), jnp.concatenat...]
    pallas_call x0 -> x4, Pallas kernels: none -> 20.4 us  [the longest x1 14.3 us: local(): pl.pallas_call(spatial_kernel, out_shape=(jax.ShapeDtypeStruct((group, 4...]
    ppermute x18 -> x10, starting transfers between devices: 54.6 us -> 34.5 us  [swap(): return lax.ppermute(x, axis, [(i, i ^ bit) for i in range(count)])]
    all_to_all x7 -> x4, starting transfers between devices: 45.5 us -> 28 us  [the longest x1 10.2 us: local(): lax.all_to_all(shares, 'seq', 0, 0, axis_index_groups=place_groups, tiled...]
  transfers between devices with their start and end apart: 25 -> 14, of which waited for: 9 -> 13; matrix products, arithmetic and copies ran while one was open for 18% -> 1% of each run, Pallas kernels for 0% -> 9%
where the time goes in v1:
time: 218 us; the launch traced here: 217 us
  waiting for transfers between devices  123 us (56%)
  starting transfers between devices  62.5 us (29%)
  Pallas kernels  20.4 us (9%)
  local copies, waits for them, and re-layouts  9.19 us (4%)
    ppermute x10, waiting for transfers between devices, swap(): return lax.ppermute(x, axis, [(i, i ^ bit) for i in range(count)])  44.6 us
    all_to_all x1, waiting for transfers between devices, local(): lax.all_to_all(packed.reshape(group, 6 * tok, D), 'seq', 0, 0, axis_index...  36.3 us
    ppermute x10, starting transfers between devices, swap(): return lax.ppermute(x, axis, [(i, i ^ bit) for i in range(count)])  34.5 us
    all_to_all x1, waiting for transfers between devices, local(): lax.all_to_all(spatial_grads, 'seq', 0, 0, axis_index_groups=frame_groups...  24.8 us
    all_to_all x1, waiting for transfers between devices, local(): lax.all_to_all(shares, 'seq', 0, 0, axis_index_groups=place_groups, tiled...  17 us
    pallas_call x1, Pallas kernels, local(): pl.pallas_call(spatial_kernel, out_shape=(jax.ShapeDtypeStruct((group, 4...  14.3 us
    all_to_all x1, starting transfers between devices, local(): lax.all_to_all(shares, 'seq', 0, 0, axis_index_groups=place_groups, tiled...  10.2 us
    all_to_all x1, starting transfers between devices, local(): lax.all_to_all(packed.reshape(group, 6 * tok, D), 'seq', 0, 0, axis_index...  7.41 us
  transfers between devices with their start and end apart: 14, of which 13 were waited for; matrix products, arithmetic and copies ran while one was open for 1% of the time, Pallas kernels for 9%

profile of v1, /device:TPU:56, one launch (start us, length us, event | category | flops | bytes accessed | tf_op | source)
XLA Modules:
  0.0 216.5 jit_solution(9854613893123219831)
XLA Ops:
  0.6 0.0 copy-start
  0.6 1.0 copy-done
  1.6 0.0 copy-start.4
  1.6 1.0 copy-done.4
  2.6 0.0 copy-start.5
  2.6 1.0 copy-done.5
  3.6 0.0 copy-start.6
  3.6 1.0 copy-done.6
  4.6 1.4 spatial_pack.1
  6.0 0.0 copy-start.1
  6.0 0.0 copy-start.8
  6.0 0.0 copy-start.9
  6.0 0.0 copy-start.10
  6.0 7.4 %all-to-all-start = ((bf16[8,768,128]{2,1,0:T(8,128)(2,1)}), bf16[8,768,128]{2,1,0:T(8,128)(2,1)S(1)}, u32[]{:S(2)}, u32[]{:S(2)}) async-start(bf16[8,768,128]{2,1,0:T(8,128)(2,1)} %bitcast.5), calls=%async_computation | async-start | bytes 3145728 | tf_op jit(solution)/shard_map/all_to_all | solution.py:224
  13.5 0.0 copy-done.1
  13.5 0.0 copy-done.8
  13.5 0.0 copy-done.9
  13.5 0.0 copy-done.10
  13.5 0.2 pad_maximum_fusion
  13.7 1.3 copy.15
  15.0 36.3 %all-to-all-done = bf16[8,768,128]{2,1,0:T(8,128)(2,1)S(1)} async-done(((bf16[8,768,128]{2,1,0:T(8,128)(2,1)}), bf16[8,768,128]{2,1,0:T(8,128)(2,1)S(1)}, u32[]{:S(2)}, u32[]{:S(2)}) %all-to-all-start) | async-done | bytes 1572896 | tf_op jit(solution)/shard_map/all_to_all | solution.py:224
  51.3 0.0 copy-start.7
  51.3 10.2 %all-to-all-start.2 = ((bf16[4,128,1536]{2,1,0:T(8,128)(2,1)}), bf16[4,128,1536]{2,1,0:T(8,128)(2,1)S(1)}, u32[]{:S(2)}, u32[]{:S(2)}) async-start(bf16[4,128,1536]{2,1,0:T(8,128)(2,1)} %bitcast.36), calls=%async_computation.2 | async-start | bytes 3145728 | tf_op jit(solution)/shard_map/all_to_all | solution.py:233
  61.5 0.8 slice.15
  62.3 1.9 collective-permute-start
  64.2 2.2 %collective-permute-done.other = bf16[8,2,128,128]{3,2,1,0:T(8,128)(2,1)} collective-permute-done((bf16[8,2,128,128]{3,2,1,0:T(8,128)(2,1)}, bf16[8,2,128,128]{3,2,1,0:T(8,128)(2,1)}, u32[]{:S(2)}, u32[]{:S(2)}) %collective-permute-start) | collective-permute-done | bytes 524320 | tf_op jit(solution)/shard_map/ppermute | solution.py:196
  66.4 0.0 copy-done.7
  66.4 14.3 %spatial_backward.1 = (bf16[8,576,128]{2,1,0:T(8,128)(2,1)S(1)}, f32[8,128]{1,0:T(8,128)S(1)}) custom-call(s32[1]{0:T(128)} %bitcast.core_ref, f32[4,128]{1,0:T(4,128)S(1)} %copy-done.7, bf16[8,6,128,128]{3,2,1,0:T(8,128)(2,1)S(1)} %bitcast.29, bf16[8,2,128,128]{3,2,1,0:T(8,128)(2,1)} %collective-permute-done.other), custom_call_target="tpu_custom_call" | custom-call | flops 2684354560 | bytes 3932160 | tf_op jit(solution)/shard_map/spatial_backward/pallas_call | solution.py:237
  80.7 0.0 copy-start.3
  80.8 1.0 copy-done.3
  81.8 17.0 %all-to-all-done.2 = bf16[4,128,1536]{2,1,0:T(8,128)(2,1)S(1)} async-done(((bf16[4,128,1536]{2,1,0:T(8,128)(2,1)}), bf16[4,128,1536]{2,1,0:T(8,128)(2,1)S(1)}, u32[]{:S(2)}, u32[]{:S(2)}) %all-to-all-start.2) | async-done | bytes 1572896 | tf_op jit(solution)/shard_map/all_to_all | solution.py:233
  98.8 3.6 %all-to-all-start.1 = ((bf16[8,576,128]{2,1,0:T(8,128)(2,1)}), bf16[8,576,128]{2,1,0:T(8,128)(2,1)S(1)}, u32[]{:S(2)}, u32[]{:S(2)}) async-start(bf16[8,576,128]{2,1,0:T(8,128)(2,1)} %copy-done.3), calls=%async_computation.1 | async-start | bytes 2359296 | tf_op jit(solution)/shard_map/all_to_all | solution.py:263
  102.4 3.5 %temporal_backward.1 = (bf16[4,3,32,1536]{3,2,1,0:T(8,128)(2,1)S(1)}, f32[8,128]{1,0:T(8,128)S(1)}) custom-call(f32[4,128]{1,0:T(4,128)S(1)} %copy-done.7, bf16[4,4,32,1536]{3,2,1,0:T(8,128)(2,1)S(1)} %bitcast.27), custom_call_target="tpu_custom_call" | custom-call | flops 251658240 | bytes 2752512 | tf_op jit(solution)/shard_map/temporal_backward/pallas_call | solution.py:267
  105.9 0.0 copy-start.2
  105.9 1.0 copy-done.2
  106.9 24.8 %all-to-all-done.1.got = bf16[8,576,128]{2,1,0:T(8,128)(2,1)S(1)} async-done(((bf16[8,576,128]{2,1,0:T(8,128)(2,1)}), bf16[8,576,128]{2,1,0:T(8,128)(2,1)S(1)}, u32[]{:S(2)}, u32[]{:S(2)}) %all-to-all-start.1) | async-done | bytes 1179680 | tf_op jit(solution)/shard_map/all_to_all | solution.py:263
  131.7 6.9 %all-to-all-start.3 = ((bf16[4,96,1536]{2,1,0:T(8,128)(2,1)}), bf16[4,96,1536]{2,1,0:T(8,128)(2,1)S(1)}, u32[]{:S(2)}, u32[]{:S(2)}) async-start(bf16[4,96,1536]{2,1,0:T(8,128)(2,1)} %bitcast.32), calls=%async_computation.3 | async-start | bytes 2359296 | tf_op jit(solution)/shard_map/all_to_all | solution.py:281
  138.6 1.9 collective-permute-start.1
  140.5 1.1 collective-permute-done.1
  141.6 1.9 collective-permute-start.2
  143.6 20.6 %collective-permute-done.2 = f32[8,128]{1,0:T(8,128)S(1)} collective-permute-done((f32[8,128]{1,0:T(8,128)S(1)}, f32[8,128]{1,0:T(8,128)S(1)}, u32[]{:S(2)}, u32[]{:S(2)}) %collective-permute-start.2) | collective-permute-done | bytes 4128 | tf_op jit(solution)/shard_map/ppermute | solution.py:196
  164.1 4.5 %collective-permute-start.3 = (f32[8,128]{1,0:T(8,128)S(1)}, f32[8,128]{1,0:T(8,128)S(1)}, u32[]{:S(2)}, u32[]{:S(2)}) collective-permute-start(f32[8,128]{1,0:T(8,128)S(1)} %add.32), channel_id=1, source_target_pairs={{0,4},{1,5},{2,6},{3,7},{4,0},{5,1},{6,2},{7,3},{8,12},{9,13},{10,... | collective-permute-start | bytes 12296 | tf_op jit(solution)/shard_map/ppermute | solution.py:196
  168.6 1.9 collective-permute-done.3
  170.5 4.8 %collective-permute-start.4 = (f32[8,128]{1,0:T(8,128)S(1)}, f32[8,128]{1,0:T(8,128)S(1)}, u32[]{:S(2)}, u32[]{:S(2)}) collective-permute-start(f32[8,128]{1,0:T(8,128)S(1)} %add.33), channel_id=1, source_target_pairs={{0,8},{1,9},{2,10},{3,11},{4,12},{5,13},{6,14},{7,15},{8,0},{9,1},... | collective-permute-start | bytes 12296 | tf_op jit(solution)/shard_map/ppermute | solution.py:196
  175.3 4.6 %collective-permute-done.4 = f32[8,128]{1,0:T(8,128)S(1)} collective-permute-done((f32[8,128]{1,0:T(8,128)S(1)}, f32[8,128]{1,0:T(8,128)S(1)}, u32[]{:S(2)}, u32[]{:S(2)}) %collective-permute-start.4) | collective-permute-done | bytes 4128 | tf_op jit(solution)/shard_map/ppermute | solution.py:196
  179.9 5.1 %collective-permute-start.5 = (f32[8,128]{1,0:T(8,128)S(1)}, f32[8,128]{1,0:T(8,128)S(1)}, u32[]{:S(2)}, u32[]{:S(2)}) collective-permute-start(f32[8,128]{1,0:T(8,128)S(1)} %add.34), channel_id=1, source_target_pairs={{0,16},{1,17},{2,18},{3,19},{4,20},{5,21},{6,22},{7,23},{8,24},{9,... | collective-permute-start | bytes 12296 | tf_op jit(solution)/shard_map/ppermute | solution.py:196
  185.0 1.9 collective-permute-done.5
  186.9 2.5 %collective-permute-start.6 = (f32[8,128]{1,0:T(8,128)S(1)}, f32[8,128]{1,0:T(8,128)S(1)}, u32[]{:S(2)}, u32[]{:S(2)}) collective-permute-start(f32[8,128]{1,0:T(8,128)S(1)} %add.35), channel_id=1, source_target_pairs={{0,32},{32,0},{64,96},{96,64},{128,160},{160,128},{192,224},{224,1... | collective-permute-start | bytes 12296 | tf_op jit(solution)/shard_map/ppermute | solution.py:196
  189.4 3.0 %collective-permute-done.6 = f32[8,128]{1,0:T(8,128)S(1)} collective-permute-done((f32[8,128]{1,0:T(8,128)S(1)}, f32[8,128]{1,0:T(8,128)S(1)}, u32[]{:S(2)}, u32[]{:S(2)}) %collective-permute-start.6) | collective-permute-done | bytes 4128 | tf_op jit(solution)/shard_map/ppermute | solution.py:196
  192.4 3.2 %collective-permute-start.7 = (f32[8,128]{1,0:T(8,128)S(1)}, f32[8,128]{1,0:T(8,128)S(1)}, u32[]{:S(2)}, u32[]{:S(2)}) collective-permute-start(f32[8,128]{1,0:T(8,128)S(1)} %add.36), channel_id=1, source_target_pairs={{0,64},{32,96},{64,0},{96,32},{128,192},{160,224},{192,128},{224,1... | collective-permute-start | bytes 12296 | tf_op jit(solution)/shard_map/ppermute | solution.py:196
  195.7 2.2 %collective-permute-done.7 = f32[8,128]{1,0:T(8,128)S(1)} collective-permute-done((f32[8,128]{1,0:T(8,128)S(1)}, f32[8,128]{1,0:T(8,128)S(1)}, u32[]{:S(2)}, u32[]{:S(2)}) %collective-permute-start.7) | collective-permute-done | bytes 4128 | tf_op jit(solution)/shard_map/ppermute | solution.py:196
  197.9 4.0 %collective-permute-start.8 = (f32[8,128]{1,0:T(8,128)S(1)}, f32[8,128]{1,0:T(8,128)S(1)}, u32[]{:S(2)}, u32[]{:S(2)}) collective-permute-start(f32[8,128]{1,0:T(8,128)S(1)} %add.37), channel_id=1, source_target_pairs={{0,128},{32,160},{64,192},{96,224},{128,0},{160,32},{192,64},{224,... | collective-permute-start | bytes 12296 | tf_op jit(solution)/shard_map/ppermute | solution.py:196
  202.0 2.4 %collective-permute-done.8 = f32[8,128]{1,0:T(8,128)S(1)} collective-permute-done((f32[8,128]{1,0:T(8,128)S(1)}, f32[8,128]{1,0:T(8,128)S(1)}, u32[]{:S(2)}, u32[]{:S(2)}) %collective-permute-start.8) | collective-permute-done | bytes 4128 | tf_op jit(solution)/shard_map/ppermute | solution.py:196
  204.3 4.7 %collective-permute-start.9 = (f32[8,128]{1,0:T(8,128)S(1)}, f32[8,128]{1,0:T(8,128)S(1)}, u32[]{:S(2)}, u32[]{:S(2)}) collective-permute-start(f32[8,128]{1,0:T(8,128)S(1)} %add.38), channel_id=1, source_target_pairs={{0,256},{32,288},{64,320},{96,352},{128,384},{160,416},{192,448},{... | collective-permute-start | bytes 12296 | tf_op jit(solution)/shard_map/ppermute | solution.py:196
  209.0 4.7 %collective-permute-done.9 = f32[8,128]{1,0:T(8,128)S(1)} collective-permute-done((f32[8,128]{1,0:T(8,128)S(1)}, f32[8,128]{1,0:T(8,128)S(1)}, u32[]{:S(2)}, u32[]{:S(2)}) %collective-permute-start.9) | collective-permute-done | bytes 4128 | tf_op jit(solution)/shard_map/ppermute | solution.py:196
  213.7 0.6 slice_multiply_fusion
  214.3 1.2 spatial_unpack.1
  215.5 0.0 all-to-all-done.3
  215.5 1.0 fusion
  (10 shorter events, 0.0 us)
Async XLA Ops:
  0.6 1.0 copy-start
  1.6 1.0 copy-start.4
  2.6 1.0 copy-start.5
  3.6 1.0 copy-start.6
  6.0 7.4 %copy-start.1 = (bf16[1,128,1536]{2,1,0:T(8,128)(2,1)S(1)}, bf16[1,128,1536]{2,1,0:T(8,128)(2,1)}, u32[]{:S(2)}) copy-start(bf16[1,128,1536]{2,1,0:T(8,128)(2,1)} %param.14) | copy-start | bytes 1179652
  6.0 7.4 %copy-start.8 = (bf16[1,128,1536]{2,1,0:T(8,128)(2,1)S(1)}, bf16[1,128,1536]{2,1,0:T(8,128)(2,1)}, u32[]{:S(2)}) copy-start(bf16[1,128,1536]{2,1,0:T(8,128)(2,1)} %param.13) | copy-start | bytes 1179652
  6.0 7.4 %copy-start.9 = (bf16[1,128,1536]{2,1,0:T(8,128)(2,1)S(1)}, bf16[1,128,1536]{2,1,0:T(8,128)(2,1)}, u32[]{:S(2)}) copy-start(bf16[1,128,1536]{2,1,0:T(8,128)(2,1)} %param.12) | copy-start | bytes 1179652
  6.0 7.4 %copy-start.10 = (bf16[1,128,1536]{2,1,0:T(8,128)(2,1)S(1)}, bf16[1,128,1536]{2,1,0:T(8,128)(2,1)}, u32[]{:S(2)}) copy-start(bf16[1,128,1536]{2,1,0:T(8,128)(2,1)} %param.11) | copy-start | bytes 1179652
  6.0 45.2 %all-to-all-start = ((bf16[8,768,128]{2,1,0:T(8,128)(2,1)}), bf16[8,768,128]{2,1,0:T(8,128)(2,1)S(1)}, u32[]{:S(2)}, u32[]{:S(2)}) async-start(bf16[8,768,128]{2,1,0:T(8,128)(2,1)} %bitcast.5), calls=%async_computation | async-start | bytes 3145728 | tf_op jit(solution)/shard_map/all_to_all | solution.py:224
  51.3 15.1 %copy-start.7 = (f32[4,128]{1,0:T(4,128)S(1)}, f32[4,128]{1,0:T(4,128)}, u32[]{:S(2)}) copy-start(f32[4,128]{1,0:T(4,128)} %gains.3) | copy-start | bytes 6148
  51.3 47.5 %all-to-all-start.2 = ((bf16[4,128,1536]{2,1,0:T(8,128)(2,1)}), bf16[4,128,1536]{2,1,0:T(8,128)(2,1)S(1)}, u32[]{:S(2)}, u32[]{:S(2)}) async-start(bf16[4,128,1536]{2,1,0:T(8,128)(2,1)} %bitcast.36), calls=%async_computation.2 | async-start | bytes 3145728 | tf_op jit(solution)/shard_map/all_to_all | solution.py:233
  62.3 4.1 %collective-permute-start = (bf16[8,2,128,128]{3,2,1,0:T(8,128)(2,1)}, bf16[8,2,128,128]{3,2,1,0:T(8,128)(2,1)}, u32[]{:S(2)}, u32[]{:S(2)}) collective-permute-start(bf16[8,2,128,128]{3,2,1,0:T(8,128)(2,1)} %slice.15), channel_id=1, source_target_pairs={{0,1},{1,0},{2,3},{3,2},{4,5},{5,4},{6,7},{7,6},{8,9},{9,8},{10,11... | collective-permute-start | bytes 1572872 | tf_op jit(solution)/shard_map/ppermute | solution.py:196
  80.7 1.0 copy-start.3
  98.8 32.9 %all-to-all-start.1 = ((bf16[8,576,128]{2,1,0:T(8,128)(2,1)}), bf16[8,576,128]{2,1,0:T(8,128)(2,1)S(1)}, u32[]{:S(2)}, u32[]{:S(2)}) async-start(bf16[8,576,128]{2,1,0:T(8,128)(2,1)} %copy-done.3), calls=%async_computation.1 | async-start | bytes 2359296 | tf_op jit(solution)/shard_map/all_to_all | solution.py:263
  105.9 1.0 copy-start.2
  131.7 83.8 %all-to-all-start.3 = ((bf16[4,96,1536]{2,1,0:T(8,128)(2,1)}), bf16[4,96,1536]{2,1,0:T(8,128)(2,1)S(1)}, u32[]{:S(2)}, u32[]{:S(2)}) async-start(bf16[4,96,1536]{2,1,0:T(8,128)(2,1)} %bitcast.32), calls=%async_computation.3 | async-start | bytes 2359296 | tf_op jit(solution)/shard_map/all_to_all | solution.py:281
  138.6 3.0 %collective-permute-start.1 = (f32[8,128]{1,0:T(8,128)S(1)}, f32[8,128]{1,0:T(8,128)S(1)}, u32[]{:S(2)}, u32[]{:S(2)}) collective-permute-start(f32[8,128]{1,0:T(8,128)S(1)} %add.30), channel_id=1, source_target_pairs={{0,1},{1,0},{2,3},{3,2},{4,5},{5,4},{6,7},{7,6},{8,9},{9,8},{10,11... | collective-permute-start | bytes 12296 | tf_op jit(solution)/shard_map/ppermute | solution.py:196
  141.6 22.5 %collective-permute-start.2 = (f32[8,128]{1,0:T(8,128)S(1)}, f32[8,128]{1,0:T(8,128)S(1)}, u32[]{:S(2)}, u32[]{:S(2)}) collective-permute-start(f32[8,128]{1,0:T(8,128)S(1)} %add.31), channel_id=1, source_target_pairs={{0,2},{1,3},{2,0},{3,1},{4,6},{5,7},{6,4},{7,5},{8,10},{9,11},{10,... | collective-permute-start | bytes 12296 | tf_op jit(solution)/shard_map/ppermute | solution.py:196
  164.1 6.4 %collective-permute-start.3 = (f32[8,128]{1,0:T(8,128)S(1)}, f32[8,128]{1,0:T(8,128)S(1)}, u32[]{:S(2)}, u32[]{:S(2)}) collective-permute-start(f32[8,128]{1,0:T(8,128)S(1)} %add.32), channel_id=1, source_target_pairs={{0,4},{1,5},{2,6},{3,7},{4,0},{5,1},{6,2},{7,3},{8,12},{9,13},{10,... | collective-permute-start | bytes 12296 | tf_op jit(solution)/shard_map/ppermute | solution.py:196
  170.5 9.4 %collective-permute-start.4 = (f32[8,128]{1,0:T(8,128)S(1)}, f32[8,128]{1,0:T(8,128)S(1)}, u32[]{:S(2)}, u32[]{:S(2)}) collective-permute-start(f32[8,128]{1,0:T(8,128)S(1)} %add.33), channel_id=1, source_target_pairs={{0,8},{1,9},{2,10},{3,11},{4,12},{5,13},{6,14},{7,15},{8,0},{9,1},... | collective-permute-start | bytes 12296 | tf_op jit(solution)/shard_map/ppermute | solution.py:196
  179.9 7.0 %collective-permute-start.5 = (f32[8,128]{1,0:T(8,128)S(1)}, f32[8,128]{1,0:T(8,128)S(1)}, u32[]{:S(2)}, u32[]{:S(2)}) collective-permute-start(f32[8,128]{1,0:T(8,128)S(1)} %add.34), channel_id=1, source_target_pairs={{0,16},{1,17},{2,18},{3,19},{4,20},{5,21},{6,22},{7,23},{8,24},{9,... | collective-permute-start | bytes 12296 | tf_op jit(solution)/shard_map/ppermute | solution.py:196
  186.9 5.5 %collective-permute-start.6 = (f32[8,128]{1,0:T(8,128)S(1)}, f32[8,128]{1,0:T(8,128)S(1)}, u32[]{:S(2)}, u32[]{:S(2)}) collective-permute-start(f32[8,128]{1,0:T(8,128)S(1)} %add.35), channel_id=1, source_target_pairs={{0,32},{32,0},{64,96},{96,64},{128,160},{160,128},{192,224},{224,1... | collective-permute-start | bytes 12296 | tf_op jit(solution)/shard_map/ppermute | solution.py:196
  192.4 5.5 %collective-permute-start.7 = (f32[8,128]{1,0:T(8,128)S(1)}, f32[8,128]{1,0:T(8,128)S(1)}, u32[]{:S(2)}, u32[]{:S(2)}) collective-permute-start(f32[8,128]{1,0:T(8,128)S(1)} %add.36), channel_id=1, source_target_pairs={{0,64},{32,96},{64,0},{96,32},{128,192},{160,224},{192,128},{224,1... | collective-permute-start | bytes 12296 | tf_op jit(solution)/shard_map/ppermute | solution.py:196
  197.9 6.4 %collective-permute-start.8 = (f32[8,128]{1,0:T(8,128)S(1)}, f32[8,128]{1,0:T(8,128)S(1)}, u32[]{:S(2)}, u32[]{:S(2)}) collective-permute-start(f32[8,128]{1,0:T(8,128)S(1)} %add.37), channel_id=1, source_target_pairs={{0,128},{32,160},{64,192},{96,224},{128,0},{160,32},{192,64},{224,... | collective-permute-start | bytes 12296 | tf_op jit(solution)/shard_map/ppermute | solution.py:196
  204.3 9.4 %collective-permute-start.9 = (f32[8,128]{1,0:T(8,128)S(1)}, f32[8,128]{1,0:T(8,128)S(1)}, u32[]{:S(2)}, u32[]{:S(2)}) collective-permute-start(f32[8,128]{1,0:T(8,128)S(1)} %add.38), channel_id=1, source_target_pairs={{0,256},{32,288},{64,320},{96,352},{128,384},{160,416},{192,448},{... | collective-permute-start | bytes 12296 | tf_op jit(solution)/shard_map/ppermute | solution.py:196

commit v2 on v1

--- a/solution.py
+++ b/solution.py
@@ -18,9 +18,10 @@
 
 VMEM = pl.BlockSpec(memory_space=pltpu.VMEM)
 SMEM = pl.BlockSpec(memory_space=pltpu.SMEM)
-
-
-def params(mib=48):
+HBM = pl.BlockSpec(memory_space=pltpu.HBM)
+
+
+def params(mib=32):
     return pltpu.CompilerParams(vmem_limit_bytes=mib * 2**20)
 
 
@@ -47,6 +48,79 @@
 
 def cols(head):
     return slice(head * D, (head + 1) * D)
+
+
+def move(plan, name, outs, scalars, *operands, src=VMEM, dst=VMEM):
+    n_in = len(operands)
+    inside = src is VMEM and dst is VMEM
+    count = len(plan(scalars, [Shape(x) for x in operands], [Shape(x) for x in outs]))
+
+    def kernel(ids, *refs):
+        outs_at = n_in + len(outs)
+        pairs = plan([ids[i] for i in range(ids.shape[0])], refs[:n_in], refs[n_in:outs_at])
+        if inside:
+            for a, b in pairs:
+                b[...] = a[...]
+            return
+        copies = [pltpu.make_async_copy(a, b, refs[-1].at[i]) for i, (a, b) in enumerate(pairs)]
+        for c in copies:
+            c.start()
+        for c in copies:
+            c.wait()
+
+    return pl.pallas_call(
+        kernel,
+        out_shape=tuple(outs),
+        in_specs=[SMEM] + [src] * n_in,
+        out_specs=(dst,) * len(outs),
+        scratch_shapes=[] if inside else [pltpu.SemaphoreType.DMA((count,))],
+        compiler_params=params(16),
+        cost_estimate=pl.CostEstimate(flops=0, bytes_accessed=0, transcendentals=0),
+        name=name,
+    )(jnp.stack(scalars), *operands)
+
+
+class Shape:
+    def __init__(self, x):
+        self.shape = x.shape
+
+    @property
+    def at(self):
+        return self
+
+    def __getitem__(self, _):
+        return self
+
+
+def quarter(which, pos):
+    return pl.ds(pl.multiple_of(which * pos, pos), pos)
+
+
+def temporal_pack(ids, ins, outs):
+    (frame,) = ids
+    keep, to_x, to_z = outs
+    pos = keep.shape[1]
+    places = ((keep, 0), (to_x.at[0], 2), (to_x.at[1], 3), (to_z, 1))
+    return [
+        (x.at[quarter(frame ^ d, pos)], target.at[i])
+        for target, d in places
+        for i, x in enumerate(ins)
+    ]
+
+
+def forward_pack(ids, ins, outs):
+    mine, from_x = ins
+    return [(mine, outs[0].at[0]), (from_x.at[1], outs[0].at[1])]
+
+
+def temporal_unpack(ids, ins, outs):
+    (frame,) = ids
+    pos = ins[0].shape[1]
+    return [
+        (r.at[i], x.at[quarter(frame ^ d, pos)])
+        for d, r in enumerate(ins)
+        for i, x in enumerate(outs)
+    ]
 
 
 def spatial_pack_kernel(q, k, v, g, out):
@@ -158,16 +232,19 @@
         grad_v[half:tok, b] = got[2 * c + 1, 4 * tok : 4 * tok + half]
 
 
-def temporal_kernel(gains, got, out, gain_out):
-    frames, _, pos, width = got.shape
-    n = frames * pos
+def temporal_kernel(gains, spatial_terms, own, from_x, from_z, own_out, out1, out2, out3, gain_out):
+    ins = (own, from_z.at[0], from_x.at[0], from_z.at[1])
+    outs = (own_out, out1, out2, out3)
+    _, pos, width = own.shape
+    n = FRAMES * pos
     gain_q, gain_k = gains[2:3, :], gains[3:4, :]
     row = lax.broadcasted_iota(jnp.int32, (n, n), 0)
     col = lax.broadcasted_iota(jnp.int32, (n, n), 1)
     same = lax.rem(row, pos) == lax.rem(col, pos)
     sum_q, sum_k = jnp.zeros((1, D), F32), jnp.zeros((1, D), F32)
     for h in range(width // D):
-        q, k, v, g = (got[:, i, :, cols(h)].reshape(n, D) for i in range(4))
+        at = slice(h * D, (h + 1) * D)
+        q, k, v, g = (jnp.concatenate([x[i, :, at] for x in ins], axis=0) for i in range(4))
         inv_q, inv_k = inv_of(q), inv_of(k)
         q_n = (q.astype(F32) * inv_q * gain_q).astype(BF16)
         k_n = (k.astype(F32) * inv_k * gain_k).astype(BF16)
@@ -185,61 +262,61 @@
         sum_q += term_q
         sum_k += term_k
         for i, x in enumerate((grad_q, grad_k, dv.astype(BF16))):
-            out[:, i, :, cols(h)] = x.reshape(frames, pos, D)
-    gain_out[...] = jnp.zeros_like(gain_out)
+            for d, out in enumerate(outs):
+                out[i, :, at] = x[d * pos : (d + 1) * pos]
+    gain_out[...] = spatial_terms[...]
     gain_out[2:3, :] = sum_q
     gain_out[3:4, :] = sum_k
 
 
-def swap(x, axis, bit):
-    count = lax.axis_size(axis)
-    return lax.ppermute(x, axis, [(i, i ^ bit) for i in range(count)])
-
-
-def sum_all(x):
-    for axis in ("seq", "dp"):
-        bit = 1
-        while bit < lax.axis_size(axis):
-            x = x + swap(x, axis, bit)
-            bit *= 2
-    return x
+def swap(x, bits, axis="seq"):
+    return lax.ppermute(x, axis, [(i, i ^ bits) for i in range(lax.axis_size(axis))])
+
+
+def sum_over_z(x, groups):
+    all_of = jnp.broadcast_to(x[None], (len(groups[0]), *x.shape))
+    return jnp.sum(lax.all_to_all(all_of, "seq", 0, 0, axis_index_groups=groups, tiled=True), axis=0)
 
 
 def local(q_spatial, k_spatial, v_spatial, q_temporal, k_temporal, v_temporal, upstream, norm_gains):
     tok, width = q_spatial.shape[1:]
     nseq = lax.axis_size("seq")
     group = nseq // FRAMES
+    n = group * tok
+    pos = tok // FRAMES
+    at = lax.axis_index("seq").astype(jnp.int32)
+    core, frame = at & 1, at // group
     frame_groups = [[f * group + j for j in range(group)] for f in range(FRAMES)]
-    place_groups = [[f * group + j for f in range(FRAMES)] for j in range(group)]
-    core = (lax.axis_index("seq") & 1).astype(jnp.int32).reshape(1)
+
+    def shape(*dims):
+        return jax.ShapeDtypeStruct(dims, BF16)
+
+    def exchange(x):
+        return lax.all_to_all(x, "seq", 0, 0, axis_index_groups=frame_groups, tiled=True)
 
     packed = pl.pallas_call(
         spatial_pack_kernel,
-        out_shape=jax.ShapeDtypeStruct((group, 6, tok, D), BF16),
+        out_shape=shape(group, 6, tok, D),
         in_specs=[VMEM] * 4,
         out_specs=VMEM,
-        compiler_params=params(),
+        compiler_params=params(16),
         name="spatial_pack",
     )(q_spatial[0], k_spatial[0], v_spatial[0], upstream[0])
-    mine = lax.all_to_all(
-        packed.reshape(group, 6 * tok, D), "seq", 0, 0, axis_index_groups=frame_groups, tiled=True
-    ).reshape(group, 6, tok, D)
-
-    pos = tok // FRAMES
-    shares = jnp.stack(
-        [x[0].reshape(FRAMES, pos, width) for x in (q_temporal, k_temporal, v_temporal, upstream)], 1
-    ).reshape(FRAMES, 4 * pos, width)
-    mine, shares = lax.optimization_barrier((mine, shares))
-    got = lax.all_to_all(shares, "seq", 0, 0, axis_index_groups=place_groups, tiled=True)
-
-    other = swap(mine[:, 4:6], "seq", 1)
-    n = group * tok
+    mine = exchange(packed.reshape(group, 6 * tok, D)).reshape(group, 6, tok, D)
+    keep, to_x, to_z = move(
+        temporal_pack, "temporal_pack",
+        [shape(4, pos, width), shape(2, 4, pos, width), shape(4, pos, width)], [frame],
+        q_temporal[0], k_temporal[0], v_temporal[0], upstream[0], src=HBM,
+    )
+    from_x = swap(to_x, 2 * group)
+    (to_z,) = move(forward_pack, "forward_pack", [shape(2, 4, pos, width)], [frame], to_z, from_x)
+    mine, to_z = lax.optimization_barrier((mine, to_z))
+    from_z = swap(to_z, group)
+
+    other = swap(mine[:, 4:6], 1)
     spatial_grads, spatial_terms = pl.pallas_call(
         spatial_kernel,
-        out_shape=(
-            jax.ShapeDtypeStruct((group, 4 * tok + tok // 2, D), BF16),
-            jax.ShapeDtypeStruct((8, D), F32),
-        ),
+        out_shape=(shape(group, 4 * tok + tok // 2, D), jax.ShapeDtypeStruct((8, D), F32)),
         in_specs=[SMEM, VMEM, VMEM, VMEM],
         out_specs=(VMEM, VMEM),
         scratch_shapes=[
@@ -255,48 +332,44 @@
             pltpu.VMEM((n, D), F32),
         ],
         compiler_params=params(),
-        cost_estimate=pl.CostEstimate(
-            flops=20 * n * n * D, bytes_accessed=30 * n * D, transcendentals=2 * n * n
-        ),
+        cost_estimate=pl.CostEstimate(flops=0, bytes_accessed=0, transcendentals=0),
         name="spatial_backward",
-    )(core, norm_gains, mine, other)
-    spatial_back = lax.all_to_all(
-        spatial_grads, "seq", 0, 0, axis_index_groups=frame_groups, tiled=True
-    )
-
-    temporal_grads, temporal_terms = pl.pallas_call(
+    )(core.reshape(1), norm_gains, mine, other)
+    back = exchange(spatial_grads)
+
+    piece = shape(3, pos, width)
+    own, o1, o2, o3, terms = pl.pallas_call(
         temporal_kernel,
-        out_shape=(
-            jax.ShapeDtypeStruct((FRAMES, 3, pos, width), BF16),
-            jax.ShapeDtypeStruct((8, D), F32),
-        ),
-        in_specs=[VMEM, VMEM],
-        out_specs=(VMEM, VMEM),
+        out_shape=(piece,) * 4 + (jax.ShapeDtypeStruct((8, D), F32),),
+        in_specs=[VMEM] * 5,
+        out_specs=(VMEM,) * 5,
         compiler_params=params(),
         cost_estimate=pl.CostEstimate(
-            flops=10 * tok * tok * width, bytes_accessed=14 * tok * width, transcendentals=tok * tok * 12
+            flops=10000 * tok * tok * width, bytes_accessed=14 * tok * width, transcendentals=tok * tok * 12
         ),
         name="temporal_backward",
-    )(norm_gains, got.reshape(FRAMES, 4, pos, width))
-    temporal_back = lax.all_to_all(
-        temporal_grads.reshape(FRAMES, 3 * pos, width), "seq", 0, 0, axis_index_groups=place_groups, tiled=True
-    ).reshape(FRAMES, 3, pos, width)
-
-    gains = sum_all(spatial_terms + temporal_terms)[:4]
+    )(norm_gains, spatial_terms, keep, from_x, from_z)
+    b1, b2, b3 = swap(o1, group), swap(o2, 2 * group), swap(o3, 3 * group)
+    for axis, bits in (("dp", 1), ("seq", nseq // 2), ("dp", 2), ("dp", 4), ("dp", 8), ("seq", 1)):
+        terms = terms + swap(terms, bits, axis)
+    terms, back, b1, b3 = lax.optimization_barrier((terms, back, b1, b3))
+    z_groups = [[x * nseq // 2 + c + i for i in range(0, nseq // 2, 2)] for x in range(2) for c in range(2)]
+    gains = sum_over_z(terms, z_groups)[:4]
+    grad_qt, grad_kt, grad_vt = move(
+        temporal_unpack, "temporal_unpack", [shape(tok, width)] * 3, [frame], own, b1, b2, b3, dst=HBM
+    )
+    grad_qs, grad_ks, grad_vs = pl.pallas_call(
+        spatial_unpack_kernel,
+        out_shape=(shape(tok, width),) * 3,
+        in_specs=[VMEM],
+        out_specs=(VMEM,) * 3,
+        compiler_params=params(16),
+        name="spatial_unpack",
+    )(back)
+
     count = lax.axis_size("dp") * nseq * tok * (width // D)
     gains = gains / jnp.float32(math.sqrt(count))
-
-    shape = jax.ShapeDtypeStruct((tok, width), BF16)
-    grad_qs, grad_ks, grad_vs = pl.pallas_call(
-        spatial_unpack_kernel,
-        out_shape=(shape,) * 3,
-        in_specs=[VMEM],
-        out_specs=(VMEM,) * 3,
-        compiler_params=params(),
-        name="spatial_unpack",
-    )(spatial_back)
-    grad_qt, grad_kt, grad_vt = (temporal_back[:, i].reshape(1, tok, width) for i in range(3))
-    return (grad_qs[None], grad_ks[None], grad_vs[None], grad_qt, grad_kt, grad_vt, gains)
+    return (grad_qs[None], grad_ks[None], grad_vs[None], grad_qt[None], grad_kt[None], grad_vt[None], gains)
 
 
 def solution(mesh):

time: 218 us -> 170 us (0.78)
  waiting for transfers between devices: 123 us -> 64.1 us
  starting transfers between devices: 62.5 us -> 70.5 us
  Pallas kernels: 20.4 us -> 27.2 us
  local copies, waits for them, and re-layouts: 9.19 us -> 5.45 us
    all_to_all x4 -> x3, waiting for transfers between devices: 78.1 us -> 16.6 us  [the longest x2 12.2 us: exchange(): lax.all_to_all(x, 'seq', 0, 0, axis_index_groups=frame_groups, tiled=True)]
    ppermute x10 -> x12, starting transfers between devices: 34.5 us -> 51.6 us  [swap(): lax.ppermute(x, axis, [(i, i ^ bits) for i in range(lax.axis_size(axis))])]
    all_to_all x4 -> x3, starting transfers between devices: 28 us -> 18.9 us  [the longest x2 11.7 us: exchange(): lax.all_to_all(x, 'seq', 0, 0, axis_index_groups=frame_groups, tiled=True)]
    pallas_call x4 -> x7, Pallas kernels: 20.4 us -> 27.2 us  [the longest x1 15.3 us: local(): pl.pallas_call(spatial_kernel, out_shape=(shape(group, 4 * tok + tok // 2...]
    ppermute x10 -> x12, waiting for transfers between devices: 44.6 us -> 47.5 us  [swap(): lax.ppermute(x, axis, [(i, i ^ bits) for i in range(lax.axis_size(axis))])]
    unnamed x22 -> x18, local copies, waits for them, and re-layouts: 6.03 us -> 4 us
  transfers between devices with their start and end apart: 14 -> 15, of which waited for: 13 -> 11; matrix products, arithmetic and copies ran while one was open for 1% -> 1% of each run, Pallas kernels for 9% -> 15%
where the time goes in v2:
time: 170 us; the launch traced here: 169 us
  starting transfers between devices  70.5 us (41%)
  waiting for transfers between devices  64.1 us (38%)
  Pallas kernels  27.2 us (16%)
  local copies, waits for them, and re-layouts  5.45 us (3%)
    ppermute x12, starting transfers between devices, swap(): lax.ppermute(x, axis, [(i, i ^ bits) for i in range(lax.axis_size(axis))])  51.6 us
    ppermute x12, waiting for transfers between devices, swap(): lax.ppermute(x, axis, [(i, i ^ bits) for i in range(lax.axis_size(axis))])  47.5 us
    pallas_call x1, Pallas kernels, local(): pl.pallas_call(spatial_kernel, out_shape=(shape(group, 4 * tok + tok // 2...  15.3 us
    all_to_all x2, waiting for transfers between devices, exchange(): lax.all_to_all(x, 'seq', 0, 0, axis_index_groups=frame_groups, tiled=True)  12.2 us
    all_to_all x2, starting transfers between devices, exchange(): lax.all_to_all(x, 'seq', 0, 0, axis_index_groups=frame_groups, tiled=True)  11.7 us
    all_to_all x1, starting transfers between devices, sum_over_z(): lax.all_to_all(all_of, 'seq', 0, 0, axis_index_groups=groups, tiled=True)  7.28 us
    pallas_call x1, Pallas kernels, local(): pl.pallas_call(temporal_kernel, out_shape=(piece,) * 4 + (jax.ShapeDtypeS...  4.65 us
    all_to_all x1, waiting for transfers between devices, sum_over_z(): lax.all_to_all(all_of, 'seq', 0, 0, axis_index_groups=groups, tiled=True)  4.44 us
  transfers between devices with their start and end apart: 15, of which 11 were waited for; matrix products, arithmetic and copies ran while one was open for 1% of the time, Pallas kernels for 15%

profile of v2, /device:TPU:56, one launch (start us, length us, event | category | flops | bytes accessed | tf_op | source)
XLA Modules:
  0.0 168.8 jit_solution(17932829382845256592)
XLA Ops:
  0.6 0.0 copy-start
  0.6 1.0 copy-done
  1.6 0.0 copy-start.2
  1.6 1.0 copy-done.2
  2.6 0.0 copy-start.3
  2.6 1.0 copy-done.3
  3.6 0.0 copy-start.4
  3.6 1.0 copy-done.4
  4.6 1.5 spatial_pack.1
  6.1 0.0 copy-start.1
  6.1 0.0 copy-start.5
  6.1 0.0 copy-start.6
  6.1 0.0 copy-start.7
  6.1 7.4 %all-to-all-start = ((bf16[8,768,128]{2,1,0:T(8,128)(2,1)}), bf16[8,768,128]{2,1,0:T(8,128)(2,1)S(1)}, u32[]{:S(2)}, u32[]{:S(2)}) async-start(bf16[8,768,128]{2,1,0:T(8,128)(2,1)} %bitcast.5), calls=%async_computation | async-start | bytes 3145728 | tf_op jit(solution)/shard_map/all_to_all | solution.py:295
  13.5 0.0 copy-done.1
  13.5 0.0 copy-done.5
  13.5 0.0 copy-done.6
  13.5 0.0 copy-done.7
  13.5 2.2 %temporal_pack.1 = (bf16[4,32,1536]{2,1,0:T(8,128)(2,1)S(1)}, bf16[2,4,32,1536]{3,2,1,0:T(8,128)(2,1)S(1)}, bf16[4,32,1536]{2,1,0:T(8,128)(2,1)S(1)}) custom-call(s32[1]{0:T(128)} %bitcast.7.ids, bf16[128,1536]{1,0:T(8,128)(2,1)S(1)} %bitcast.24, bf16[128,1536]{1,0:T(8,128)(2,1)S(1)} %bitcast.25, bf16[128,1536]{1,0:T(8,128)(2,1)S(1)} %bitcast.26, ...), custom_call_target="tpu_custom_call" | custom-call | tf_op jit(solution)/shard_map/temporal_pack/pallas_call | solution.py:71
  15.7 0.0 copy-start.8
  15.8 4.9 %collective-permute-start = (bf16[2,4,32,1536]{3,2,1,0:T(8,128)(2,1)S(1)}, bf16[2,4,32,1536]{3,2,1,0:T(8,128)(2,1)S(1)}, u32[]{:S(2)}, u32[]{:S(2)}) collective-permute-start(bf16[2,4,32,1536]{3,2,1,0:T(8,128)(2,1)S(1)} %get-tuple-element.30), channel_id=1, source_target_pairs={{0,16},{1,17},{2,18},{3,19},{4,20},{5,21},{6,22},{7,23},{8,24},{9,... | collective-permute-start | bytes 2359304 | tf_op jit(solution)/shard_map/ppermute | solution.py:273
  20.7 18.4 %collective-permute-done.refs_1_.from_x = bf16[2,4,32,1536]{3,2,1,0:T(8,128)(2,1)S(1)} collective-permute-done((bf16[2,4,32,1536]{3,2,1,0:T(8,128)(2,1)S(1)}, bf16[2,4,32,1536]{3,2,1,0:T(8,128)(2,1)S(1)}, u32[]{:S(2)}, u32[]{:S(2)}) %collective-permute-start) | collective-permute-done | bytes 786464 | tf_op jit(solution)/shard_map/ppermute | solution.py:273
  39.1 0.1 forward_pack.1
  39.2 12.2 %all-to-all-done = bf16[8,768,128]{2,1,0:T(8,128)(2,1)S(1)} async-done(((bf16[8,768,128]{2,1,0:T(8,128)(2,1)}), bf16[8,768,128]{2,1,0:T(8,128)(2,1)S(1)}, u32[]{:S(2)}, u32[]{:S(2)}) %all-to-all-start) | async-done | bytes 1572896 | tf_op jit(solution)/shard_map/all_to_all | solution.py:295
  51.3 8.2 %collective-permute-start.2 = (bf16[2,4,32,1536]{3,2,1,0:T(8,128)(2,1)S(1)}, bf16[2,4,32,1536]{3,2,1,0:T(8,128)(2,1)}, u32[]{:S(2)}, u32[]{:S(2)}) collective-permute-start(bf16[2,4,32,1536]{3,2,1,0:T(8,128)(2,1)S(1)} %forward_pack.1), channel_id=1, source_target_pairs={{0,8},{1,9},{2,10},{3,11},{4,12},{5,13},{6,14},{7,15},{8,0},{9,1},... | collective-permute-start | bytes 2359304 | tf_op jit(solution)/shard_map/ppermute | solution.py:273
  59.5 0.8 slice.6
  60.4 1.9 %collective-permute-start.1 = (bf16[8,2,128,128]{3,2,1,0:T(8,128)(2,1)}, bf16[8,2,128,128]{3,2,1,0:T(8,128)(2,1)}, u32[]{:S(2)}, u32[]{:S(2)}) collective-permute-start(bf16[8,2,128,128]{3,2,1,0:T(8,128)(2,1)} %slice.6), channel_id=1, source_target_pairs={{0,1},{1,0},{2,3},{3,2},{4,5},{5,4},{6,7},{7,6},{8,9},{9,8},{10,11... | collective-permute-start | bytes 1572872 | tf_op jit(solution)/shard_map/ppermute | solution.py:273
  62.3 2.2 %collective-permute-done.1.other = bf16[8,2,128,128]{3,2,1,0:T(8,128)(2,1)} collective-permute-done((bf16[8,2,128,128]{3,2,1,0:T(8,128)(2,1)}, bf16[8,2,128,128]{3,2,1,0:T(8,128)(2,1)}, u32[]{:S(2)}, u32[]{:S(2)}) %collective-permute-start.1) | collective-permute-done | bytes 524320 | tf_op jit(solution)/shard_map/ppermute | solution.py:273
  64.5 0.0 copy-done.8
  64.5 15.3 %spatial_backward.1 = (bf16[8,576,128]{2,1,0:T(8,128)(2,1)}, f32[8,128]{1,0:T(8,128)S(1)}) custom-call(s32[1]{0:T(128)} %bitcast.core_ref, f32[4,128]{1,0:T(4,128)S(1)} %copy-done.8, bf16[8,6,128,128]{3,2,1,0:T(8,128)(2,1)S(1)} %bitcast.18, bf16[8,2,128,128]{3,2,1,0:T(8,128)(2,1)} %collective-permute-done.1.other), custom_call_target="tpu_custom_call" | custom-call | tf_op jit(solution)/shard_map/spatial_backward/pallas_call | solution.py:317
  79.8 4.3 %all-to-all-start.1 = ((bf16[8,576,128]{2,1,0:T(8,128)(2,1)}), bf16[8,576,128]{2,1,0:T(8,128)(2,1)}, u32[]{:S(2)}, u32[]{:S(2)}) async-start(bf16[8,576,128]{2,1,0:T(8,128)(2,1)} %get-tuple-element.36), calls=%async_computation.1 | async-start | bytes 2359296 | tf_op jit(solution)/shard_map/all_to_all | solution.py:295
  84.1 11.3 %collective-permute-done.2.from_z = bf16[2,4,32,1536]{3,2,1,0:T(8,128)(2,1)} collective-permute-done((bf16[2,4,32,1536]{3,2,1,0:T(8,128)(2,1)S(1)}, bf16[2,4,32,1536]{3,2,1,0:T(8,128)(2,1)}, u32[]{:S(2)}, u32[]{:S(2)}) %collective-permute-start.2) | collective-permute-done | bytes 786464 | tf_op jit(solution)/shard_map/ppermute | solution.py:273
  95.4 4.6 %temporal_backward.1 = (bf16[3,32,1536]{2,1,0:T(8,128)(2,1)S(1)}, bf16[3,32,1536]{2,1,0:T(8,128)(2,1)S(1)}, bf16[3,32,1536]{2,1,0:T(8,128)(2,1)S(1)}, bf16[3,32,1536]{2,1,0:T(8,128)(2,1)S(1)}, f32[8,128]{1,0:T(8,128)S(1)}) custom-call(f32[4,128]{1,0:T(4,128)S(1)} %copy-done.8, f32[8,128]{1,0:T(8,128)S(1)} %get-tuple-element.32.spatial_terms, ...), custom_call_target="tpu_custom_call" | custom-call | flops 251658240000 | bytes 2752512 | tf_op jit(solution)/shard_map/temporal_backward/pallas_call | solution.py:341
  100.1 5.0 %collective-permute-start.9 = (bf16[3,32,1536]{2,1,0:T(8,128)(2,1)S(1)}, bf16[3,32,1536]{2,1,0:T(8,128)(2,1)S(1)}, u32[]{:S(2)}, u32[]{:S(2)}) collective-permute-start(bf16[3,32,1536]{2,1,0:T(8,128)(2,1)S(1)} %get-tuple-element.37), channel_id=1, source_target_pairs={{0,8},{1,9},{2,10},{3,11},{4,12},{5,13},{6,14},{7,15},{8,0},{9,1},... | collective-permute-start | bytes 884744 | tf_op jit(solution)/shard_map/ppermute | solution.py:273
  105.1 7.2 %collective-permute-start.10 = (bf16[3,32,1536]{2,1,0:T(8,128)(2,1)S(1)}, bf16[3,32,1536]{2,1,0:T(8,128)(2,1)S(1)}, u32[]{:S(2)}, u32[]{:S(2)}) collective-permute-start(bf16[3,32,1536]{2,1,0:T(8,128)(2,1)S(1)} %get-tuple-element.38), channel_id=1, source_target_pairs={{0,24},{1,25},{2,26},{3,27},{4,28},{5,29},{6,30},{7,31},{8,16},{9,... | collective-permute-start | bytes 884744 | tf_op jit(solution)/shard_map/ppermute | solution.py:273
  112.3 2.4 %collective-permute-start.11 = (bf16[3,32,1536]{2,1,0:T(8,128)(2,1)S(1)}, bf16[3,32,1536]{2,1,0:T(8,128)(2,1)S(1)}, u32[]{:S(2)}, u32[]{:S(2)}) collective-permute-start(bf16[3,32,1536]{2,1,0:T(8,128)(2,1)S(1)} %get-tuple-element.45), channel_id=1, source_target_pairs={{0,16},{1,17},{2,18},{3,19},{4,20},{5,21},{6,22},{7,23},{8,24},{9,... | collective-permute-start | bytes 884744 | tf_op jit(solution)/shard_map/ppermute | solution.py:273
  114.7 3.4 %collective-permute-start.3 = (f32[8,128]{1,0:T(8,128)S(1)}, f32[8,128]{1,0:T(8,128)S(1)}, u32[]{:S(2)}, u32[]{:S(2)}) collective-permute-start(f32[8,128]{1,0:T(8,128)S(1)} %get-tuple-element.35), channel_id=1, source_target_pairs={{0,32},{32,0},{64,96},{96,64},{128,160},{160,128},{192,224},{224,1... | collective-permute-start | bytes 12296 | tf_op jit(solution)/shard_map/ppermute | solution.py:273
  118.1 2.8 %collective-permute-done.3 = f32[8,128]{1,0:T(8,128)S(1)} collective-permute-done((f32[8,128]{1,0:T(8,128)S(1)}, f32[8,128]{1,0:T(8,128)S(1)}, u32[]{:S(2)}, u32[]{:S(2)}) %collective-permute-start.3) | collective-permute-done | bytes 4128 | tf_op jit(solution)/shard_map/ppermute | solution.py:273
  120.9 4.6 %collective-permute-start.4 = (f32[8,128]{1,0:T(8,128)S(1)}, f32[8,128]{1,0:T(8,128)S(1)}, u32[]{:S(2)}, u32[]{:S(2)}) collective-permute-start(f32[8,128]{1,0:T(8,128)S(1)} %add.19), channel_id=1, source_target_pairs={{0,16},{1,17},{2,18},{3,19},{4,20},{5,21},{6,22},{7,23},{8,24},{9,... | collective-permute-start | bytes 12296 | tf_op jit(solution)/shard_map/ppermute | solution.py:273
  125.6 2.4 %collective-permute-done.4 = f32[8,128]{1,0:T(8,128)S(1)} collective-permute-done((f32[8,128]{1,0:T(8,128)S(1)}, f32[8,128]{1,0:T(8,128)S(1)}, u32[]{:S(2)}, u32[]{:S(2)}) %collective-permute-start.4) | collective-permute-done | bytes 4128 | tf_op jit(solution)/shard_map/ppermute | solution.py:273
  127.9 3.2 %collective-permute-start.5 = (f32[8,128]{1,0:T(8,128)S(1)}, f32[8,128]{1,0:T(8,128)S(1)}, u32[]{:S(2)}, u32[]{:S(2)}) collective-permute-start(f32[8,128]{1,0:T(8,128)S(1)} %add.20), channel_id=1, source_target_pairs={{0,64},{32,96},{64,0},{96,32},{128,192},{160,224},{192,128},{224,1... | collective-permute-start | bytes 12296 | tf_op jit(solution)/shard_map/ppermute | solution.py:273
  131.2 2.2 %collective-permute-done.5 = f32[8,128]{1,0:T(8,128)S(1)} collective-permute-done((f32[8,128]{1,0:T(8,128)S(1)}, f32[8,128]{1,0:T(8,128)S(1)}, u32[]{:S(2)}, u32[]{:S(2)}) %collective-permute-start.5) | collective-permute-done | bytes 4128 | tf_op jit(solution)/shard_map/ppermute | solution.py:273
  133.4 4.0 %collective-permute-start.6 = (f32[8,128]{1,0:T(8,128)S(1)}, f32[8,128]{1,0:T(8,128)S(1)}, u32[]{:S(2)}, u32[]{:S(2)}) collective-permute-start(f32[8,128]{1,0:T(8,128)S(1)} %add.21), channel_id=1, source_target_pairs={{0,128},{32,160},{64,192},{96,224},{128,0},{160,32},{192,64},{224,... | collective-permute-start | bytes 12296 | tf_op jit(solution)/shard_map/ppermute | solution.py:273
  137.5 2.3 %collective-permute-done.6 = f32[8,128]{1,0:T(8,128)S(1)} collective-permute-done((f32[8,128]{1,0:T(8,128)S(1)}, f32[8,128]{1,0:T(8,128)S(1)}, u32[]{:S(2)}, u32[]{:S(2)}) %collective-permute-start.6) | collective-permute-done | bytes 4128 | tf_op jit(solution)/shard_map/ppermute | solution.py:273
  139.8 4.7 %collective-permute-start.7 = (f32[8,128]{1,0:T(8,128)S(1)}, f32[8,128]{1,0:T(8,128)S(1)}, u32[]{:S(2)}, u32[]{:S(2)}) collective-permute-start(f32[8,128]{1,0:T(8,128)S(1)} %add.22), channel_id=1, source_target_pairs={{0,256},{32,288},{64,320},{96,352},{128,384},{160,416},{192,448},{... | collective-permute-start | bytes 12296 | tf_op jit(solution)/shard_map/ppermute | solution.py:273
  144.5 4.7 %collective-permute-done.7 = f32[8,128]{1,0:T(8,128)S(1)} collective-permute-done((f32[8,128]{1,0:T(8,128)S(1)}, f32[8,128]{1,0:T(8,128)S(1)}, u32[]{:S(2)}, u32[]{:S(2)}) %collective-permute-start.7) | collective-permute-done | bytes 4128 | tf_op jit(solution)/shard_map/ppermute | solution.py:273
  149.2 1.9 %collective-permute-start.8 = (f32[8,128]{1,0:T(8,128)S(1)}, f32[8,128]{1,0:T(8,128)S(1)}, u32[]{:S(2)}, u32[]{:S(2)}) collective-permute-start(f32[8,128]{1,0:T(8,128)S(1)} %add.23), channel_id=1, source_target_pairs={{0,1},{1,0},{2,3},{3,2},{4,5},{5,4},{6,7},{7,6},{8,9},{9,8},{10,11... | collective-permute-start | bytes 12296 | tf_op jit(solution)/shard_map/ppermute | solution.py:273
  151.1 1.1 collective-permute-done.8
  152.3 0.0 collective-permute-done.9.refs_1_
  152.3 0.0 collective-permute-done.10.refs_3_
  152.3 0.0 all-to-all-done.1.got
  152.3 0.6 broadcast_in_dim.30
  152.9 7.3 %all-to-all-start.2 = ((f32[8,8,128]{2,1,0:T(8,128)}), f32[8,8,128]{2,1,0:T(8,128)S(1)}, u32[]{:S(2)}, u32[]{:S(2)}) async-start(f32[8,8,128]{2,1,0:T(8,128)} %broadcast_in_dim.30), calls=%async_computation.2 | async-start | bytes 65536 | tf_op jit(solution)/shard_map/all_to_all | solution.py:278
  160.2 2.5 %spatial_unpack.1 = (bf16[128,1536]{1,0:T(8,128)(2,1)}, bf16[128,1536]{1,0:T(8,128)(2,1)}, bf16[128,1536]{1,0:T(8,128)(2,1)}) custom-call(bf16[8,576,128]{2,1,0:T(8,128)(2,1)} %all-to-all-done.1.got), custom_call_target="tpu_custom_call" | custom-call | tf_op jit(solution)/shard_map/spatial_unpack/pallas_call | solution.py:361
  162.7 0.0 collective-permute-done.11.refs_2_
  162.7 1.1 temporal_unpack.1
  163.8 4.4 %all-to-all-done.2 = f32[8,8,128]{2,1,0:T(8,128)S(1)} async-done(((f32[8,8,128]{2,1,0:T(8,128)}), f32[8,8,128]{2,1,0:T(8,128)S(1)}, u32[]{:S(2)}, u32[]{:S(2)}) %all-to-all-start.2) | async-done | bytes 32800 | tf_op jit(solution)/shard_map/all_to_all | solution.py:278
  168.2 0.6 slice_multiply_fusion
  (7 shorter events, 0.0 us)
Async XLA Ops:
  0.6 1.0 copy-start
  1.6 1.0 copy-start.2
  2.6 1.0 copy-start.3
  3.6 1.0 copy-start.4
  6.1 7.4 %copy-start.1 = (bf16[1,128,1536]{2,1,0:T(8,128)(2,1)S(1)}, bf16[1,128,1536]{2,1,0:T(8,128)(2,1)}, u32[]{:S(2)}) copy-start(bf16[1,128,1536]{2,1,0:T(8,128)(2,1)} %param.14) | copy-start | bytes 1179652
  6.1 7.4 %copy-start.5 = (bf16[1,128,1536]{2,1,0:T(8,128)(2,1)S(1)}, bf16[1,128,1536]{2,1,0:T(8,128)(2,1)}, u32[]{:S(2)}) copy-start(bf16[1,128,1536]{2,1,0:T(8,128)(2,1)} %param.11) | copy-start | bytes 1179652
  6.1 7.4 %copy-start.6 = (bf16[1,128,1536]{2,1,0:T(8,128)(2,1)S(1)}, bf16[1,128,1536]{2,1,0:T(8,128)(2,1)}, u32[]{:S(2)}) copy-start(bf16[1,128,1536]{2,1,0:T(8,128)(2,1)} %param.12) | copy-start | bytes 1179652
  6.1 7.4 %copy-start.7 = (bf16[1,128,1536]{2,1,0:T(8,128)(2,1)S(1)}, bf16[1,128,1536]{2,1,0:T(8,128)(2,1)}, u32[]{:S(2)}) copy-start(bf16[1,128,1536]{2,1,0:T(8,128)(2,1)} %param.13) | copy-start | bytes 1179652
  6.1 45.2 %all-to-all-start = ((bf16[8,768,128]{2,1,0:T(8,128)(2,1)}), bf16[8,768,128]{2,1,0:T(8,128)(2,1)S(1)}, u32[]{:S(2)}, u32[]{:S(2)}) async-start(bf16[8,768,128]{2,1,0:T(8,128)(2,1)} %bitcast.5), calls=%async_computation | async-start | bytes 3145728 | tf_op jit(solution)/shard_map/all_to_all | solution.py:295
  15.7 48.8 %copy-start.8 = (f32[4,128]{1,0:T(4,128)S(1)}, f32[4,128]{1,0:T(4,128)}, u32[]{:S(2)}) copy-start(f32[4,128]{1,0:T(4,128)} %gains.3) | copy-start | bytes 6148
  15.8 23.3 %collective-permute-start = (bf16[2,4,32,1536]{3,2,1,0:T(8,128)(2,1)S(1)}, bf16[2,4,32,1536]{3,2,1,0:T(8,128)(2,1)S(1)}, u32[]{:S(2)}, u32[]{:S(2)}) collective-permute-start(bf16[2,4,32,1536]{3,2,1,0:T(8,128)(2,1)S(1)} %get-tuple-element.30), channel_id=1, source_target_pairs={{0,16},{1,17},{2,18},{3,19},{4,20},{5,21},{6,22},{7,23},{8,24},{9,... | collective-permute-start | bytes 2359304 | tf_op jit(solution)/shard_map/ppermute | solution.py:273
  51.3 44.1 %collective-permute-start.2 = (bf16[2,4,32,1536]{3,2,1,0:T(8,128)(2,1)S(1)}, bf16[2,4,32,1536]{3,2,1,0:T(8,128)(2,1)}, u32[]{:S(2)}, u32[]{:S(2)}) collective-permute-start(bf16[2,4,32,1536]{3,2,1,0:T(8,128)(2,1)S(1)} %forward_pack.1), channel_id=1, source_target_pairs={{0,8},{1,9},{2,10},{3,11},{4,12},{5,13},{6,14},{7,15},{8,0},{9,1},... | collective-permute-start | bytes 2359304 | tf_op jit(solution)/shard_map/ppermute | solution.py:273
  60.4 4.1 %collective-permute-start.1 = (bf16[8,2,128,128]{3,2,1,0:T(8,128)(2,1)}, bf16[8,2,128,128]{3,2,1,0:T(8,128)(2,1)}, u32[]{:S(2)}, u32[]{:S(2)}) collective-permute-start(bf16[8,2,128,128]{3,2,1,0:T(8,128)(2,1)} %slice.6), channel_id=1, source_target_pairs={{0,1},{1,0},{2,3},{3,2},{4,5},{5,4},{6,7},{7,6},{8,9},{9,8},{10,11... | collective-permute-start | bytes 1572872 | tf_op jit(solution)/shard_map/ppermute | solution.py:273
  79.8 72.4 %all-to-all-start.1 = ((bf16[8,576,128]{2,1,0:T(8,128)(2,1)}), bf16[8,576,128]{2,1,0:T(8,128)(2,1)}, u32[]{:S(2)}, u32[]{:S(2)}) async-start(bf16[8,576,128]{2,1,0:T(8,128)(2,1)} %get-tuple-element.36), calls=%async_computation.1 | async-start | bytes 2359296 | tf_op jit(solution)/shard_map/all_to_all | solution.py:295
  100.1 52.2 %collective-permute-start.9 = (bf16[3,32,1536]{2,1,0:T(8,128)(2,1)S(1)}, bf16[3,32,1536]{2,1,0:T(8,128)(2,1)S(1)}, u32[]{:S(2)}, u32[]{:S(2)}) collective-permute-start(bf16[3,32,1536]{2,1,0:T(8,128)(2,1)S(1)} %get-tuple-element.37), channel_id=1, source_target_pairs={{0,8},{1,9},{2,10},{3,11},{4,12},{5,13},{6,14},{7,15},{8,0},{9,1},... | collective-permute-start | bytes 884744 | tf_op jit(solution)/shard_map/ppermute | solution.py:273
  105.1 47.2 %collective-permute-start.10 = (bf16[3,32,1536]{2,1,0:T(8,128)(2,1)S(1)}, bf16[3,32,1536]{2,1,0:T(8,128)(2,1)S(1)}, u32[]{:S(2)}, u32[]{:S(2)}) collective-permute-start(bf16[3,32,1536]{2,1,0:T(8,128)(2,1)S(1)} %get-tuple-element.38), channel_id=1, source_target_pairs={{0,24},{1,25},{2,26},{3,27},{4,28},{5,29},{6,30},{7,31},{8,16},{9,... | collective-permute-start | bytes 884744 | tf_op jit(solution)/shard_map/ppermute | solution.py:273
  112.3 50.4 %collective-permute-start.11 = (bf16[3,32,1536]{2,1,0:T(8,128)(2,1)S(1)}, bf16[3,32,1536]{2,1,0:T(8,128)(2,1)S(1)}, u32[]{:S(2)}, u32[]{:S(2)}) collective-permute-start(bf16[3,32,1536]{2,1,0:T(8,128)(2,1)S(1)} %get-tuple-element.45), channel_id=1, source_target_pairs={{0,16},{1,17},{2,18},{3,19},{4,20},{5,21},{6,22},{7,23},{8,24},{9,... | collective-permute-start | bytes 884744 | tf_op jit(solution)/shard_map/ppermute | solution.py:273
  114.7 6.2 %collective-permute-start.3 = (f32[8,128]{1,0:T(8,128)S(1)}, f32[8,128]{1,0:T(8,128)S(1)}, u32[]{:S(2)}, u32[]{:S(2)}) collective-permute-start(f32[8,128]{1,0:T(8,128)S(1)} %get-tuple-element.35), channel_id=1, source_target_pairs={{0,32},{32,0},{64,96},{96,64},{128,160},{160,128},{192,224},{224,1... | collective-permute-start | bytes 12296 | tf_op jit(solution)/shard_map/ppermute | solution.py:273
  120.9 7.0 %collective-permute-start.4 = (f32[8,128]{1,0:T(8,128)S(1)}, f32[8,128]{1,0:T(8,128)S(1)}, u32[]{:S(2)}, u32[]{:S(2)}) collective-permute-start(f32[8,128]{1,0:T(8,128)S(1)} %add.19), channel_id=1, source_target_pairs={{0,16},{1,17},{2,18},{3,19},{4,20},{5,21},{6,22},{7,23},{8,24},{9,... | collective-permute-start | bytes 12296 | tf_op jit(solution)/shard_map/ppermute | solution.py:273
  127.9 5.5 %collective-permute-start.5 = (f32[8,128]{1,0:T(8,128)S(1)}, f32[8,128]{1,0:T(8,128)S(1)}, u32[]{:S(2)}, u32[]{:S(2)}) collective-permute-start(f32[8,128]{1,0:T(8,128)S(1)} %add.20), channel_id=1, source_target_pairs={{0,64},{32,96},{64,0},{96,32},{128,192},{160,224},{192,128},{224,1... | collective-permute-start | bytes 12296 | tf_op jit(solution)/shard_map/ppermute | solution.py:273
  133.4 6.4 %collective-permute-start.6 = (f32[8,128]{1,0:T(8,128)S(1)}, f32[8,128]{1,0:T(8,128)S(1)}, u32[]{:S(2)}, u32[]{:S(2)}) collective-permute-start(f32[8,128]{1,0:T(8,128)S(1)} %add.21), channel_id=1, source_target_pairs={{0,128},{32,160},{64,192},{96,224},{128,0},{160,32},{192,64},{224,... | collective-permute-start | bytes 12296 | tf_op jit(solution)/shard_map/ppermute | solution.py:273
  139.8 9.4 %collective-permute-start.7 = (f32[8,128]{1,0:T(8,128)S(1)}, f32[8,128]{1,0:T(8,128)S(1)}, u32[]{:S(2)}, u32[]{:S(2)}) collective-permute-start(f32[8,128]{1,0:T(8,128)S(1)} %add.22), channel_id=1, source_target_pairs={{0,256},{32,288},{64,320},{96,352},{128,384},{160,416},{192,448},{... | collective-permute-start | bytes 12296 | tf_op jit(solution)/shard_map/ppermute | solution.py:273
  149.2 3.0 %collective-permute-start.8 = (f32[8,128]{1,0:T(8,128)S(1)}, f32[8,128]{1,0:T(8,128)S(1)}, u32[]{:S(2)}, u32[]{:S(2)}) collective-permute-start(f32[8,128]{1,0:T(8,128)S(1)} %add.23), channel_id=1, source_target_pairs={{0,1},{1,0},{2,3},{3,2},{4,5},{5,4},{6,7},{7,6},{8,9},{9,8},{10,11... | collective-permute-start | bytes 12296 | tf_op jit(solution)/shard_map/ppermute | solution.py:273
  152.9 15.3 %all-to-all-start.2 = ((f32[8,8,128]{2,1,0:T(8,128)}), f32[8,8,128]{2,1,0:T(8,128)S(1)}, u32[]{:S(2)}, u32[]{:S(2)}) async-start(f32[8,8,128]{2,1,0:T(8,128)} %broadcast_in_dim.30), calls=%async_computation.2 | async-start | bytes 65536 | tf_op jit(solution)/shard_map/all_to_all | solution.py:278

commit v3 on v2

--- a/solution.py
+++ b/solution.py
@@ -115,10 +115,12 @@
 
 def temporal_unpack(ids, ins, outs):
     (frame,) = ids
-    pos = ins[0].shape[1]
+    own, from_x, from_z = ins
+    pos = own.shape[1]
+    places = ((own, 0), (from_x.at[0], 2), (from_z.at[0], 1), (from_z.at[1], 3))
     return [
         (r.at[i], x.at[quarter(frame ^ d, pos)])
-        for d, r in enumerate(ins)
+        for r, d in places
         for i, x in enumerate(outs)
     ]
 
@@ -232,9 +234,9 @@
         grad_v[half:tok, b] = got[2 * c + 1, 4 * tok : 4 * tok + half]
 
 
-def temporal_kernel(gains, spatial_terms, own, from_x, from_z, own_out, out1, out2, out3, gain_out):
-    ins = (own, from_z.at[0], from_x.at[0], from_z.at[1])
-    outs = (own_out, out1, out2, out3)
+def temporal_kernel(gains, spatial_terms, own, from_x, from_z, own_out, to_x, to_z, gain_out):
+    ins = (own, from_x.at[0], from_z.at[0], from_z.at[1])
+    outs = (own_out, to_x.at[0], to_z, to_x.at[1])
     _, pos, width = own.shape
     n = FRAMES * pos
     gain_q, gain_k = gains[2:3, :], gains[3:4, :]
@@ -273,9 +275,13 @@
     return lax.ppermute(x, axis, [(i, i ^ bits) for i in range(lax.axis_size(axis))])
 
 
-def sum_over_z(x, groups):
-    all_of = jnp.broadcast_to(x[None], (len(groups[0]), *x.shape))
-    return jnp.sum(lax.all_to_all(all_of, "seq", 0, 0, axis_index_groups=groups, tiled=True), axis=0)
+def add_swapped(x, bits, axis):
+    return x + swap(x, bits, axis)
+
+
+def sum_over(x, axis):
+    all_of = jnp.broadcast_to(x[None], (lax.axis_size(axis), *x.shape))
+    return jnp.sum(lax.all_to_all(all_of, axis, 0, 0, tiled=True), axis=0)
 
 
 def local(q_spatial, k_spatial, v_spatial, q_temporal, k_temporal, v_temporal, upstream, norm_gains):
@@ -338,25 +344,27 @@
     back = exchange(spatial_grads)
 
     piece = shape(3, pos, width)
-    own, o1, o2, o3, terms = pl.pallas_call(
+    own, to_x, to_z, terms = pl.pallas_call(
         temporal_kernel,
-        out_shape=(piece,) * 4 + (jax.ShapeDtypeStruct((8, D), F32),),
+        out_shape=(piece, shape(2, 3, pos, width), piece, jax.ShapeDtypeStruct((8, D), F32)),
         in_specs=[VMEM] * 5,
-        out_specs=(VMEM,) * 5,
+        out_specs=(VMEM,) * 4,
         compiler_params=params(),
         cost_estimate=pl.CostEstimate(
             flops=10000 * tok * tok * width, bytes_accessed=14 * tok * width, transcendentals=tok * tok * 12
         ),
         name="temporal_backward",
     )(norm_gains, spatial_terms, keep, from_x, from_z)
-    b1, b2, b3 = swap(o1, group), swap(o2, 2 * group), swap(o3, 3 * group)
-    for axis, bits in (("dp", 1), ("seq", nseq // 2), ("dp", 2), ("dp", 4), ("dp", 8), ("seq", 1)):
-        terms = terms + swap(terms, bits, axis)
-    terms, back, b1, b3 = lax.optimization_barrier((terms, back, b1, b3))
-    z_groups = [[x * nseq // 2 + c + i for i in range(0, nseq // 2, 2)] for x in range(2) for c in range(2)]
-    gains = sum_over_z(terms, z_groups)[:4]
+    back_x = swap(to_x, 2 * group)
+    terms = add_swapped(add_swapped(terms, 2, "dp"), 4, "dp")
+    to_z, terms = lax.optimization_barrier((to_z, terms))
+    (to_z,) = move(forward_pack, "forward_back_pack", [shape(2, 3, pos, width)], [frame], to_z, back_x)
+    back_z = swap(to_z, group)
+    terms = add_swapped(add_swapped(terms, 8, "dp"), 1, "dp")
+    terms, back = lax.optimization_barrier((terms, back))
+    gains = sum_over(terms, "seq")[:4]
     grad_qt, grad_kt, grad_vt = move(
-        temporal_unpack, "temporal_unpack", [shape(tok, width)] * 3, [frame], own, b1, b2, b3, dst=HBM
+        temporal_unpack, "temporal_unpack", [shape(tok, width)] * 3, [frame], own, back_x, back_z, dst=HBM
     )
     grad_qs, grad_ks, grad_vs = pl.pallas_call(
         spatial_unpack_kernel,

time: 170 us -> 158 us (0.929)
  starting transfers between devices: 70.5 us -> 57.8 us
    ppermute x12 -> x9, starting transfers between devices: 51.6 us -> 39.5 us  [swap(): lax.ppermute(x, axis, [(i, i ^ bits) for i in range(lax.axis_size(axis))])]
    ppermute x12 -> x9, waiting for transfers between devices: 47.5 us -> 46.6 us  [swap(): lax.ppermute(x, axis, [(i, i ^ bits) for i in range(lax.axis_size(axis))])]
  transfers between devices with their start and end apart: 15 -> 12, of which waited for: 11 -> 10; matrix products, arithmetic and copies ran while one was open for 1% -> 1% of each run, Pallas kernels for 15% -> 16%
where the time goes in v3:
time: 158 us; the launch traced here: 157 us
  waiting for transfers between devices  64.8 us (41%)
  starting transfers between devices  57.8 us (37%)
  Pallas kernels  27.3 us (17%)
  local copies, waits for them, and re-layouts  5.5 us (3%)
    ppermute x9, waiting for transfers between devices, swap(): lax.ppermute(x, axis, [(i, i ^ bits) for i in range(lax.axis_size(axis))])  46.6 us
    ppermute x9, starting transfers between devices, swap(): lax.ppermute(x, axis, [(i, i ^ bits) for i in range(lax.axis_size(axis))])  39.5 us
    pallas_call x1, Pallas kernels, local(): pl.pallas_call(spatial_kernel, out_shape=(shape(group, 4 * tok + tok // 2...  15.3 us
    all_to_all x2, waiting for transfers between devices, exchange(): lax.all_to_all(x, 'seq', 0, 0, axis_index_groups=frame_groups, tiled=True)  12.2 us
    all_to_all x2, starting transfers between devices, exchange(): lax.all_to_all(x, 'seq', 0, 0, axis_index_groups=frame_groups, tiled=True)  11.7 us
    all_to_all x1, starting transfers between devices, sum_over(): return jnp.sum(lax.all_to_all(all_of, axis, 0, 0, tiled=True), axis=0)  6.68 us
    all_to_all x1, waiting for transfers between devices, sum_over(): return jnp.sum(lax.all_to_all(all_of, axis, 0, 0, tiled=True), axis=0)  5.98 us
    pallas_call x1, Pallas kernels, local(): pl.pallas_call(temporal_kernel, out_shape=(piece, shape(2, 3, pos, width)...  4.65 us
  transfers between devices with their start and end apart: 12, of which 10 were waited for; matrix products, arithmetic and copies ran while one was open for 1% of the time, Pallas kernels for 16%

profile of v3, /device:TPU:56, one launch (start us, length us, event | category | flops | bytes accessed | tf_op | source)
XLA Modules:
  0.0 156.8 jit_solution(453293182870395195)
XLA Ops:
  0.6 0.0 copy-start
  0.6 1.0 copy-done
  1.6 0.0 copy-start.2
  1.6 1.0 copy-done.2
  2.6 0.0 copy-start.3
  2.6 1.0 copy-done.3
  3.6 0.0 copy-start.4
  3.6 1.0 copy-done.4
  4.6 1.5 spatial_pack.1
  6.1 0.0 copy-start.1
  6.1 0.0 copy-start.5
  6.1 0.0 copy-start.6
  6.1 0.0 copy-start.7
  6.1 7.4 %all-to-all-start = ((bf16[8,768,128]{2,1,0:T(8,128)(2,1)}), bf16[8,768,128]{2,1,0:T(8,128)(2,1)S(1)}, u32[]{:S(2)}, u32[]{:S(2)}) async-start(bf16[8,768,128]{2,1,0:T(8,128)(2,1)} %bitcast.5), calls=%async_computation | async-start | bytes 3145728 | tf_op jit(solution)/shard_map/all_to_all | solution.py:301
  13.5 0.0 copy-done.1
  13.5 0.0 copy-done.5
  13.5 0.0 copy-done.6
  13.5 0.0 copy-done.7
  13.5 2.2 %temporal_pack.1 = (bf16[4,32,1536]{2,1,0:T(8,128)(2,1)S(1)}, bf16[2,4,32,1536]{3,2,1,0:T(8,128)(2,1)S(1)}, bf16[4,32,1536]{2,1,0:T(8,128)(2,1)S(1)}) custom-call(s32[1]{0:T(128)} %bitcast.7.ids, bf16[128,1536]{1,0:T(8,128)(2,1)S(1)} %bitcast.24, bf16[128,1536]{1,0:T(8,128)(2,1)S(1)} %bitcast.25, bf16[128,1536]{1,0:T(8,128)(2,1)S(1)} %bitcast.26, ...), custom_call_target="tpu_custom_call" | custom-call | tf_op jit(solution)/shard_map/temporal_pack/pallas_call | solution.py:71
  15.7 0.0 copy-start.8
  15.8 4.9 %collective-permute-start = (bf16[2,4,32,1536]{3,2,1,0:T(8,128)(2,1)S(1)}, bf16[2,4,32,1536]{3,2,1,0:T(8,128)(2,1)S(1)}, u32[]{:S(2)}, u32[]{:S(2)}) collective-permute-start(bf16[2,4,32,1536]{3,2,1,0:T(8,128)(2,1)S(1)} %get-tuple-element.29), channel_id=1, source_target_pairs={{0,16},{1,17},{2,18},{3,19},{4,20},{5,21},{6,22},{7,23},{8,24},{9,... | collective-permute-start | bytes 2359304 | tf_op jit(solution)/shard_map/ppermute | solution.py:275
  20.7 18.4 %collective-permute-done.refs_1_.from_x = bf16[2,4,32,1536]{3,2,1,0:T(8,128)(2,1)S(1)} collective-permute-done((bf16[2,4,32,1536]{3,2,1,0:T(8,128)(2,1)S(1)}, bf16[2,4,32,1536]{3,2,1,0:T(8,128)(2,1)S(1)}, u32[]{:S(2)}, u32[]{:S(2)}) %collective-permute-start) | collective-permute-done | bytes 786464 | tf_op jit(solution)/shard_map/ppermute | solution.py:275
  39.1 0.1 forward_pack.1
  39.2 12.2 %all-to-all-done = bf16[8,768,128]{2,1,0:T(8,128)(2,1)S(1)} async-done(((bf16[8,768,128]{2,1,0:T(8,128)(2,1)}), bf16[8,768,128]{2,1,0:T(8,128)(2,1)S(1)}, u32[]{:S(2)}, u32[]{:S(2)}) %all-to-all-start) | async-done | bytes 1572896 | tf_op jit(solution)/shard_map/all_to_all | solution.py:301
  51.3 8.2 %collective-permute-start.2 = (bf16[2,4,32,1536]{3,2,1,0:T(8,128)(2,1)S(1)}, bf16[2,4,32,1536]{3,2,1,0:T(8,128)(2,1)}, u32[]{:S(2)}, u32[]{:S(2)}) collective-permute-start(bf16[2,4,32,1536]{3,2,1,0:T(8,128)(2,1)S(1)} %forward_pack.1), channel_id=1, source_target_pairs={{0,8},{1,9},{2,10},{3,11},{4,12},{5,13},{6,14},{7,15},{8,0},{9,1},... | collective-permute-start | bytes 2359304 | tf_op jit(solution)/shard_map/ppermute | solution.py:275
  59.5 0.8 slice.6
  60.4 1.9 %collective-permute-start.1 = (bf16[8,2,128,128]{3,2,1,0:T(8,128)(2,1)}, bf16[8,2,128,128]{3,2,1,0:T(8,128)(2,1)}, u32[]{:S(2)}, u32[]{:S(2)}) collective-permute-start(bf16[8,2,128,128]{3,2,1,0:T(8,128)(2,1)} %slice.6), channel_id=1, source_target_pairs={{0,1},{1,0},{2,3},{3,2},{4,5},{5,4},{6,7},{7,6},{8,9},{9,8},{10,11... | collective-permute-start | bytes 1572872 | tf_op jit(solution)/shard_map/ppermute | solution.py:275
  62.3 2.2 %collective-permute-done.1.other = bf16[8,2,128,128]{3,2,1,0:T(8,128)(2,1)} collective-permute-done((bf16[8,2,128,128]{3,2,1,0:T(8,128)(2,1)}, bf16[8,2,128,128]{3,2,1,0:T(8,128)(2,1)}, u32[]{:S(2)}, u32[]{:S(2)}) %collective-permute-start.1) | collective-permute-done | bytes 524320 | tf_op jit(solution)/shard_map/ppermute | solution.py:275
  64.5 0.0 copy-done.8
  64.5 15.3 %spatial_backward.1 = (bf16[8,576,128]{2,1,0:T(8,128)(2,1)}, f32[8,128]{1,0:T(8,128)S(1)}) custom-call(s32[1]{0:T(128)} %bitcast.core_ref, f32[4,128]{1,0:T(4,128)S(1)} %copy-done.8, bf16[8,6,128,128]{3,2,1,0:T(8,128)(2,1)S(1)} %bitcast.18, bf16[8,2,128,128]{3,2,1,0:T(8,128)(2,1)} %collective-permute-done.1.other), custom_call_target="tpu_custom_call" | custom-call | tf_op jit(solution)/shard_map/spatial_backward/pallas_call | solution.py:323
  79.8 4.2 %all-to-all-start.1 = ((bf16[8,576,128]{2,1,0:T(8,128)(2,1)}), bf16[8,576,128]{2,1,0:T(8,128)(2,1)}, u32[]{:S(2)}, u32[]{:S(2)}) async-start(bf16[8,576,128]{2,1,0:T(8,128)(2,1)} %get-tuple-element.37), calls=%async_computation.1 | async-start | bytes 2359296 | tf_op jit(solution)/shard_map/all_to_all | solution.py:301
  84.1 11.3 %collective-permute-done.2.from_z = bf16[2,4,32,1536]{3,2,1,0:T(8,128)(2,1)} collective-permute-done((bf16[2,4,32,1536]{3,2,1,0:T(8,128)(2,1)S(1)}, bf16[2,4,32,1536]{3,2,1,0:T(8,128)(2,1)}, u32[]{:S(2)}, u32[]{:S(2)}) %collective-permute-start.2) | collective-permute-done | bytes 786464 | tf_op jit(solution)/shard_map/ppermute | solution.py:275
  95.4 4.6 %temporal_backward.1 = (bf16[3,32,1536]{2,1,0:T(8,128)(2,1)S(1)}, bf16[2,3,32,1536]{3,2,1,0:T(8,128)(2,1)S(1)}, bf16[3,32,1536]{2,1,0:T(8,128)(2,1)S(1)}, f32[8,128]{1,0:T(8,128)S(1)}) custom-call(f32[4,128]{1,0:T(4,128)S(1)} %copy-done.8, f32[8,128]{1,0:T(8,128)S(1)} %get-tuple-element.31.spatial_terms, bf16[4,32,1536]{2,1,0:T(8,128)(2,1)S(1)} %get-tuple-element.32.own, ...), custom_call_target="tpu_custom_call" | custom-call | flops 251658240000 | bytes 2752512 | tf_op jit(solution)/shard_map/temporal_backward/pallas_call | solution.py:347
  100.1 4.9 %collective-permute-start.7 = (bf16[2,3,32,1536]{3,2,1,0:T(8,128)(2,1)S(1)}, bf16[2,3,32,1536]{3,2,1,0:T(8,128)(2,1)S(1)}, u32[]{:S(2)}, u32[]{:S(2)}) collective-permute-start(bf16[2,3,32,1536]{3,2,1,0:T(8,128)(2,1)S(1)} %get-tuple-element.43), channel_id=1, source_target_pairs={{0,16},{1,17},{2,18},{3,19},{4,20},{5,21},{6,22},{7,23},{8,24},{9,... | collective-permute-start | bytes 1769480 | tf_op jit(solution)/shard_map/ppermute | solution.py:275
  105.0 3.3 %collective-permute-start.3 = (f32[8,128]{1,0:T(8,128)S(1)}, f32[8,128]{1,0:T(8,128)S(1)}, u32[]{:S(2)}, u32[]{:S(2)}) collective-permute-start(f32[8,128]{1,0:T(8,128)S(1)} %get-tuple-element.35), channel_id=1, source_target_pairs={{0,64},{32,96},{64,0},{96,32},{128,192},{160,224},{192,128},{224,1... | collective-permute-start | bytes 12296 | tf_op jit(solution)/shard_map/ppermute | solution.py:275
  108.3 2.2 %collective-permute-done.3 = f32[8,128]{1,0:T(8,128)S(1)} collective-permute-done((f32[8,128]{1,0:T(8,128)S(1)}, f32[8,128]{1,0:T(8,128)S(1)}, u32[]{:S(2)}, u32[]{:S(2)}) %collective-permute-start.3) | collective-permute-done | bytes 4128 | tf_op jit(solution)/shard_map/ppermute | solution.py:275
  110.5 4.0 %collective-permute-start.4 = (f32[8,128]{1,0:T(8,128)S(1)}, f32[8,128]{1,0:T(8,128)S(1)}, u32[]{:S(2)}, u32[]{:S(2)}) collective-permute-start(f32[8,128]{1,0:T(8,128)S(1)} %add.13), channel_id=1, source_target_pairs={{0,128},{32,160},{64,192},{96,224},{128,0},{160,32},{192,64},{224,... | collective-permute-start | bytes 12296 | tf_op jit(solution)/shard_map/ppermute | solution.py:275
  114.6 2.3 %collective-permute-done.4 = f32[8,128]{1,0:T(8,128)S(1)} collective-permute-done((f32[8,128]{1,0:T(8,128)S(1)}, f32[8,128]{1,0:T(8,128)S(1)}, u32[]{:S(2)}, u32[]{:S(2)}) %collective-permute-start.4) | collective-permute-done | bytes 4128 | tf_op jit(solution)/shard_map/ppermute | solution.py:275
  116.9 0.0 collective-permute-done.7.refs_1_
  117.0 5.0 %collective-permute-start.8 = (bf16[2,3,32,1536]{3,2,1,0:T(8,128)(2,1)S(1)}, bf16[2,3,32,1536]{3,2,1,0:T(8,128)(2,1)S(1)}, u32[]{:S(2)}, u32[]{:S(2)}) collective-permute-start(bf16[2,3,32,1536]{3,2,1,0:T(8,128)(2,1)S(1)} %forward_back_pack.1), channel_id=1, source_target_pairs={{0,8},{1,9},{2,10},{3,11},{4,12},{5,13},{6,14},{7,15},{8,0},{9,1},... | collective-permute-start | bytes 1769480 | tf_op jit(solution)/shard_map/ppermute | solution.py:275
  122.0 4.7 %collective-permute-start.5 = (f32[8,128]{1,0:T(8,128)S(1)}, f32[8,128]{1,0:T(8,128)S(1)}, u32[]{:S(2)}, u32[]{:S(2)}) collective-permute-start(f32[8,128]{1,0:T(8,128)S(1)} %add.14), channel_id=1, source_target_pairs={{0,256},{32,288},{64,320},{96,352},{128,384},{160,416},{192,448},{... | collective-permute-start | bytes 12296 | tf_op jit(solution)/shard_map/ppermute | solution.py:275
  126.7 4.7 %collective-permute-done.5 = f32[8,128]{1,0:T(8,128)S(1)} collective-permute-done((f32[8,128]{1,0:T(8,128)S(1)}, f32[8,128]{1,0:T(8,128)S(1)}, u32[]{:S(2)}, u32[]{:S(2)}) %collective-permute-start.5) | collective-permute-done | bytes 4128 | tf_op jit(solution)/shard_map/ppermute | solution.py:275
  131.4 2.5 %collective-permute-start.6 = (f32[8,128]{1,0:T(8,128)S(1)}, f32[8,128]{1,0:T(8,128)S(1)}, u32[]{:S(2)}, u32[]{:S(2)}) collective-permute-start(f32[8,128]{1,0:T(8,128)S(1)} %add.15), channel_id=1, source_target_pairs={{0,32},{32,0},{64,96},{96,64},{128,160},{160,128},{192,224},{224,1... | collective-permute-start | bytes 12296 | tf_op jit(solution)/shard_map/ppermute | solution.py:275
  133.9 3.0 %collective-permute-done.6 = f32[8,128]{1,0:T(8,128)S(1)} collective-permute-done((f32[8,128]{1,0:T(8,128)S(1)}, f32[8,128]{1,0:T(8,128)S(1)}, u32[]{:S(2)}, u32[]{:S(2)}) %collective-permute-start.6) | collective-permute-done | bytes 4128 | tf_op jit(solution)/shard_map/ppermute | solution.py:275
  136.9 0.0 all-to-all-done.1.got
  136.9 0.7 broadcast_in_dim.30
  137.6 6.7 %all-to-all-start.2 = ((f32[32,8,128]{2,1,0:T(8,128)}), f32[32,8,128]{2,1,0:T(8,128)S(1)}, u32[]{:S(2)}, u32[]{:S(2)}) async-start(f32[32,8,128]{2,1,0:T(8,128)} %broadcast_in_dim.30), calls=%async_computation.2 | async-start | bytes 262144 | tf_op jit(solution)/shard_map/all_to_all | solution.py:284
  144.2 2.4 %collective-permute-done.8.refs_2_ = bf16[2,3,32,1536]{3,2,1,0:T(8,128)(2,1)S(1)} collective-permute-done((bf16[2,3,32,1536]{3,2,1,0:T(8,128)(2,1)S(1)}, bf16[2,3,32,1536]{3,2,1,0:T(8,128)(2,1)S(1)}, u32[]{:S(2)}, u32[]{:S(2)}) %collective-permute-start.8) | collective-permute-done | bytes 589856 | tf_op jit(solution)/shard_map/ppermute | solution.py:275
  146.6 1.1 temporal_unpack.1
  147.7 2.5 %spatial_unpack.1 = (bf16[128,1536]{1,0:T(8,128)(2,1)}, bf16[128,1536]{1,0:T(8,128)(2,1)}, bf16[128,1536]{1,0:T(8,128)(2,1)}) custom-call(bf16[8,576,128]{2,1,0:T(8,128)(2,1)} %all-to-all-done.1.got), custom_call_target="tpu_custom_call" | custom-call | tf_op jit(solution)/shard_map/spatial_unpack/pallas_call | solution.py:369
  150.2 6.0 %all-to-all-done.2 = f32[32,8,128]{2,1,0:T(8,128)S(1)} async-done(((f32[32,8,128]{2,1,0:T(8,128)}), f32[32,8,128]{2,1,0:T(8,128)S(1)}, u32[]{:S(2)}, u32[]{:S(2)}) %all-to-all-start.2) | async-done | bytes 131104 | tf_op jit(solution)/shard_map/all_to_all | solution.py:284
  156.2 0.6 slice_multiply_fusion
  (6 shorter events, 0.1 us)
Async XLA Ops:
  0.6 1.0 copy-start
  1.6 1.0 copy-start.2
  2.6 1.0 copy-start.3
  3.6 1.0 copy-start.4
  6.1 7.4 %copy-start.1 = (bf16[1,128,1536]{2,1,0:T(8,128)(2,1)S(1)}, bf16[1,128,1536]{2,1,0:T(8,128)(2,1)}, u32[]{:S(2)}) copy-start(bf16[1,128,1536]{2,1,0:T(8,128)(2,1)} %param.14) | copy-start | bytes 1179652
  6.1 7.4 %copy-start.5 = (bf16[1,128,1536]{2,1,0:T(8,128)(2,1)S(1)}, bf16[1,128,1536]{2,1,0:T(8,128)(2,1)}, u32[]{:S(2)}) copy-start(bf16[1,128,1536]{2,1,0:T(8,128)(2,1)} %param.11) | copy-start | bytes 1179652
  6.1 7.4 %copy-start.6 = (bf16[1,128,1536]{2,1,0:T(8,128)(2,1)S(1)}, bf16[1,128,1536]{2,1,0:T(8,128)(2,1)}, u32[]{:S(2)}) copy-start(bf16[1,128,1536]{2,1,0:T(8,128)(2,1)} %param.12) | copy-start | bytes 1179652
  6.1 7.4 %copy-start.7 = (bf16[1,128,1536]{2,1,0:T(8,128)(2,1)S(1)}, bf16[1,128,1536]{2,1,0:T(8,128)(2,1)}, u32[]{:S(2)}) copy-start(bf16[1,128,1536]{2,1,0:T(8,128)(2,1)} %param.13) | copy-start | bytes 1179652
  6.1 45.2 %all-to-all-start = ((bf16[8,768,128]{2,1,0:T(8,128)(2,1)}), bf16[8,768,128]{2,1,0:T(8,128)(2,1)S(1)}, u32[]{:S(2)}, u32[]{:S(2)}) async-start(bf16[8,768,128]{2,1,0:T(8,128)(2,1)} %bitcast.5), calls=%async_computation | async-start | bytes 3145728 | tf_op jit(solution)/shard_map/all_to_all | solution.py:301
  15.7 48.8 %copy-start.8 = (f32[4,128]{1,0:T(4,128)S(1)}, f32[4,128]{1,0:T(4,128)}, u32[]{:S(2)}) copy-start(f32[4,128]{1,0:T(4,128)} %gains.3) | copy-start | bytes 6148
  15.8 23.3 %collective-permute-start = (bf16[2,4,32,1536]{3,2,1,0:T(8,128)(2,1)S(1)}, bf16[2,4,32,1536]{3,2,1,0:T(8,128)(2,1)S(1)}, u32[]{:S(2)}, u32[]{:S(2)}) collective-permute-start(bf16[2,4,32,1536]{3,2,1,0:T(8,128)(2,1)S(1)} %get-tuple-element.29), channel_id=1, source_target_pairs={{0,16},{1,17},{2,18},{3,19},{4,20},{5,21},{6,22},{7,23},{8,24},{9,... | collective-permute-start | bytes 2359304 | tf_op jit(solution)/shard_map/ppermute | solution.py:275
  51.3 44.1 %collective-permute-start.2 = (bf16[2,4,32,1536]{3,2,1,0:T(8,128)(2,1)S(1)}, bf16[2,4,32,1536]{3,2,1,0:T(8,128)(2,1)}, u32[]{:S(2)}, u32[]{:S(2)}) collective-permute-start(bf16[2,4,32,1536]{3,2,1,0:T(8,128)(2,1)S(1)} %forward_pack.1), channel_id=1, source_target_pairs={{0,8},{1,9},{2,10},{3,11},{4,12},{5,13},{6,14},{7,15},{8,0},{9,1},... | collective-permute-start | bytes 2359304 | tf_op jit(solution)/shard_map/ppermute | solution.py:275
  60.4 4.1 %collective-permute-start.1 = (bf16[8,2,128,128]{3,2,1,0:T(8,128)(2,1)}, bf16[8,2,128,128]{3,2,1,0:T(8,128)(2,1)}, u32[]{:S(2)}, u32[]{:S(2)}) collective-permute-start(bf16[8,2,128,128]{3,2,1,0:T(8,128)(2,1)} %slice.6), channel_id=1, source_target_pairs={{0,1},{1,0},{2,3},{3,2},{4,5},{5,4},{6,7},{7,6},{8,9},{9,8},{10,11... | collective-permute-start | bytes 1572872 | tf_op jit(solution)/shard_map/ppermute | solution.py:275
  79.8 57.1 %all-to-all-start.1 = ((bf16[8,576,128]{2,1,0:T(8,128)(2,1)}), bf16[8,576,128]{2,1,0:T(8,128)(2,1)}, u32[]{:S(2)}, u32[]{:S(2)}) async-start(bf16[8,576,128]{2,1,0:T(8,128)(2,1)} %get-tuple-element.37), calls=%async_computation.1 | async-start | bytes 2359296 | tf_op jit(solution)/shard_map/all_to_all | solution.py:301
  100.1 16.8 %collective-permute-start.7 = (bf16[2,3,32,1536]{3,2,1,0:T(8,128)(2,1)S(1)}, bf16[2,3,32,1536]{3,2,1,0:T(8,128)(2,1)S(1)}, u32[]{:S(2)}, u32[]{:S(2)}) collective-permute-start(bf16[2,3,32,1536]{3,2,1,0:T(8,128)(2,1)S(1)} %get-tuple-element.43), channel_id=1, source_target_pairs={{0,16},{1,17},{2,18},{3,19},{4,20},{5,21},{6,22},{7,23},{8,24},{9,... | collective-permute-start | bytes 1769480 | tf_op jit(solution)/shard_map/ppermute | solution.py:275
  105.0 5.5 %collective-permute-start.3 = (f32[8,128]{1,0:T(8,128)S(1)}, f32[8,128]{1,0:T(8,128)S(1)}, u32[]{:S(2)}, u32[]{:S(2)}) collective-permute-start(f32[8,128]{1,0:T(8,128)S(1)} %get-tuple-element.35), channel_id=1, source_target_pairs={{0,64},{32,96},{64,0},{96,32},{128,192},{160,224},{192,128},{224,1... | collective-permute-start | bytes 12296 | tf_op jit(solution)/shard_map/ppermute | solution.py:275
  110.5 6.4 %collective-permute-start.4 = (f32[8,128]{1,0:T(8,128)S(1)}, f32[8,128]{1,0:T(8,128)S(1)}, u32[]{:S(2)}, u32[]{:S(2)}) collective-permute-start(f32[8,128]{1,0:T(8,128)S(1)} %add.13), channel_id=1, source_target_pairs={{0,128},{32,160},{64,192},{96,224},{128,0},{160,32},{192,64},{224,... | collective-permute-start | bytes 12296 | tf_op jit(solution)/shard_map/ppermute | solution.py:275
  117.0 29.7 %collective-permute-start.8 = (bf16[2,3,32,1536]{3,2,1,0:T(8,128)(2,1)S(1)}, bf16[2,3,32,1536]{3,2,1,0:T(8,128)(2,1)S(1)}, u32[]{:S(2)}, u32[]{:S(2)}) collective-permute-start(bf16[2,3,32,1536]{3,2,1,0:T(8,128)(2,1)S(1)} %forward_back_pack.1), channel_id=1, source_target_pairs={{0,8},{1,9},{2,10},{3,11},{4,12},{5,13},{6,14},{7,15},{8,0},{9,1},... | collective-permute-start | bytes 1769480 | tf_op jit(solution)/shard_map/ppermute | solution.py:275
  122.0 9.4 %collective-permute-start.5 = (f32[8,128]{1,0:T(8,128)S(1)}, f32[8,128]{1,0:T(8,128)S(1)}, u32[]{:S(2)}, u32[]{:S(2)}) collective-permute-start(f32[8,128]{1,0:T(8,128)S(1)} %add.14), channel_id=1, source_target_pairs={{0,256},{32,288},{64,320},{96,352},{128,384},{160,416},{192,448},{... | collective-permute-start | bytes 12296 | tf_op jit(solution)/shard_map/ppermute | solution.py:275
  131.4 5.5 %collective-permute-start.6 = (f32[8,128]{1,0:T(8,128)S(1)}, f32[8,128]{1,0:T(8,128)S(1)}, u32[]{:S(2)}, u32[]{:S(2)}) collective-permute-start(f32[8,128]{1,0:T(8,128)S(1)} %add.15), channel_id=1, source_target_pairs={{0,32},{32,0},{64,96},{96,64},{128,160},{160,128},{192,224},{224,1... | collective-permute-start | bytes 12296 | tf_op jit(solution)/shard_map/ppermute | solution.py:275
  137.6 18.6 %all-to-all-start.2 = ((f32[32,8,128]{2,1,0:T(8,128)}), f32[32,8,128]{2,1,0:T(8,128)S(1)}, u32[]{:S(2)}, u32[]{:S(2)}) async-start(f32[32,8,128]{2,1,0:T(8,128)} %broadcast_in_dim.30), calls=%async_computation.2 | async-start | bytes 262144 | tf_op jit(solution)/shard_map/all_to_all | solution.py:284

commit v4 on v3

--- a/solution.py
+++ b/solution.py
@@ -125,13 +125,26 @@
     ]
 
 
-def spatial_pack_kernel(q, k, v, g, out):
+def spatial_pack_kernel(q, k, v, g, out, held, read, write):
+    targets = []
     for c in range(CHIPS):
         a, b, e = cols(3 * c), cols(3 * c + 1), cols(3 * c + 2)
-        for i, (ref, h) in enumerate([(q, a), (k, a), (v, a), (g, a), (q, b), (g, b)]):
-            out[2 * c, i] = ref[:, h]
-        for i, (ref, h) in enumerate([(q, e), (k, e), (v, e), (g, e), (k, b), (v, b)]):
-            out[2 * c + 1, i] = ref[:, h]
+        targets.append([(q, a), (k, a), (v, a), (g, a), (q, b), (g, b)])
+        targets.append([(q, e), (k, e), (v, e), (g, e), (k, b), (v, b)])
+    blocks = [
+        [pltpu.make_async_copy(x.at[:, h], held.at[t, i], read.at[t, i]) for i, (x, h) in enumerate(target)]
+        for t, target in enumerate(targets)
+    ]
+    ends = [pltpu.make_async_copy(held.at[t], out.at[t], write.at[t]) for t in range(len(targets))]
+    for target in blocks:
+        for block in target:
+            block.start()
+    for target, end in zip(blocks, ends):
+        for block in target:
+            block.wait()
+        end.start()
+    for end in ends:
+        end.wait()
 
 
 def spatial_kernel(core_ref, gains, mine, other, out, gain_out, qn, kn, knt, gg, vv, raw_q, raw_k, dq, dk, dv):
@@ -303,9 +316,15 @@
     packed = pl.pallas_call(
         spatial_pack_kernel,
         out_shape=shape(group, 6, tok, D),
-        in_specs=[VMEM] * 4,
-        out_specs=VMEM,
-        compiler_params=params(16),
+        in_specs=[HBM] * 4,
+        out_specs=HBM,
+        scratch_shapes=[
+            pltpu.VMEM((group, 6, tok, D), BF16),
+            pltpu.SemaphoreType.DMA((group, 6)),
+            pltpu.SemaphoreType.DMA((group,)),
+        ],
+        compiler_params=params(60),
+        cost_estimate=pl.CostEstimate(flops=0, bytes_accessed=0, transcendentals=0),
         name="spatial_pack",
     )(q_spatial[0], k_spatial[0], v_spatial[0], upstream[0])
     mine = exchange(packed.reshape(group, 6 * tok, D)).reshape(group, 6, tok, D)
@@ -374,7 +393,6 @@
         compiler_params=params(16),
         name="spatial_unpack",
     )(back)
-
     count = lax.axis_size("dp") * nseq * tok * (width // D)
     gains = gains / jnp.float32(math.sqrt(count))
     return (grad_qs[None], grad_ks[None], grad_vs[None], grad_qt[None], grad_kt[None], grad_vt[None], gains)

time: 158 us -> 155 us (0.981)
  local copies, waits for them, and re-layouts: 5.5 us -> 1.53 us
    unnamed x18 -> x10, local copies, waits for them, and re-layouts: 4 us -> 0.03 us
  transfers between devices with their start and end apart: 12 -> 12, of which waited for: 10 -> 10; matrix products, arithmetic and copies ran while one was open for 1% -> 1% of each run, Pallas kernels for 16% -> 17%
where the time goes in v4:
time: 155 us; the launch traced here: 154 us
  waiting for transfers between devices  64.8 us (42%)
  starting transfers between devices  57.8 us (37%)
  Pallas kernels  28.4 us (18%)
    ppermute x9, waiting for transfers between devices, swap(): lax.ppermute(x, axis, [(i, i ^ bits) for i in range(lax.axis_size(axis))])  46.7 us
    ppermute x9, starting transfers between devices, swap(): lax.ppermute(x, axis, [(i, i ^ bits) for i in range(lax.axis_size(axis))])  39.5 us
    pallas_call x1, Pallas kernels, local(): pl.pallas_call(spatial_kernel, out_shape=(shape(group, 4 * tok + tok // 2...  15.3 us
    all_to_all x2, waiting for transfers between devices, exchange(): lax.all_to_all(x, 'seq', 0, 0, axis_index_groups=frame_groups, tiled=True)  12.2 us
    all_to_all x2, starting transfers between devices, exchange(): lax.all_to_all(x, 'seq', 0, 0, axis_index_groups=frame_groups, tiled=True)  11.7 us
    all_to_all x1, starting transfers between devices, sum_over(): return jnp.sum(lax.all_to_all(all_of, axis, 0, 0, tiled=True), axis=0)  6.68 us
    all_to_all x1, waiting for transfers between devices, sum_over(): return jnp.sum(lax.all_to_all(all_of, axis, 0, 0, tiled=True), axis=0)  5.94 us
    pallas_call x1, Pallas kernels, local(): pl.pallas_call(temporal_kernel, out_shape=(piece, shape(2, 3, pos, width)...  4.64 us
  transfers between devices with their start and end apart: 12, of which 10 were waited for; matrix products, arithmetic and copies ran while one was open for 1% of the time, Pallas kernels for 17%

profile of v4, /device:TPU:56, one launch (start us, length us, event | category | flops | bytes accessed | tf_op | source)
XLA Modules:
  0.0 154.0 jit_solution(10972055800603944873)
XLA Ops:
  0.6 2.6 %spatial_pack.1 = bf16[8,6,128,128]{3,2,1,0:T(8,128)(2,1)} custom-call(bf16[128,1536]{1,0:T(8,128)(2,1)} %bitcast.25, bf16[128,1536]{1,0:T(8,128)(2,1)} %bitcast.26, bf16[128,1536]{1,0:T(8,128)(2,1)} %bitcast.27, bf16[128,1536]{1,0:T(8,128)(2,1)} %bitcast.19), custom_call_target="tpu_custom_call" | custom-call | tf_op jit(solution)/shard_map/spatial_pack/pallas_call | solution.py:316
  3.2 0.0 copy-start
  3.2 0.0 copy-start.1
  3.2 0.0 copy-start.2
  3.3 0.0 copy-start.3
  3.3 7.4 %all-to-all-start = ((bf16[8,768,128]{2,1,0:T(8,128)(2,1)}), bf16[8,768,128]{2,1,0:T(8,128)(2,1)S(1)}, u32[]{:S(2)}, u32[]{:S(2)}) async-start(bf16[8,768,128]{2,1,0:T(8,128)(2,1)} %bitcast.24), calls=%async_computation | async-start | bytes 3145728 | tf_op jit(solution)/shard_map/all_to_all | solution.py:314
  10.7 0.0 copy-done
  10.7 0.0 copy-done.1
  10.7 0.0 copy-done.2
  10.7 0.0 copy-done.3
  10.7 2.2 %temporal_pack.1 = (bf16[4,32,1536]{2,1,0:T(8,128)(2,1)S(1)}, bf16[2,4,32,1536]{3,2,1,0:T(8,128)(2,1)S(1)}, bf16[4,32,1536]{2,1,0:T(8,128)(2,1)S(1)}) custom-call(s32[1]{0:T(128)} %bitcast.7.ids, bf16[128,1536]{1,0:T(8,128)(2,1)S(1)} %bitcast.21, bf16[128,1536]{1,0:T(8,128)(2,1)S(1)} %bitcast.22, bf16[128,1536]{1,0:T(8,128)(2,1)S(1)} %bitcast.23, ...), custom_call_target="tpu_custom_call" | custom-call | tf_op jit(solution)/shard_map/temporal_pack/pallas_call | solution.py:71
  12.9 0.0 copy-start.4
  12.9 4.9 %collective-permute-start = (bf16[2,4,32,1536]{3,2,1,0:T(8,128)(2,1)S(1)}, bf16[2,4,32,1536]{3,2,1,0:T(8,128)(2,1)S(1)}, u32[]{:S(2)}, u32[]{:S(2)}) collective-permute-start(bf16[2,4,32,1536]{3,2,1,0:T(8,128)(2,1)S(1)} %get-tuple-element.29), channel_id=1, source_target_pairs={{0,16},{1,17},{2,18},{3,19},{4,20},{5,21},{6,22},{7,23},{8,24},{9,... | collective-permute-start | bytes 2359304 | tf_op jit(solution)/shard_map/ppermute | solution.py:288
  17.9 18.4 %collective-permute-done.refs_1_.from_x = bf16[2,4,32,1536]{3,2,1,0:T(8,128)(2,1)S(1)} collective-permute-done((bf16[2,4,32,1536]{3,2,1,0:T(8,128)(2,1)S(1)}, bf16[2,4,32,1536]{3,2,1,0:T(8,128)(2,1)S(1)}, u32[]{:S(2)}, u32[]{:S(2)}) %collective-permute-start) | collective-permute-done | bytes 786464 | tf_op jit(solution)/shard_map/ppermute | solution.py:288
  36.3 0.1 forward_pack.1
  36.3 12.2 %all-to-all-done = bf16[8,768,128]{2,1,0:T(8,128)(2,1)S(1)} async-done(((bf16[8,768,128]{2,1,0:T(8,128)(2,1)}), bf16[8,768,128]{2,1,0:T(8,128)(2,1)S(1)}, u32[]{:S(2)}, u32[]{:S(2)}) %all-to-all-start) | async-done | bytes 1572896 | tf_op jit(solution)/shard_map/all_to_all | solution.py:314
  48.5 8.2 %collective-permute-start.2 = (bf16[2,4,32,1536]{3,2,1,0:T(8,128)(2,1)S(1)}, bf16[2,4,32,1536]{3,2,1,0:T(8,128)(2,1)}, u32[]{:S(2)}, u32[]{:S(2)}) collective-permute-start(bf16[2,4,32,1536]{3,2,1,0:T(8,128)(2,1)S(1)} %forward_pack.1), channel_id=1, source_target_pairs={{0,8},{1,9},{2,10},{3,11},{4,12},{5,13},{6,14},{7,15},{8,0},{9,1},... | collective-permute-start | bytes 2359304 | tf_op jit(solution)/shard_map/ppermute | solution.py:288
  56.7 0.8 slice.6
  57.6 1.9 %collective-permute-start.1 = (bf16[8,2,128,128]{3,2,1,0:T(8,128)(2,1)}, bf16[8,2,128,128]{3,2,1,0:T(8,128)(2,1)}, u32[]{:S(2)}, u32[]{:S(2)}) collective-permute-start(bf16[8,2,128,128]{3,2,1,0:T(8,128)(2,1)} %slice.6), channel_id=1, source_target_pairs={{0,1},{1,0},{2,3},{3,2},{4,5},{5,4},{6,7},{7,6},{8,9},{9,8},{10,11... | collective-permute-start | bytes 1572872 | tf_op jit(solution)/shard_map/ppermute | solution.py:288
  59.5 2.2 %collective-permute-done.1.other = bf16[8,2,128,128]{3,2,1,0:T(8,128)(2,1)} collective-permute-done((bf16[8,2,128,128]{3,2,1,0:T(8,128)(2,1)}, bf16[8,2,128,128]{3,2,1,0:T(8,128)(2,1)}, u32[]{:S(2)}, u32[]{:S(2)}) %collective-permute-start.1) | collective-permute-done | bytes 524320 | tf_op jit(solution)/shard_map/ppermute | solution.py:288
  61.7 0.0 copy-done.4
  61.7 15.3 %spatial_backward.1 = (bf16[8,576,128]{2,1,0:T(8,128)(2,1)}, f32[8,128]{1,0:T(8,128)S(1)}) custom-call(s32[1]{0:T(128)} %bitcast.core_ref, f32[4,128]{1,0:T(4,128)S(1)} %copy-done.4, bf16[8,6,128,128]{3,2,1,0:T(8,128)(2,1)S(1)} %bitcast.18, bf16[8,2,128,128]{3,2,1,0:T(8,128)(2,1)} %collective-permute-done.1.other), custom_call_target="tpu_custom_call" | custom-call | tf_op jit(solution)/shard_map/spatial_backward/pallas_call | solution.py:342
  77.0 4.3 %all-to-all-start.1 = ((bf16[8,576,128]{2,1,0:T(8,128)(2,1)}), bf16[8,576,128]{2,1,0:T(8,128)(2,1)}, u32[]{:S(2)}, u32[]{:S(2)}) async-start(bf16[8,576,128]{2,1,0:T(8,128)(2,1)} %get-tuple-element.37), calls=%async_computation.1 | async-start | bytes 2359296 | tf_op jit(solution)/shard_map/all_to_all | solution.py:314
  81.3 11.3 %collective-permute-done.2.from_z = bf16[2,4,32,1536]{3,2,1,0:T(8,128)(2,1)} collective-permute-done((bf16[2,4,32,1536]{3,2,1,0:T(8,128)(2,1)S(1)}, bf16[2,4,32,1536]{3,2,1,0:T(8,128)(2,1)}, u32[]{:S(2)}, u32[]{:S(2)}) %collective-permute-start.2) | collective-permute-done | bytes 786464 | tf_op jit(solution)/shard_map/ppermute | solution.py:288
  92.6 4.6 %temporal_backward.1 = (bf16[3,32,1536]{2,1,0:T(8,128)(2,1)S(1)}, bf16[2,3,32,1536]{3,2,1,0:T(8,128)(2,1)S(1)}, bf16[3,32,1536]{2,1,0:T(8,128)(2,1)S(1)}, f32[8,128]{1,0:T(8,128)S(1)}) custom-call(f32[4,128]{1,0:T(4,128)S(1)} %copy-done.4, f32[8,128]{1,0:T(8,128)S(1)} %get-tuple-element.31.spatial_terms, bf16[4,32,1536]{2,1,0:T(8,128)(2,1)S(1)} %get-tuple-element.32.own, ...), custom_call_target="tpu_custom_call" | custom-call | flops 251658240000 | bytes 2752512 | tf_op jit(solution)/shard_map/temporal_backward/pallas_call | solution.py:366
  97.2 4.9 %collective-permute-start.7 = (bf16[2,3,32,1536]{3,2,1,0:T(8,128)(2,1)S(1)}, bf16[2,3,32,1536]{3,2,1,0:T(8,128)(2,1)S(1)}, u32[]{:S(2)}, u32[]{:S(2)}) collective-permute-start(bf16[2,3,32,1536]{3,2,1,0:T(8,128)(2,1)S(1)} %get-tuple-element.43), channel_id=1, source_target_pairs={{0,16},{1,17},{2,18},{3,19},{4,20},{5,21},{6,22},{7,23},{8,24},{9,... | collective-permute-start | bytes 1769480 | tf_op jit(solution)/shard_map/ppermute | solution.py:288
  102.2 3.3 %collective-permute-start.3 = (f32[8,128]{1,0:T(8,128)S(1)}, f32[8,128]{1,0:T(8,128)S(1)}, u32[]{:S(2)}, u32[]{:S(2)}) collective-permute-start(f32[8,128]{1,0:T(8,128)S(1)} %get-tuple-element.35), channel_id=1, source_target_pairs={{0,64},{32,96},{64,0},{96,32},{128,192},{160,224},{192,128},{224,1... | collective-permute-start | bytes 12296 | tf_op jit(solution)/shard_map/ppermute | solution.py:288
  105.5 2.2 %collective-permute-done.3 = f32[8,128]{1,0:T(8,128)S(1)} collective-permute-done((f32[8,128]{1,0:T(8,128)S(1)}, f32[8,128]{1,0:T(8,128)S(1)}, u32[]{:S(2)}, u32[]{:S(2)}) %collective-permute-start.3) | collective-permute-done | bytes 4128 | tf_op jit(solution)/shard_map/ppermute | solution.py:288
  107.7 4.0 %collective-permute-start.4 = (f32[8,128]{1,0:T(8,128)S(1)}, f32[8,128]{1,0:T(8,128)S(1)}, u32[]{:S(2)}, u32[]{:S(2)}) collective-permute-start(f32[8,128]{1,0:T(8,128)S(1)} %add.13), channel_id=1, source_target_pairs={{0,128},{32,160},{64,192},{96,224},{128,0},{160,32},{192,64},{224,... | collective-permute-start | bytes 12296 | tf_op jit(solution)/shard_map/ppermute | solution.py:288
  111.7 2.3 %collective-permute-done.4 = f32[8,128]{1,0:T(8,128)S(1)} collective-permute-done((f32[8,128]{1,0:T(8,128)S(1)}, f32[8,128]{1,0:T(8,128)S(1)}, u32[]{:S(2)}, u32[]{:S(2)}) %collective-permute-start.4) | collective-permute-done | bytes 4128 | tf_op jit(solution)/shard_map/ppermute | solution.py:288
  114.1 0.0 collective-permute-done.7.refs_1_
  114.1 5.0 %collective-permute-start.8 = (bf16[2,3,32,1536]{3,2,1,0:T(8,128)(2,1)S(1)}, bf16[2,3,32,1536]{3,2,1,0:T(8,128)(2,1)S(1)}, u32[]{:S(2)}, u32[]{:S(2)}) collective-permute-start(bf16[2,3,32,1536]{3,2,1,0:T(8,128)(2,1)S(1)} %forward_back_pack.1), channel_id=1, source_target_pairs={{0,8},{1,9},{2,10},{3,11},{4,12},{5,13},{6,14},{7,15},{8,0},{9,1},... | collective-permute-start | bytes 1769480 | tf_op jit(solution)/shard_map/ppermute | solution.py:288
  119.2 4.7 %collective-permute-start.5 = (f32[8,128]{1,0:T(8,128)S(1)}, f32[8,128]{1,0:T(8,128)S(1)}, u32[]{:S(2)}, u32[]{:S(2)}) collective-permute-start(f32[8,128]{1,0:T(8,128)S(1)} %add.14), channel_id=1, source_target_pairs={{0,256},{32,288},{64,320},{96,352},{128,384},{160,416},{192,448},{... | collective-permute-start | bytes 12296 | tf_op jit(solution)/shard_map/ppermute | solution.py:288
  123.9 4.7 %collective-permute-done.5 = f32[8,128]{1,0:T(8,128)S(1)} collective-permute-done((f32[8,128]{1,0:T(8,128)S(1)}, f32[8,128]{1,0:T(8,128)S(1)}, u32[]{:S(2)}, u32[]{:S(2)}) %collective-permute-start.5) | collective-permute-done | bytes 4128 | tf_op jit(solution)/shard_map/ppermute | solution.py:288
  128.6 2.5 %collective-permute-start.6 = (f32[8,128]{1,0:T(8,128)S(1)}, f32[8,128]{1,0:T(8,128)S(1)}, u32[]{:S(2)}, u32[]{:S(2)}) collective-permute-start(f32[8,128]{1,0:T(8,128)S(1)} %add.15), channel_id=1, source_target_pairs={{0,32},{32,0},{64,96},{96,64},{128,160},{160,128},{192,224},{224,1... | collective-permute-start | bytes 12296 | tf_op jit(solution)/shard_map/ppermute | solution.py:288
  131.1 3.0 %collective-permute-done.6 = f32[8,128]{1,0:T(8,128)S(1)} collective-permute-done((f32[8,128]{1,0:T(8,128)S(1)}, f32[8,128]{1,0:T(8,128)S(1)}, u32[]{:S(2)}, u32[]{:S(2)}) %collective-permute-start.6) | collective-permute-done | bytes 4128 | tf_op jit(solution)/shard_map/ppermute | solution.py:288
  134.1 0.0 all-to-all-done.1.got
  134.1 0.7 broadcast_in_dim.30
  134.7 6.7 %all-to-all-start.2 = ((f32[32,8,128]{2,1,0:T(8,128)}), f32[32,8,128]{2,1,0:T(8,128)S(1)}, u32[]{:S(2)}, u32[]{:S(2)}) async-start(f32[32,8,128]{2,1,0:T(8,128)} %broadcast_in_dim.30), calls=%async_computation.2 | async-start | bytes 262144 | tf_op jit(solution)/shard_map/all_to_all | solution.py:297
  141.4 2.4 %collective-permute-done.8.refs_2_ = bf16[2,3,32,1536]{3,2,1,0:T(8,128)(2,1)S(1)} collective-permute-done((bf16[2,3,32,1536]{3,2,1,0:T(8,128)(2,1)S(1)}, bf16[2,3,32,1536]{3,2,1,0:T(8,128)(2,1)S(1)}, u32[]{:S(2)}, u32[]{:S(2)}) %collective-permute-start.8) | collective-permute-done | bytes 589856 | tf_op jit(solution)/shard_map/ppermute | solution.py:288
  143.9 1.1 temporal_unpack.1
  145.0 2.5 %spatial_unpack.1 = (bf16[128,1536]{1,0:T(8,128)(2,1)}, bf16[128,1536]{1,0:T(8,128)(2,1)}, bf16[128,1536]{1,0:T(8,128)(2,1)}) custom-call(bf16[8,576,128]{2,1,0:T(8,128)(2,1)} %all-to-all-done.1.got), custom_call_target="tpu_custom_call" | custom-call | tf_op jit(solution)/shard_map/spatial_unpack/pallas_call | solution.py:388
  147.4 5.9 %all-to-all-done.2 = f32[32,8,128]{2,1,0:T(8,128)S(1)} async-done(((f32[32,8,128]{2,1,0:T(8,128)}), f32[32,8,128]{2,1,0:T(8,128)S(1)}, u32[]{:S(2)}, u32[]{:S(2)}) %all-to-all-start.2) | async-done | bytes 131104 | tf_op jit(solution)/shard_map/all_to_all | solution.py:297
  153.4 0.6 slice_multiply_fusion
  (6 shorter events, 0.1 us)
Async XLA Ops:
  3.2 7.5 %copy-start = (bf16[1,128,1536]{2,1,0:T(8,128)(2,1)S(1)}, bf16[1,128,1536]{2,1,0:T(8,128)(2,1)}, u32[]{:S(2)}) copy-start(bf16[1,128,1536]{2,1,0:T(8,128)(2,1)} %param.14) | copy-start | bytes 1179652
  3.2 7.5 %copy-start.1 = (bf16[1,128,1536]{2,1,0:T(8,128)(2,1)S(1)}, bf16[1,128,1536]{2,1,0:T(8,128)(2,1)}, u32[]{:S(2)}) copy-start(bf16[1,128,1536]{2,1,0:T(8,128)(2,1)} %param.11) | copy-start | bytes 1179652
  3.2 7.5 %copy-start.2 = (bf16[1,128,1536]{2,1,0:T(8,128)(2,1)S(1)}, bf16[1,128,1536]{2,1,0:T(8,128)(2,1)}, u32[]{:S(2)}) copy-start(bf16[1,128,1536]{2,1,0:T(8,128)(2,1)} %param.12) | copy-start | bytes 1179652
  3.3 7.4 %copy-start.3 = (bf16[1,128,1536]{2,1,0:T(8,128)(2,1)S(1)}, bf16[1,128,1536]{2,1,0:T(8,128)(2,1)}, u32[]{:S(2)}) copy-start(bf16[1,128,1536]{2,1,0:T(8,128)(2,1)} %param.13) | copy-start | bytes 1179652
  3.3 45.2 %all-to-all-start = ((bf16[8,768,128]{2,1,0:T(8,128)(2,1)}), bf16[8,768,128]{2,1,0:T(8,128)(2,1)S(1)}, u32[]{:S(2)}, u32[]{:S(2)}) async-start(bf16[8,768,128]{2,1,0:T(8,128)(2,1)} %bitcast.24), calls=%async_computation | async-start | bytes 3145728 | tf_op jit(solution)/shard_map/all_to_all | solution.py:314
  12.9 48.8 %copy-start.4 = (f32[4,128]{1,0:T(4,128)S(1)}, f32[4,128]{1,0:T(4,128)}, u32[]{:S(2)}) copy-start(f32[4,128]{1,0:T(4,128)} %gains.3) | copy-start | bytes 6148
  12.9 23.3 %collective-permute-start = (bf16[2,4,32,1536]{3,2,1,0:T(8,128)(2,1)S(1)}, bf16[2,4,32,1536]{3,2,1,0:T(8,128)(2,1)S(1)}, u32[]{:S(2)}, u32[]{:S(2)}) collective-permute-start(bf16[2,4,32,1536]{3,2,1,0:T(8,128)(2,1)S(1)} %get-tuple-element.29), channel_id=1, source_target_pairs={{0,16},{1,17},{2,18},{3,19},{4,20},{5,21},{6,22},{7,23},{8,24},{9,... | collective-permute-start | bytes 2359304 | tf_op jit(solution)/shard_map/ppermute | solution.py:288
  48.5 44.1 %collective-permute-start.2 = (bf16[2,4,32,1536]{3,2,1,0:T(8,128)(2,1)S(1)}, bf16[2,4,32,1536]{3,2,1,0:T(8,128)(2,1)}, u32[]{:S(2)}, u32[]{:S(2)}) collective-permute-start(bf16[2,4,32,1536]{3,2,1,0:T(8,128)(2,1)S(1)} %forward_pack.1), channel_id=1, source_target_pairs={{0,8},{1,9},{2,10},{3,11},{4,12},{5,13},{6,14},{7,15},{8,0},{9,1},... | collective-permute-start | bytes 2359304 | tf_op jit(solution)/shard_map/ppermute | solution.py:288
  57.6 4.1 %collective-permute-start.1 = (bf16[8,2,128,128]{3,2,1,0:T(8,128)(2,1)}, bf16[8,2,128,128]{3,2,1,0:T(8,128)(2,1)}, u32[]{:S(2)}, u32[]{:S(2)}) collective-permute-start(bf16[8,2,128,128]{3,2,1,0:T(8,128)(2,1)} %slice.6), channel_id=1, source_target_pairs={{0,1},{1,0},{2,3},{3,2},{4,5},{5,4},{6,7},{7,6},{8,9},{9,8},{10,11... | collective-permute-start | bytes 1572872 | tf_op jit(solution)/shard_map/ppermute | solution.py:288
  77.0 57.1 %all-to-all-start.1 = ((bf16[8,576,128]{2,1,0:T(8,128)(2,1)}), bf16[8,576,128]{2,1,0:T(8,128)(2,1)}, u32[]{:S(2)}, u32[]{:S(2)}) async-start(bf16[8,576,128]{2,1,0:T(8,128)(2,1)} %get-tuple-element.37), calls=%async_computation.1 | async-start | bytes 2359296 | tf_op jit(solution)/shard_map/all_to_all | solution.py:314
  97.2 16.8 %collective-permute-start.7 = (bf16[2,3,32,1536]{3,2,1,0:T(8,128)(2,1)S(1)}, bf16[2,3,32,1536]{3,2,1,0:T(8,128)(2,1)S(1)}, u32[]{:S(2)}, u32[]{:S(2)}) collective-permute-start(bf16[2,3,32,1536]{3,2,1,0:T(8,128)(2,1)S(1)} %get-tuple-element.43), channel_id=1, source_target_pairs={{0,16},{1,17},{2,18},{3,19},{4,20},{5,21},{6,22},{7,23},{8,24},{9,... | collective-permute-start | bytes 1769480 | tf_op jit(solution)/shard_map/ppermute | solution.py:288
  102.2 5.5 %collective-permute-start.3 = (f32[8,128]{1,0:T(8,128)S(1)}, f32[8,128]{1,0:T(8,128)S(1)}, u32[]{:S(2)}, u32[]{:S(2)}) collective-permute-start(f32[8,128]{1,0:T(8,128)S(1)} %get-tuple-element.35), channel_id=1, source_target_pairs={{0,64},{32,96},{64,0},{96,32},{128,192},{160,224},{192,128},{224,1... | collective-permute-start | bytes 12296 | tf_op jit(solution)/shard_map/ppermute | solution.py:288
  107.7 6.4 %collective-permute-start.4 = (f32[8,128]{1,0:T(8,128)S(1)}, f32[8,128]{1,0:T(8,128)S(1)}, u32[]{:S(2)}, u32[]{:S(2)}) collective-permute-start(f32[8,128]{1,0:T(8,128)S(1)} %add.13), channel_id=1, source_target_pairs={{0,128},{32,160},{64,192},{96,224},{128,0},{160,32},{192,64},{224,... | collective-permute-start | bytes 12296 | tf_op jit(solution)/shard_map/ppermute | solution.py:288
  114.1 29.7 %collective-permute-start.8 = (bf16[2,3,32,1536]{3,2,1,0:T(8,128)(2,1)S(1)}, bf16[2,3,32,1536]{3,2,1,0:T(8,128)(2,1)S(1)}, u32[]{:S(2)}, u32[]{:S(2)}) collective-permute-start(bf16[2,3,32,1536]{3,2,1,0:T(8,128)(2,1)S(1)} %forward_back_pack.1), channel_id=1, source_target_pairs={{0,8},{1,9},{2,10},{3,11},{4,12},{5,13},{6,14},{7,15},{8,0},{9,1},... | collective-permute-start | bytes 1769480 | tf_op jit(solution)/shard_map/ppermute | solution.py:288
  119.2 9.4 %collective-permute-start.5 = (f32[8,128]{1,0:T(8,128)S(1)}, f32[8,128]{1,0:T(8,128)S(1)}, u32[]{:S(2)}, u32[]{:S(2)}) collective-permute-start(f32[8,128]{1,0:T(8,128)S(1)} %add.14), channel_id=1, source_target_pairs={{0,256},{32,288},{64,320},{96,352},{128,384},{160,416},{192,448},{... | collective-permute-start | bytes 12296 | tf_op jit(solution)/shard_map/ppermute | solution.py:288
  128.6 5.5 %collective-permute-start.6 = (f32[8,128]{1,0:T(8,128)S(1)}, f32[8,128]{1,0:T(8,128)S(1)}, u32[]{:S(2)}, u32[]{:S(2)}) collective-permute-start(f32[8,128]{1,0:T(8,128)S(1)} %add.15), channel_id=1, source_target_pairs={{0,32},{32,0},{64,96},{96,64},{128,160},{160,128},{192,224},{224,1... | collective-permute-start | bytes 12296 | tf_op jit(solution)/shard_map/ppermute | solution.py:288
  134.7 18.6 %all-to-all-start.2 = ((f32[32,8,128]{2,1,0:T(8,128)}), f32[32,8,128]{2,1,0:T(8,128)S(1)}, u32[]{:S(2)}, u32[]{:S(2)}) async-start(f32[32,8,128]{2,1,0:T(8,128)} %broadcast_in_dim.30), calls=%async_computation.2 | async-start | bytes 262144 | tf_op jit(solution)/shard_map/all_to_all | solution.py:297

commit v5 on v4

--- a/solution.py
+++ b/solution.py
@@ -375,11 +375,12 @@
         name="temporal_backward",
     )(norm_gains, spatial_terms, keep, from_x, from_z)
     back_x = swap(to_x, 2 * group)
-    terms = add_swapped(add_swapped(terms, 2, "dp"), 4, "dp")
+    for bits in (2, 4, 1):
+        terms = add_swapped(terms, bits, "dp")
     to_z, terms = lax.optimization_barrier((to_z, terms))
     (to_z,) = move(forward_pack, "forward_back_pack", [shape(2, 3, pos, width)], [frame], to_z, back_x)
     back_z = swap(to_z, group)
-    terms = add_swapped(add_swapped(terms, 8, "dp"), 1, "dp")
+    terms = add_swapped(terms, 8, "dp")
     terms, back = lax.optimization_barrier((terms, back))
     gains = sum_over(terms, "seq")[:4]
     grad_qt, grad_kt, grad_vt = move(

time: 155 us -> 153 us (0.987)
  starting transfers between devices: 57.8 us -> 55.7 us
    all_to_all x1, waiting for transfers between devices: 5.94 us -> 1.93 us  [sum_over(): return jnp.sum(lax.all_to_all(all_of, axis, 0, 0, tiled=True), axis=0)]
    ppermute x9, waiting for transfers between devices: 46.7 us -> 50.1 us  [swap(): lax.ppermute(x, axis, [(i, i ^ bits) for i in range(lax.axis_size(axis))])]
    all_to_all x1, starting transfers between devices: 6.68 us -> 4.51 us  [sum_over(): return jnp.sum(lax.all_to_all(all_of, axis, 0, 0, tiled=True), axis=0)]
where the time goes in v5:
time: 153 us; the launch traced here: 151 us
  waiting for transfers between devices  64.2 us (42%)
  starting transfers between devices  55.7 us (36%)
  Pallas kernels  28.4 us (19%)
  local copies, waits for them, and re-layouts  1.53 us (1%)
    ppermute x9, waiting for transfers between devices, swap(): lax.ppermute(x, axis, [(i, i ^ bits) for i in range(lax.axis_size(axis))])  50.1 us
    ppermute x9, starting transfers between devices, swap(): lax.ppermute(x, axis, [(i, i ^ bits) for i in range(lax.axis_size(axis))])  39.5 us
    pallas_call x1, Pallas kernels, local(): pl.pallas_call(spatial_kernel, out_shape=(shape(group, 4 * tok + tok // 2...  15.3 us
    all_to_all x2, waiting for transfers between devices, exchange(): lax.all_to_all(x, 'seq', 0, 0, axis_index_groups=frame_groups, tiled=True)  12.2 us
    all_to_all x2, starting transfers between devices, exchange(): lax.all_to_all(x, 'seq', 0, 0, axis_index_groups=frame_groups, tiled=True)  11.7 us
    pallas_call x1, Pallas kernels, local(): pl.pallas_call(temporal_kernel, out_shape=(piece, shape(2, 3, pos, width)...  4.64 us
    all_to_all x1, starting transfers between devices, sum_over(): return jnp.sum(lax.all_to_all(all_of, axis, 0, 0, tiled=True), axis=0)  4.51 us
    pallas_call x4, Pallas kernels, move(): pl.pallas_call(kernel, out_shape=tuple(outs), in_specs=[SMEM] + [src] * n...  3.4 us
  transfers between devices with their start and end apart: 12, of which 10 were waited for; matrix products, arithmetic and copies ran while one was open for 1% of the time, Pallas kernels for 17%

profile of v5, /device:TPU:56, one launch (start us, length us, event | category | flops | bytes accessed | tf_op | source)
XLA Modules:
  0.0 151.3 jit_solution(14922417631597197129)
XLA Ops:
  0.6 2.6 %spatial_pack.1 = bf16[8,6,128,128]{3,2,1,0:T(8,128)(2,1)} custom-call(bf16[128,1536]{1,0:T(8,128)(2,1)} %bitcast.25, bf16[128,1536]{1,0:T(8,128)(2,1)} %bitcast.26, bf16[128,1536]{1,0:T(8,128)(2,1)} %bitcast.27, bf16[128,1536]{1,0:T(8,128)(2,1)} %bitcast.19), custom_call_target="tpu_custom_call" | custom-call | tf_op jit(solution)/shard_map/spatial_pack/pallas_call | solution.py:316
  3.2 0.0 copy-start
  3.2 0.0 copy-start.1
  3.2 0.0 copy-start.2
  3.3 0.0 copy-start.3
  3.3 7.4 %all-to-all-start = ((bf16[8,768,128]{2,1,0:T(8,128)(2,1)}), bf16[8,768,128]{2,1,0:T(8,128)(2,1)S(1)}, u32[]{:S(2)}, u32[]{:S(2)}) async-start(bf16[8,768,128]{2,1,0:T(8,128)(2,1)} %bitcast.24), calls=%async_computation | async-start | bytes 3145728 | tf_op jit(solution)/shard_map/all_to_all | solution.py:314
  10.7 0.0 copy-done
  10.7 0.0 copy-done.1
  10.7 0.0 copy-done.2
  10.7 0.0 copy-done.3
  10.7 2.2 %temporal_pack.1 = (bf16[4,32,1536]{2,1,0:T(8,128)(2,1)S(1)}, bf16[2,4,32,1536]{3,2,1,0:T(8,128)(2,1)S(1)}, bf16[4,32,1536]{2,1,0:T(8,128)(2,1)S(1)}) custom-call(s32[1]{0:T(128)} %bitcast.7.ids, bf16[128,1536]{1,0:T(8,128)(2,1)S(1)} %bitcast.21, bf16[128,1536]{1,0:T(8,128)(2,1)S(1)} %bitcast.22, bf16[128,1536]{1,0:T(8,128)(2,1)S(1)} %bitcast.23, ...), custom_call_target="tpu_custom_call" | custom-call | tf_op jit(solution)/shard_map/temporal_pack/pallas_call | solution.py:71
  12.9 0.0 copy-start.4
  12.9 4.9 %collective-permute-start = (bf16[2,4,32,1536]{3,2,1,0:T(8,128)(2,1)S(1)}, bf16[2,4,32,1536]{3,2,1,0:T(8,128)(2,1)S(1)}, u32[]{:S(2)}, u32[]{:S(2)}) collective-permute-start(bf16[2,4,32,1536]{3,2,1,0:T(8,128)(2,1)S(1)} %get-tuple-element.29), channel_id=1, source_target_pairs={{0,16},{1,17},{2,18},{3,19},{4,20},{5,21},{6,22},{7,23},{8,24},{9,... | collective-permute-start | bytes 2359304 | tf_op jit(solution)/shard_map/ppermute | solution.py:288
  17.9 18.4 %collective-permute-done.refs_1_.from_x = bf16[2,4,32,1536]{3,2,1,0:T(8,128)(2,1)S(1)} collective-permute-done((bf16[2,4,32,1536]{3,2,1,0:T(8,128)(2,1)S(1)}, bf16[2,4,32,1536]{3,2,1,0:T(8,128)(2,1)S(1)}, u32[]{:S(2)}, u32[]{:S(2)}) %collective-permute-start) | collective-permute-done | bytes 786464 | tf_op jit(solution)/shard_map/ppermute | solution.py:288
  36.3 0.1 forward_pack.1
  36.3 12.2 %all-to-all-done = bf16[8,768,128]{2,1,0:T(8,128)(2,1)S(1)} async-done(((bf16[8,768,128]{2,1,0:T(8,128)(2,1)}), bf16[8,768,128]{2,1,0:T(8,128)(2,1)S(1)}, u32[]{:S(2)}, u32[]{:S(2)}) %all-to-all-start) | async-done | bytes 1572896 | tf_op jit(solution)/shard_map/all_to_all | solution.py:314
  48.5 8.2 %collective-permute-start.2 = (bf16[2,4,32,1536]{3,2,1,0:T(8,128)(2,1)S(1)}, bf16[2,4,32,1536]{3,2,1,0:T(8,128)(2,1)}, u32[]{:S(2)}, u32[]{:S(2)}) collective-permute-start(bf16[2,4,32,1536]{3,2,1,0:T(8,128)(2,1)S(1)} %forward_pack.1), channel_id=1, source_target_pairs={{0,8},{1,9},{2,10},{3,11},{4,12},{5,13},{6,14},{7,15},{8,0},{9,1},... | collective-permute-start | bytes 2359304 | tf_op jit(solution)/shard_map/ppermute | solution.py:288
  56.7 0.8 slice.6
  57.6 1.9 %collective-permute-start.1 = (bf16[8,2,128,128]{3,2,1,0:T(8,128)(2,1)}, bf16[8,2,128,128]{3,2,1,0:T(8,128)(2,1)}, u32[]{:S(2)}, u32[]{:S(2)}) collective-permute-start(bf16[8,2,128,128]{3,2,1,0:T(8,128)(2,1)} %slice.6), channel_id=1, source_target_pairs={{0,1},{1,0},{2,3},{3,2},{4,5},{5,4},{6,7},{7,6},{8,9},{9,8},{10,11... | collective-permute-start | bytes 1572872 | tf_op jit(solution)/shard_map/ppermute | solution.py:288
  59.5 2.2 %collective-permute-done.1.other = bf16[8,2,128,128]{3,2,1,0:T(8,128)(2,1)} collective-permute-done((bf16[8,2,128,128]{3,2,1,0:T(8,128)(2,1)}, bf16[8,2,128,128]{3,2,1,0:T(8,128)(2,1)}, u32[]{:S(2)}, u32[]{:S(2)}) %collective-permute-start.1) | collective-permute-done | bytes 524320 | tf_op jit(solution)/shard_map/ppermute | solution.py:288
  61.7 0.0 copy-done.4
  61.7 15.3 %spatial_backward.1 = (bf16[8,576,128]{2,1,0:T(8,128)(2,1)}, f32[8,128]{1,0:T(8,128)S(1)}) custom-call(s32[1]{0:T(128)} %bitcast.core_ref, f32[4,128]{1,0:T(4,128)S(1)} %copy-done.4, bf16[8,6,128,128]{3,2,1,0:T(8,128)(2,1)S(1)} %bitcast.18, bf16[8,2,128,128]{3,2,1,0:T(8,128)(2,1)} %collective-permute-done.1.other), custom_call_target="tpu_custom_call" | custom-call | tf_op jit(solution)/shard_map/spatial_backward/pallas_call | solution.py:342
  77.0 4.3 %all-to-all-start.1 = ((bf16[8,576,128]{2,1,0:T(8,128)(2,1)}), bf16[8,576,128]{2,1,0:T(8,128)(2,1)}, u32[]{:S(2)}, u32[]{:S(2)}) async-start(bf16[8,576,128]{2,1,0:T(8,128)(2,1)} %get-tuple-element.37), calls=%async_computation.1 | async-start | bytes 2359296 | tf_op jit(solution)/shard_map/all_to_all | solution.py:314
  81.3 11.3 %collective-permute-done.2.from_z = bf16[2,4,32,1536]{3,2,1,0:T(8,128)(2,1)} collective-permute-done((bf16[2,4,32,1536]{3,2,1,0:T(8,128)(2,1)S(1)}, bf16[2,4,32,1536]{3,2,1,0:T(8,128)(2,1)}, u32[]{:S(2)}, u32[]{:S(2)}) %collective-permute-start.2) | collective-permute-done | bytes 786464 | tf_op jit(solution)/shard_map/ppermute | solution.py:288
  92.6 4.6 %temporal_backward.1 = (bf16[3,32,1536]{2,1,0:T(8,128)(2,1)S(1)}, bf16[2,3,32,1536]{3,2,1,0:T(8,128)(2,1)S(1)}, bf16[3,32,1536]{2,1,0:T(8,128)(2,1)S(1)}, f32[8,128]{1,0:T(8,128)S(1)}) custom-call(f32[4,128]{1,0:T(4,128)S(1)} %copy-done.4, f32[8,128]{1,0:T(8,128)S(1)} %get-tuple-element.31.spatial_terms, bf16[4,32,1536]{2,1,0:T(8,128)(2,1)S(1)} %get-tuple-element.32.own, ...), custom_call_target="tpu_custom_call" | custom-call | flops 251658240000 | bytes 2752512 | tf_op jit(solution)/shard_map/temporal_backward/pallas_call | solution.py:366
  97.2 4.9 %collective-permute-start.7 = (bf16[2,3,32,1536]{3,2,1,0:T(8,128)(2,1)S(1)}, bf16[2,3,32,1536]{3,2,1,0:T(8,128)(2,1)S(1)}, u32[]{:S(2)}, u32[]{:S(2)}) collective-permute-start(bf16[2,3,32,1536]{3,2,1,0:T(8,128)(2,1)S(1)} %get-tuple-element.43), channel_id=1, source_target_pairs={{0,16},{1,17},{2,18},{3,19},{4,20},{5,21},{6,22},{7,23},{8,24},{9,... | collective-permute-start | bytes 1769480 | tf_op jit(solution)/shard_map/ppermute | solution.py:288
  102.2 3.3 %collective-permute-start.3 = (f32[8,128]{1,0:T(8,128)S(1)}, f32[8,128]{1,0:T(8,128)S(1)}, u32[]{:S(2)}, u32[]{:S(2)}) collective-permute-start(f32[8,128]{1,0:T(8,128)S(1)} %get-tuple-element.35), channel_id=1, source_target_pairs={{0,64},{32,96},{64,0},{96,32},{128,192},{160,224},{192,128},{224,1... | collective-permute-start | bytes 12296 | tf_op jit(solution)/shard_map/ppermute | solution.py:288
  105.5 2.2 %collective-permute-done.3 = f32[8,128]{1,0:T(8,128)S(1)} collective-permute-done((f32[8,128]{1,0:T(8,128)S(1)}, f32[8,128]{1,0:T(8,128)S(1)}, u32[]{:S(2)}, u32[]{:S(2)}) %collective-permute-start.3) | collective-permute-done | bytes 4128 | tf_op jit(solution)/shard_map/ppermute | solution.py:288
  107.7 4.0 %collective-permute-start.4 = (f32[8,128]{1,0:T(8,128)S(1)}, f32[8,128]{1,0:T(8,128)S(1)}, u32[]{:S(2)}, u32[]{:S(2)}) collective-permute-start(f32[8,128]{1,0:T(8,128)S(1)} %add.13), channel_id=1, source_target_pairs={{0,128},{32,160},{64,192},{96,224},{128,0},{160,32},{192,64},{224,... | collective-permute-start | bytes 12296 | tf_op jit(solution)/shard_map/ppermute | solution.py:288
  111.7 2.3 %collective-permute-done.4 = f32[8,128]{1,0:T(8,128)S(1)} collective-permute-done((f32[8,128]{1,0:T(8,128)S(1)}, f32[8,128]{1,0:T(8,128)S(1)}, u32[]{:S(2)}, u32[]{:S(2)}) %collective-permute-start.4) | collective-permute-done | bytes 4128 | tf_op jit(solution)/shard_map/ppermute | solution.py:288
  114.1 2.5 %collective-permute-start.5 = (f32[8,128]{1,0:T(8,128)S(1)}, f32[8,128]{1,0:T(8,128)S(1)}, u32[]{:S(2)}, u32[]{:S(2)}) collective-permute-start(f32[8,128]{1,0:T(8,128)S(1)} %add.14), channel_id=1, source_target_pairs={{0,32},{32,0},{64,96},{96,64},{128,160},{160,128},{192,224},{224,1... | collective-permute-start | bytes 12296 | tf_op jit(solution)/shard_map/ppermute | solution.py:288
  116.6 3.0 %collective-permute-done.5 = f32[8,128]{1,0:T(8,128)S(1)} collective-permute-done((f32[8,128]{1,0:T(8,128)S(1)}, f32[8,128]{1,0:T(8,128)S(1)}, u32[]{:S(2)}, u32[]{:S(2)}) %collective-permute-start.5) | collective-permute-done | bytes 4128 | tf_op jit(solution)/shard_map/ppermute | solution.py:288
  119.6 0.0 collective-permute-done.7.refs_1_
  119.6 5.0 %collective-permute-start.8 = (bf16[2,3,32,1536]{3,2,1,0:T(8,128)(2,1)S(1)}, bf16[2,3,32,1536]{3,2,1,0:T(8,128)(2,1)S(1)}, u32[]{:S(2)}, u32[]{:S(2)}) collective-permute-start(bf16[2,3,32,1536]{3,2,1,0:T(8,128)(2,1)S(1)} %forward_back_pack.1), channel_id=1, source_target_pairs={{0,8},{1,9},{2,10},{3,11},{4,12},{5,13},{6,14},{7,15},{8,0},{9,1},... | collective-permute-start | bytes 1769480 | tf_op jit(solution)/shard_map/ppermute | solution.py:288
  124.7 4.7 %collective-permute-start.6 = (f32[8,128]{1,0:T(8,128)S(1)}, f32[8,128]{1,0:T(8,128)S(1)}, u32[]{:S(2)}, u32[]{:S(2)}) collective-permute-start(f32[8,128]{1,0:T(8,128)S(1)} %add.15), channel_id=1, source_target_pairs={{0,256},{32,288},{64,320},{96,352},{128,384},{160,416},{192,448},{... | collective-permute-start | bytes 12296 | tf_op jit(solution)/shard_map/ppermute | solution.py:288
  129.4 4.7 %collective-permute-done.6 = f32[8,128]{1,0:T(8,128)S(1)} collective-permute-done((f32[8,128]{1,0:T(8,128)S(1)}, f32[8,128]{1,0:T(8,128)S(1)}, u32[]{:S(2)}, u32[]{:S(2)}) %collective-permute-start.6) | collective-permute-done | bytes 4128 | tf_op jit(solution)/shard_map/ppermute | solution.py:288
  134.1 0.0 all-to-all-done.1.got
  134.1 0.7 broadcast_in_dim.30
  134.7 4.5 %all-to-all-start.2 = ((f32[32,8,128]{2,1,0:T(8,128)}), f32[32,8,128]{2,1,0:T(8,128)S(1)}, u32[]{:S(2)}, u32[]{:S(2)}) async-start(f32[32,8,128]{2,1,0:T(8,128)} %broadcast_in_dim.30), calls=%async_computation.2 | async-start | bytes 262144 | tf_op jit(solution)/shard_map/all_to_all | solution.py:297
  139.3 5.9 %collective-permute-done.8.refs_2_ = bf16[2,3,32,1536]{3,2,1,0:T(8,128)(2,1)S(1)} collective-permute-done((bf16[2,3,32,1536]{3,2,1,0:T(8,128)(2,1)S(1)}, bf16[2,3,32,1536]{3,2,1,0:T(8,128)(2,1)S(1)}, u32[]{:S(2)}, u32[]{:S(2)}) %collective-permute-start.8) | collective-permute-done | bytes 589856 | tf_op jit(solution)/shard_map/ppermute | solution.py:288
  145.1 1.1 temporal_unpack.1
  146.2 2.5 %spatial_unpack.1 = (bf16[128,1536]{1,0:T(8,128)(2,1)}, bf16[128,1536]{1,0:T(8,128)(2,1)}, bf16[128,1536]{1,0:T(8,128)(2,1)}) custom-call(bf16[8,576,128]{2,1,0:T(8,128)(2,1)} %all-to-all-done.1.got), custom_call_target="tpu_custom_call" | custom-call | tf_op jit(solution)/shard_map/spatial_unpack/pallas_call | solution.py:389
  148.7 1.9 %all-to-all-done.2 = f32[32,8,128]{2,1,0:T(8,128)S(1)} async-done(((f32[32,8,128]{2,1,0:T(8,128)}), f32[32,8,128]{2,1,0:T(8,128)S(1)}, u32[]{:S(2)}, u32[]{:S(2)}) %all-to-all-start.2) | async-done | bytes 131104 | tf_op jit(solution)/shard_map/all_to_all | solution.py:297
  150.7 0.6 slice_multiply_fusion
  (6 shorter events, 0.1 us)
Async XLA Ops:
  3.2 7.5 %copy-start = (bf16[1,128,1536]{2,1,0:T(8,128)(2,1)S(1)}, bf16[1,128,1536]{2,1,0:T(8,128)(2,1)}, u32[]{:S(2)}) copy-start(bf16[1,128,1536]{2,1,0:T(8,128)(2,1)} %param.14) | copy-start | bytes 1179652
  3.2 7.5 %copy-start.1 = (bf16[1,128,1536]{2,1,0:T(8,128)(2,1)S(1)}, bf16[1,128,1536]{2,1,0:T(8,128)(2,1)}, u32[]{:S(2)}) copy-start(bf16[1,128,1536]{2,1,0:T(8,128)(2,1)} %param.11) | copy-start | bytes 1179652
  3.2 7.5 %copy-start.2 = (bf16[1,128,1536]{2,1,0:T(8,128)(2,1)S(1)}, bf16[1,128,1536]{2,1,0:T(8,128)(2,1)}, u32[]{:S(2)}) copy-start(bf16[1,128,1536]{2,1,0:T(8,128)(2,1)} %param.12) | copy-start | bytes 1179652
  3.3 7.4 %copy-start.3 = (bf16[1,128,1536]{2,1,0:T(8,128)(2,1)S(1)}, bf16[1,128,1536]{2,1,0:T(8,128)(2,1)}, u32[]{:S(2)}) copy-start(bf16[1,128,1536]{2,1,0:T(8,128)(2,1)} %param.13) | copy-start | bytes 1179652
  3.3 45.2 %all-to-all-start = ((bf16[8,768,128]{2,1,0:T(8,128)(2,1)}), bf16[8,768,128]{2,1,0:T(8,128)(2,1)S(1)}, u32[]{:S(2)}, u32[]{:S(2)}) async-start(bf16[8,768,128]{2,1,0:T(8,128)(2,1)} %bitcast.24), calls=%async_computation | async-start | bytes 3145728 | tf_op jit(solution)/shard_map/all_to_all | solution.py:314
  12.9 48.8 %copy-start.4 = (f32[4,128]{1,0:T(4,128)S(1)}, f32[4,128]{1,0:T(4,128)}, u32[]{:S(2)}) copy-start(f32[4,128]{1,0:T(4,128)} %gains.3) | copy-start | bytes 6148
  12.9 23.3 %collective-permute-start = (bf16[2,4,32,1536]{3,2,1,0:T(8,128)(2,1)S(1)}, bf16[2,4,32,1536]{3,2,1,0:T(8,128)(2,1)S(1)}, u32[]{:S(2)}, u32[]{:S(2)}) collective-permute-start(bf16[2,4,32,1536]{3,2,1,0:T(8,128)(2,1)S(1)} %get-tuple-element.29), channel_id=1, source_target_pairs={{0,16},{1,17},{2,18},{3,19},{4,20},{5,21},{6,22},{7,23},{8,24},{9,... | collective-permute-start | bytes 2359304 | tf_op jit(solution)/shard_map/ppermute | solution.py:288
  48.5 44.1 %collective-permute-start.2 = (bf16[2,4,32,1536]{3,2,1,0:T(8,128)(2,1)S(1)}, bf16[2,4,32,1536]{3,2,1,0:T(8,128)(2,1)}, u32[]{:S(2)}, u32[]{:S(2)}) collective-permute-start(bf16[2,4,32,1536]{3,2,1,0:T(8,128)(2,1)S(1)} %forward_pack.1), channel_id=1, source_target_pairs={{0,8},{1,9},{2,10},{3,11},{4,12},{5,13},{6,14},{7,15},{8,0},{9,1},... | collective-permute-start | bytes 2359304 | tf_op jit(solution)/shard_map/ppermute | solution.py:288
  57.6 4.1 %collective-permute-start.1 = (bf16[8,2,128,128]{3,2,1,0:T(8,128)(2,1)}, bf16[8,2,128,128]{3,2,1,0:T(8,128)(2,1)}, u32[]{:S(2)}, u32[]{:S(2)}) collective-permute-start(bf16[8,2,128,128]{3,2,1,0:T(8,128)(2,1)} %slice.6), channel_id=1, source_target_pairs={{0,1},{1,0},{2,3},{3,2},{4,5},{5,4},{6,7},{7,6},{8,9},{9,8},{10,11... | collective-permute-start | bytes 1572872 | tf_op jit(solution)/shard_map/ppermute | solution.py:288
  77.0 57.1 %all-to-all-start.1 = ((bf16[8,576,128]{2,1,0:T(8,128)(2,1)}), bf16[8,576,128]{2,1,0:T(8,128)(2,1)}, u32[]{:S(2)}, u32[]{:S(2)}) async-start(bf16[8,576,128]{2,1,0:T(8,128)(2,1)} %get-tuple-element.37), calls=%async_computation.1 | async-start | bytes 2359296 | tf_op jit(solution)/shard_map/all_to_all | solution.py:314
  97.2 22.3 %collective-permute-start.7 = (bf16[2,3,32,1536]{3,2,1,0:T(8,128)(2,1)S(1)}, bf16[2,3,32,1536]{3,2,1,0:T(8,128)(2,1)S(1)}, u32[]{:S(2)}, u32[]{:S(2)}) collective-permute-start(bf16[2,3,32,1536]{3,2,1,0:T(8,128)(2,1)S(1)} %get-tuple-element.43), channel_id=1, source_target_pairs={{0,16},{1,17},{2,18},{3,19},{4,20},{5,21},{6,22},{7,23},{8,24},{9,... | collective-permute-start | bytes 1769480 | tf_op jit(solution)/shard_map/ppermute | solution.py:288
  102.2 5.5 %collective-permute-start.3 = (f32[8,128]{1,0:T(8,128)S(1)}, f32[8,128]{1,0:T(8,128)S(1)}, u32[]{:S(2)}, u32[]{:S(2)}) collective-permute-start(f32[8,128]{1,0:T(8,128)S(1)} %get-tuple-element.35), channel_id=1, source_target_pairs={{0,64},{32,96},{64,0},{96,32},{128,192},{160,224},{192,128},{224,1... | collective-permute-start | bytes 12296 | tf_op jit(solution)/shard_map/ppermute | solution.py:288
  107.7 6.4 %collective-permute-start.4 = (f32[8,128]{1,0:T(8,128)S(1)}, f32[8,128]{1,0:T(8,128)S(1)}, u32[]{:S(2)}, u32[]{:S(2)}) collective-permute-start(f32[8,128]{1,0:T(8,128)S(1)} %add.13), channel_id=1, source_target_pairs={{0,128},{32,160},{64,192},{96,224},{128,0},{160,32},{192,64},{224,... | collective-permute-start | bytes 12296 | tf_op jit(solution)/shard_map/ppermute | solution.py:288
  114.1 5.5 %collective-permute-start.5 = (f32[8,128]{1,0:T(8,128)S(1)}, f32[8,128]{1,0:T(8,128)S(1)}, u32[]{:S(2)}, u32[]{:S(2)}) collective-permute-start(f32[8,128]{1,0:T(8,128)S(1)} %add.14), channel_id=1, source_target_pairs={{0,32},{32,0},{64,96},{96,64},{128,160},{160,128},{192,224},{224,1... | collective-permute-start | bytes 12296 | tf_op jit(solution)/shard_map/ppermute | solution.py:288
  119.6 25.5 %collective-permute-start.8 = (bf16[2,3,32,1536]{3,2,1,0:T(8,128)(2,1)S(1)}, bf16[2,3,32,1536]{3,2,1,0:T(8,128)(2,1)S(1)}, u32[]{:S(2)}, u32[]{:S(2)}) collective-permute-start(bf16[2,3,32,1536]{3,2,1,0:T(8,128)(2,1)S(1)} %forward_back_pack.1), channel_id=1, source_target_pairs={{0,8},{1,9},{2,10},{3,11},{4,12},{5,13},{6,14},{7,15},{8,0},{9,1},... | collective-permute-start | bytes 1769480 | tf_op jit(solution)/shard_map/ppermute | solution.py:288
  124.7 9.4 %collective-permute-start.6 = (f32[8,128]{1,0:T(8,128)S(1)}, f32[8,128]{1,0:T(8,128)S(1)}, u32[]{:S(2)}, u32[]{:S(2)}) collective-permute-start(f32[8,128]{1,0:T(8,128)S(1)} %add.15), channel_id=1, source_target_pairs={{0,256},{32,288},{64,320},{96,352},{128,384},{160,416},{192,448},{... | collective-permute-start | bytes 12296 | tf_op jit(solution)/shard_map/ppermute | solution.py:288
  134.7 15.9 %all-to-all-start.2 = ((f32[32,8,128]{2,1,0:T(8,128)}), f32[32,8,128]{2,1,0:T(8,128)S(1)}, u32[]{:S(2)}, u32[]{:S(2)}) async-start(f32[32,8,128]{2,1,0:T(8,128)} %broadcast_in_dim.30), calls=%async_computation.2 | async-start | bytes 262144 | tf_op jit(solution)/shard_map/all_to_all | solution.py:297

commit v6 on v5

--- a/solution.py
+++ b/solution.py
@@ -360,6 +360,10 @@
         cost_estimate=pl.CostEstimate(flops=0, bytes_accessed=0, transcendentals=0),
         name="spatial_backward",
     )(core.reshape(1), norm_gains, mine, other)
+    spatial_grads, temporal_gains = lax.optimization_barrier((spatial_grads, norm_gains))
+    for _ in range(2):
+        temporal_gains = swap(temporal_gains, 1)
+    spatial_grads, temporal_gains = lax.optimization_barrier((spatial_grads, temporal_gains))
     back = exchange(spatial_grads)
 
     piece = shape(3, pos, width)
@@ -373,7 +377,7 @@
             flops=10000 * tok * tok * width, bytes_accessed=14 * tok * width, transcendentals=tok * tok * 12
         ),
         name="temporal_backward",
-    )(norm_gains, spatial_terms, keep, from_x, from_z)
+    )(temporal_gains, spatial_terms, keep, from_x, from_z)
     back_x = swap(to_x, 2 * group)
     for bits in (2, 4, 1):
         terms = add_swapped(terms, bits, "dp")

time: 153 us -> 153 us (level)
  waiting for transfers between devices: 64.2 us -> 59.5 us
  starting transfers between devices: 55.7 us -> 59.7 us
    ppermute x9 -> x11, waiting for transfers between devices: 50.1 us -> 46.6 us  [swap(): lax.ppermute(x, axis, [(i, i ^ bits) for i in range(lax.axis_size(axis))])]
    ppermute x9 -> x11, starting transfers between devices: 39.5 us -> 42.2 us  [swap(): lax.ppermute(x, axis, [(i, i ^ bits) for i in range(lax.axis_size(axis))])]
  transfers between devices with their start and end apart: 12 -> 14, of which waited for: 10 -> 12; matrix products, arithmetic and copies ran while one was open for 1% -> 1% of each run, Pallas kernels for 17% -> 17%
where the time goes in v6:
time: 153 us; the launch traced here: 151 us
  starting transfers between devices  59.7 us (39%)
  waiting for transfers between devices  59.5 us (39%)
  Pallas kernels  28.4 us (19%)
  local copies, waits for them, and re-layouts  1.54 us (1%)
    ppermute x11, waiting for transfers between devices, swap(): lax.ppermute(x, axis, [(i, i ^ bits) for i in range(lax.axis_size(axis))])  46.6 us
    ppermute x11, starting transfers between devices, swap(): lax.ppermute(x, axis, [(i, i ^ bits) for i in range(lax.axis_size(axis))])  42.2 us
    pallas_call x1, Pallas kernels, local(): pl.pallas_call(spatial_kernel, out_shape=(shape(group, 4 * tok + tok // 2...  15.3 us
    all_to_all x2, waiting for transfers between devices, exchange(): lax.all_to_all(x, 'seq', 0, 0, axis_index_groups=frame_groups, tiled=True)  12.2 us
    all_to_all x2, starting transfers between devices, exchange(): lax.all_to_all(x, 'seq', 0, 0, axis_index_groups=frame_groups, tiled=True)  11.7 us
    all_to_all x1, starting transfers between devices, sum_over(): return jnp.sum(lax.all_to_all(all_of, axis, 0, 0, tiled=True), axis=0)  5.91 us
    pallas_call x1, Pallas kernels, local(): pl.pallas_call(temporal_kernel, out_shape=(piece, shape(2, 3, pos, width)...  4.64 us
    pallas_call x4, Pallas kernels, move(): pl.pallas_call(kernel, out_shape=tuple(outs), in_specs=[SMEM] + [src] * n...  3.4 us
  transfers between devices with their start and end apart: 14, of which 12 were waited for; matrix products, arithmetic and copies ran while one was open for 1% of the time, Pallas kernels for 17%

profile of v6, /device:TPU:56, one launch (start us, length us, event | category | flops | bytes accessed | tf_op | source)
XLA Modules:
  0.0 150.6 jit_solution(866617835439053802)
XLA Ops:
  0.6 2.6 %spatial_pack.1 = bf16[8,6,128,128]{3,2,1,0:T(8,128)(2,1)} custom-call(bf16[128,1536]{1,0:T(8,128)(2,1)} %bitcast.25, bf16[128,1536]{1,0:T(8,128)(2,1)} %bitcast.26, bf16[128,1536]{1,0:T(8,128)(2,1)} %bitcast.27, bf16[128,1536]{1,0:T(8,128)(2,1)} %bitcast.19), custom_call_target="tpu_custom_call" | custom-call | tf_op jit(solution)/shard_map/spatial_pack/pallas_call | solution.py:316
  3.2 0.0 copy-start
  3.2 0.0 copy-start.1
  3.2 0.0 copy-start.2
  3.3 0.0 copy-start.3
  3.3 7.4 %all-to-all-start = ((bf16[8,768,128]{2,1,0:T(8,128)(2,1)}), bf16[8,768,128]{2,1,0:T(8,128)(2,1)S(1)}, u32[]{:S(2)}, u32[]{:S(2)}) async-start(bf16[8,768,128]{2,1,0:T(8,128)(2,1)} %bitcast.24), calls=%async_computation | async-start | bytes 3145728 | tf_op jit(solution)/shard_map/all_to_all | solution.py:314
  10.7 0.0 copy-done
  10.7 0.0 copy-done.1
  10.7 0.0 copy-done.2
  10.7 0.0 copy-done.3
  10.7 2.2 %temporal_pack.1 = (bf16[4,32,1536]{2,1,0:T(8,128)(2,1)S(1)}, bf16[2,4,32,1536]{3,2,1,0:T(8,128)(2,1)S(1)}, bf16[4,32,1536]{2,1,0:T(8,128)(2,1)S(1)}) custom-call(s32[1]{0:T(128)} %bitcast.7.ids, bf16[128,1536]{1,0:T(8,128)(2,1)S(1)} %bitcast.21, bf16[128,1536]{1,0:T(8,128)(2,1)S(1)} %bitcast.22, bf16[128,1536]{1,0:T(8,128)(2,1)S(1)} %bitcast.23, ...), custom_call_target="tpu_custom_call" | custom-call | tf_op jit(solution)/shard_map/temporal_pack/pallas_call | solution.py:71
  12.9 0.0 copy-start.4
  12.9 4.9 %collective-permute-start = (bf16[2,4,32,1536]{3,2,1,0:T(8,128)(2,1)S(1)}, bf16[2,4,32,1536]{3,2,1,0:T(8,128)(2,1)S(1)}, u32[]{:S(2)}, u32[]{:S(2)}) collective-permute-start(bf16[2,4,32,1536]{3,2,1,0:T(8,128)(2,1)S(1)} %get-tuple-element.33), channel_id=1, source_target_pairs={{0,16},{1,17},{2,18},{3,19},{4,20},{5,21},{6,22},{7,23},{8,24},{9,... | collective-permute-start | bytes 2359304 | tf_op jit(solution)/shard_map/ppermute | solution.py:288
  17.9 18.4 %collective-permute-done.refs_1_.from_x = bf16[2,4,32,1536]{3,2,1,0:T(8,128)(2,1)S(1)} collective-permute-done((bf16[2,4,32,1536]{3,2,1,0:T(8,128)(2,1)S(1)}, bf16[2,4,32,1536]{3,2,1,0:T(8,128)(2,1)S(1)}, u32[]{:S(2)}, u32[]{:S(2)}) %collective-permute-start) | collective-permute-done | bytes 786464 | tf_op jit(solution)/shard_map/ppermute | solution.py:288
  36.3 0.1 forward_pack.1
  36.3 12.2 %all-to-all-done = bf16[8,768,128]{2,1,0:T(8,128)(2,1)S(1)} async-done(((bf16[8,768,128]{2,1,0:T(8,128)(2,1)}), bf16[8,768,128]{2,1,0:T(8,128)(2,1)S(1)}, u32[]{:S(2)}, u32[]{:S(2)}) %all-to-all-start) | async-done | bytes 1572896 | tf_op jit(solution)/shard_map/all_to_all | solution.py:314
  48.5 8.2 %collective-permute-start.4 = (bf16[2,4,32,1536]{3,2,1,0:T(8,128)(2,1)S(1)}, bf16[2,4,32,1536]{3,2,1,0:T(8,128)(2,1)}, u32[]{:S(2)}, u32[]{:S(2)}) collective-permute-start(bf16[2,4,32,1536]{3,2,1,0:T(8,128)(2,1)S(1)} %forward_pack.1), channel_id=1, source_target_pairs={{0,8},{1,9},{2,10},{3,11},{4,12},{5,13},{6,14},{7,15},{8,0},{9,1},... | collective-permute-start | bytes 2359304 | tf_op jit(solution)/shard_map/ppermute | solution.py:288
  56.7 0.8 slice.6
  57.6 1.9 %collective-permute-start.1 = (bf16[8,2,128,128]{3,2,1,0:T(8,128)(2,1)}, bf16[8,2,128,128]{3,2,1,0:T(8,128)(2,1)}, u32[]{:S(2)}, u32[]{:S(2)}) collective-permute-start(bf16[8,2,128,128]{3,2,1,0:T(8,128)(2,1)} %slice.6), channel_id=1, source_target_pairs={{0,1},{1,0},{2,3},{3,2},{4,5},{5,4},{6,7},{7,6},{8,9},{9,8},{10,11... | collective-permute-start | bytes 1572872 | tf_op jit(solution)/shard_map/ppermute | solution.py:288
  59.5 2.2 %collective-permute-done.1.other = bf16[8,2,128,128]{3,2,1,0:T(8,128)(2,1)} collective-permute-done((bf16[8,2,128,128]{3,2,1,0:T(8,128)(2,1)}, bf16[8,2,128,128]{3,2,1,0:T(8,128)(2,1)}, u32[]{:S(2)}, u32[]{:S(2)}) %collective-permute-start.1) | collective-permute-done | bytes 524320 | tf_op jit(solution)/shard_map/ppermute | solution.py:288
  61.7 0.0 copy-done.4
  61.7 15.3 %spatial_backward.1 = (bf16[8,576,128]{2,1,0:T(8,128)(2,1)}, f32[8,128]{1,0:T(8,128)S(1)}) custom-call(s32[1]{0:T(128)} %bitcast.core_ref, f32[4,128]{1,0:T(4,128)S(1)} %copy-done.4, bf16[8,6,128,128]{3,2,1,0:T(8,128)(2,1)S(1)} %bitcast.18, bf16[8,2,128,128]{3,2,1,0:T(8,128)(2,1)} %collective-permute-done.1.other), custom_call_target="tpu_custom_call" | custom-call | tf_op jit(solution)/shard_map/spatial_backward/pallas_call | solution.py:342
  77.0 2.0 %collective-permute-start.2 = (f32[4,128]{1,0:T(4,128)S(1)}, f32[4,128]{1,0:T(4,128)S(1)}, u32[]{:S(2)}, u32[]{:S(2)}) collective-permute-start(f32[4,128]{1,0:T(4,128)S(1)} %copy-done.4), channel_id=1, source_target_pairs={{0,1},{1,0},{2,3},{3,2},{4,5},{5,4},{6,7},{7,6},{8,9},{9,8},{10,11... | collective-permute-start | bytes 6152 | tf_op jit(solution)/shard_map/ppermute | solution.py:288
  79.1 1.0 collective-permute-done.2
  80.1 2.1 %collective-permute-start.3 = (f32[4,128]{1,0:T(4,128)S(1)}, f32[4,128]{1,0:T(4,128)S(1)}, u32[]{:S(2)}, u32[]{:S(2)}) collective-permute-start(f32[4,128]{1,0:T(4,128)S(1)} %collective-permute-done.2), channel_id=1, source_target_pairs={{0,1},{1,0},{2,3},{3,2},{4,5},{5,4},{6,7},{7,6},{8,9},{9,8},{10,11... | collective-permute-start | bytes 6152 | tf_op jit(solution)/shard_map/ppermute | solution.py:288
  82.1 1.0 collective-permute-done.3.gains
  83.1 4.2 %all-to-all-start.1 = ((bf16[8,576,128]{2,1,0:T(8,128)(2,1)}), bf16[8,576,128]{2,1,0:T(8,128)(2,1)}, u32[]{:S(2)}, u32[]{:S(2)}) async-start(bf16[8,576,128]{2,1,0:T(8,128)(2,1)} %get-tuple-element.45), calls=%async_computation.1 | async-start | bytes 2359296 | tf_op jit(solution)/shard_map/all_to_all | solution.py:314
  87.4 5.2 %collective-permute-done.4.from_z = bf16[2,4,32,1536]{3,2,1,0:T(8,128)(2,1)} collective-permute-done((bf16[2,4,32,1536]{3,2,1,0:T(8,128)(2,1)S(1)}, bf16[2,4,32,1536]{3,2,1,0:T(8,128)(2,1)}, u32[]{:S(2)}, u32[]{:S(2)}) %collective-permute-start.4) | collective-permute-done | bytes 786464 | tf_op jit(solution)/shard_map/ppermute | solution.py:288
  92.5 4.6 %temporal_backward.1 = (bf16[3,32,1536]{2,1,0:T(8,128)(2,1)S(1)}, bf16[2,3,32,1536]{3,2,1,0:T(8,128)(2,1)S(1)}, bf16[3,32,1536]{2,1,0:T(8,128)(2,1)S(1)}, f32[8,128]{1,0:T(8,128)S(1)}) custom-call(f32[4,128]{1,0:T(4,128)S(1)} %collective-permute-done.3.gains, f32[8,128]{1,0:T(8,128)S(1)} %get-tuple-element.39.spatial_terms, ...), custom_call_target="tpu_custom_call" | custom-call | flops 251658240000 | bytes 2752512 | tf_op jit(solution)/shard_map/temporal_backward/pallas_call | solution.py:370
  97.2 4.9 %collective-permute-start.9 = (bf16[2,3,32,1536]{3,2,1,0:T(8,128)(2,1)S(1)}, bf16[2,3,32,1536]{3,2,1,0:T(8,128)(2,1)S(1)}, u32[]{:S(2)}, u32[]{:S(2)}) collective-permute-start(bf16[2,3,32,1536]{3,2,1,0:T(8,128)(2,1)S(1)} %get-tuple-element.51), channel_id=1, source_target_pairs={{0,16},{1,17},{2,18},{3,19},{4,20},{5,21},{6,22},{7,23},{8,24},{9,... | collective-permute-start | bytes 1769480 | tf_op jit(solution)/shard_map/ppermute | solution.py:288
  102.1 3.3 %collective-permute-start.5 = (f32[8,128]{1,0:T(8,128)S(1)}, f32[8,128]{1,0:T(8,128)S(1)}, u32[]{:S(2)}, u32[]{:S(2)}) collective-permute-start(f32[8,128]{1,0:T(8,128)S(1)} %get-tuple-element.43), channel_id=1, source_target_pairs={{0,64},{32,96},{64,0},{96,32},{128,192},{160,224},{192,128},{224,1... | collective-permute-start | bytes 12296 | tf_op jit(solution)/shard_map/ppermute | solution.py:288
  105.4 2.2 %collective-permute-done.5 = f32[8,128]{1,0:T(8,128)S(1)} collective-permute-done((f32[8,128]{1,0:T(8,128)S(1)}, f32[8,128]{1,0:T(8,128)S(1)}, u32[]{:S(2)}, u32[]{:S(2)}) %collective-permute-start.5) | collective-permute-done | bytes 4128 | tf_op jit(solution)/shard_map/ppermute | solution.py:288
  107.6 4.0 %collective-permute-start.6 = (f32[8,128]{1,0:T(8,128)S(1)}, f32[8,128]{1,0:T(8,128)S(1)}, u32[]{:S(2)}, u32[]{:S(2)}) collective-permute-start(f32[8,128]{1,0:T(8,128)S(1)} %add.13), channel_id=1, source_target_pairs={{0,128},{32,160},{64,192},{96,224},{128,0},{160,32},{192,64},{224,... | collective-permute-start | bytes 12296 | tf_op jit(solution)/shard_map/ppermute | solution.py:288
  111.6 2.4 %collective-permute-done.6 = f32[8,128]{1,0:T(8,128)S(1)} collective-permute-done((f32[8,128]{1,0:T(8,128)S(1)}, f32[8,128]{1,0:T(8,128)S(1)}, u32[]{:S(2)}, u32[]{:S(2)}) %collective-permute-start.6) | collective-permute-done | bytes 4128 | tf_op jit(solution)/shard_map/ppermute | solution.py:288
  114.0 2.5 %collective-permute-start.7 = (f32[8,128]{1,0:T(8,128)S(1)}, f32[8,128]{1,0:T(8,128)S(1)}, u32[]{:S(2)}, u32[]{:S(2)}) collective-permute-start(f32[8,128]{1,0:T(8,128)S(1)} %add.14), channel_id=1, source_target_pairs={{0,32},{32,0},{64,96},{96,64},{128,160},{160,128},{192,224},{224,1... | collective-permute-start | bytes 12296 | tf_op jit(solution)/shard_map/ppermute | solution.py:288
  116.5 3.0 %collective-permute-done.7 = f32[8,128]{1,0:T(8,128)S(1)} collective-permute-done((f32[8,128]{1,0:T(8,128)S(1)}, f32[8,128]{1,0:T(8,128)S(1)}, u32[]{:S(2)}, u32[]{:S(2)}) %collective-permute-start.7) | collective-permute-done | bytes 4128 | tf_op jit(solution)/shard_map/ppermute | solution.py:288
  119.5 0.0 collective-permute-done.9.refs_1_
  119.5 3.6 %collective-permute-start.10 = (bf16[2,3,32,1536]{3,2,1,0:T(8,128)(2,1)S(1)}, bf16[2,3,32,1536]{3,2,1,0:T(8,128)(2,1)S(1)}, u32[]{:S(2)}, u32[]{:S(2)}) collective-permute-start(bf16[2,3,32,1536]{3,2,1,0:T(8,128)(2,1)S(1)} %forward_back_pack.1), channel_id=1, source_target_pairs={{0,8},{1,9},{2,10},{3,11},{4,12},{5,13},{6,14},{7,15},{8,0},{9,1},... | collective-permute-start | bytes 1769480 | tf_op jit(solution)/shard_map/ppermute | solution.py:288
  123.2 4.7 %collective-permute-start.8 = (f32[8,128]{1,0:T(8,128)S(1)}, f32[8,128]{1,0:T(8,128)S(1)}, u32[]{:S(2)}, u32[]{:S(2)}) collective-permute-start(f32[8,128]{1,0:T(8,128)S(1)} %add.15), channel_id=1, source_target_pairs={{0,256},{32,288},{64,320},{96,352},{128,384},{160,416},{192,448},{... | collective-permute-start | bytes 12296 | tf_op jit(solution)/shard_map/ppermute | solution.py:288
  127.9 4.7 %collective-permute-done.8 = f32[8,128]{1,0:T(8,128)S(1)} collective-permute-done((f32[8,128]{1,0:T(8,128)S(1)}, f32[8,128]{1,0:T(8,128)S(1)}, u32[]{:S(2)}, u32[]{:S(2)}) %collective-permute-start.8) | collective-permute-done | bytes 4128 | tf_op jit(solution)/shard_map/ppermute | solution.py:288
  132.6 0.0 all-to-all-done.1.got
  132.6 0.7 broadcast_in_dim.30
  133.2 5.9 %all-to-all-start.2 = ((f32[32,8,128]{2,1,0:T(8,128)}), f32[32,8,128]{2,1,0:T(8,128)S(1)}, u32[]{:S(2)}, u32[]{:S(2)}) async-start(f32[32,8,128]{2,1,0:T(8,128)} %broadcast_in_dim.30), calls=%async_computation.2 | async-start | bytes 262144 | tf_op jit(solution)/shard_map/all_to_all | solution.py:297
  139.2 6.6 %collective-permute-done.10.refs_2_ = bf16[2,3,32,1536]{3,2,1,0:T(8,128)(2,1)S(1)} collective-permute-done((bf16[2,3,32,1536]{3,2,1,0:T(8,128)(2,1)S(1)}, bf16[2,3,32,1536]{3,2,1,0:T(8,128)(2,1)S(1)}, u32[]{:S(2)}, u32[]{:S(2)}) %collective-permute-start.10) | collective-permute-done | bytes 589856 | tf_op jit(solution)/shard_map/ppermute | solution.py:288
  145.8 1.1 temporal_unpack.1
  146.9 2.5 %spatial_unpack.1 = (bf16[128,1536]{1,0:T(8,128)(2,1)}, bf16[128,1536]{1,0:T(8,128)(2,1)}, bf16[128,1536]{1,0:T(8,128)(2,1)}) custom-call(bf16[8,576,128]{2,1,0:T(8,128)(2,1)} %all-to-all-done.1.got), custom_call_target="tpu_custom_call" | custom-call | tf_op jit(solution)/shard_map/spatial_unpack/pallas_call | solution.py:393
  149.3 0.7 all-to-all-done.2
  150.1 0.6 slice_multiply_fusion
  (6 shorter events, 0.1 us)
Async XLA Ops:
  3.2 7.5 %copy-start = (bf16[1,128,1536]{2,1,0:T(8,128)(2,1)S(1)}, bf16[1,128,1536]{2,1,0:T(8,128)(2,1)}, u32[]{:S(2)}) copy-start(bf16[1,128,1536]{2,1,0:T(8,128)(2,1)} %param.14) | copy-start | bytes 1179652
  3.2 7.5 %copy-start.1 = (bf16[1,128,1536]{2,1,0:T(8,128)(2,1)S(1)}, bf16[1,128,1536]{2,1,0:T(8,128)(2,1)}, u32[]{:S(2)}) copy-start(bf16[1,128,1536]{2,1,0:T(8,128)(2,1)} %param.11) | copy-start | bytes 1179652
  3.2 7.5 %copy-start.2 = (bf16[1,128,1536]{2,1,0:T(8,128)(2,1)S(1)}, bf16[1,128,1536]{2,1,0:T(8,128)(2,1)}, u32[]{:S(2)}) copy-start(bf16[1,128,1536]{2,1,0:T(8,128)(2,1)} %param.12) | copy-start | bytes 1179652
  3.3 7.4 %copy-start.3 = (bf16[1,128,1536]{2,1,0:T(8,128)(2,1)S(1)}, bf16[1,128,1536]{2,1,0:T(8,128)(2,1)}, u32[]{:S(2)}) copy-start(bf16[1,128,1536]{2,1,0:T(8,128)(2,1)} %param.13) | copy-start | bytes 1179652
  3.3 45.2 %all-to-all-start = ((bf16[8,768,128]{2,1,0:T(8,128)(2,1)}), bf16[8,768,128]{2,1,0:T(8,128)(2,1)S(1)}, u32[]{:S(2)}, u32[]{:S(2)}) async-start(bf16[8,768,128]{2,1,0:T(8,128)(2,1)} %bitcast.24), calls=%async_computation | async-start | bytes 3145728 | tf_op jit(solution)/shard_map/all_to_all | solution.py:314
  12.9 48.8 %copy-start.4 = (f32[4,128]{1,0:T(4,128)S(1)}, f32[4,128]{1,0:T(4,128)}, u32[]{:S(2)}) copy-start(f32[4,128]{1,0:T(4,128)} %gains.1) | copy-start | bytes 6148
  12.9 23.3 %collective-permute-start = (bf16[2,4,32,1536]{3,2,1,0:T(8,128)(2,1)S(1)}, bf16[2,4,32,1536]{3,2,1,0:T(8,128)(2,1)S(1)}, u32[]{:S(2)}, u32[]{:S(2)}) collective-permute-start(bf16[2,4,32,1536]{3,2,1,0:T(8,128)(2,1)S(1)} %get-tuple-element.33), channel_id=1, source_target_pairs={{0,16},{1,17},{2,18},{3,19},{4,20},{5,21},{6,22},{7,23},{8,24},{9,... | collective-permute-start | bytes 2359304 | tf_op jit(solution)/shard_map/ppermute | solution.py:288
  48.5 44.0 %collective-permute-start.4 = (bf16[2,4,32,1536]{3,2,1,0:T(8,128)(2,1)S(1)}, bf16[2,4,32,1536]{3,2,1,0:T(8,128)(2,1)}, u32[]{:S(2)}, u32[]{:S(2)}) collective-permute-start(bf16[2,4,32,1536]{3,2,1,0:T(8,128)(2,1)S(1)} %forward_pack.1), channel_id=1, source_target_pairs={{0,8},{1,9},{2,10},{3,11},{4,12},{5,13},{6,14},{7,15},{8,0},{9,1},... | collective-permute-start | bytes 2359304 | tf_op jit(solution)/shard_map/ppermute | solution.py:288
  57.6 4.1 %collective-permute-start.1 = (bf16[8,2,128,128]{3,2,1,0:T(8,128)(2,1)}, bf16[8,2,128,128]{3,2,1,0:T(8,128)(2,1)}, u32[]{:S(2)}, u32[]{:S(2)}) collective-permute-start(bf16[8,2,128,128]{3,2,1,0:T(8,128)(2,1)} %slice.6), channel_id=1, source_target_pairs={{0,1},{1,0},{2,3},{3,2},{4,5},{5,4},{6,7},{7,6},{8,9},{9,8},{10,11... | collective-permute-start | bytes 1572872 | tf_op jit(solution)/shard_map/ppermute | solution.py:288
  77.0 3.0 %collective-permute-start.2 = (f32[4,128]{1,0:T(4,128)S(1)}, f32[4,128]{1,0:T(4,128)S(1)}, u32[]{:S(2)}, u32[]{:S(2)}) collective-permute-start(f32[4,128]{1,0:T(4,128)S(1)} %copy-done.4), channel_id=1, source_target_pairs={{0,1},{1,0},{2,3},{3,2},{4,5},{5,4},{6,7},{7,6},{8,9},{9,8},{10,11... | collective-permute-start | bytes 6152 | tf_op jit(solution)/shard_map/ppermute | solution.py:288
  80.1 3.0 %collective-permute-start.3 = (f32[4,128]{1,0:T(4,128)S(1)}, f32[4,128]{1,0:T(4,128)S(1)}, u32[]{:S(2)}, u32[]{:S(2)}) collective-permute-start(f32[4,128]{1,0:T(4,128)S(1)} %collective-permute-done.2), channel_id=1, source_target_pairs={{0,1},{1,0},{2,3},{3,2},{4,5},{5,4},{6,7},{7,6},{8,9},{9,8},{10,11... | collective-permute-start | bytes 6152 | tf_op jit(solution)/shard_map/ppermute | solution.py:288
  83.1 49.5 %all-to-all-start.1 = ((bf16[8,576,128]{2,1,0:T(8,128)(2,1)}), bf16[8,576,128]{2,1,0:T(8,128)(2,1)}, u32[]{:S(2)}, u32[]{:S(2)}) async-start(bf16[8,576,128]{2,1,0:T(8,128)(2,1)} %get-tuple-element.45), calls=%async_computation.1 | async-start | bytes 2359296 | tf_op jit(solution)/shard_map/all_to_all | solution.py:314
  97.2 22.3 %collective-permute-start.9 = (bf16[2,3,32,1536]{3,2,1,0:T(8,128)(2,1)S(1)}, bf16[2,3,32,1536]{3,2,1,0:T(8,128)(2,1)S(1)}, u32[]{:S(2)}, u32[]{:S(2)}) collective-permute-start(bf16[2,3,32,1536]{3,2,1,0:T(8,128)(2,1)S(1)} %get-tuple-element.51), channel_id=1, source_target_pairs={{0,16},{1,17},{2,18},{3,19},{4,20},{5,21},{6,22},{7,23},{8,24},{9,... | collective-permute-start | bytes 1769480 | tf_op jit(solution)/shard_map/ppermute | solution.py:288
  102.1 5.5 %collective-permute-start.5 = (f32[8,128]{1,0:T(8,128)S(1)}, f32[8,128]{1,0:T(8,128)S(1)}, u32[]{:S(2)}, u32[]{:S(2)}) collective-permute-start(f32[8,128]{1,0:T(8,128)S(1)} %get-tuple-element.43), channel_id=1, source_target_pairs={{0,64},{32,96},{64,0},{96,32},{128,192},{160,224},{192,128},{224,1... | collective-permute-start | bytes 12296 | tf_op jit(solution)/shard_map/ppermute | solution.py:288
  107.6 6.4 %collective-permute-start.6 = (f32[8,128]{1,0:T(8,128)S(1)}, f32[8,128]{1,0:T(8,128)S(1)}, u32[]{:S(2)}, u32[]{:S(2)}) collective-permute-start(f32[8,128]{1,0:T(8,128)S(1)} %add.13), channel_id=1, source_target_pairs={{0,128},{32,160},{64,192},{96,224},{128,0},{160,32},{192,64},{224,... | collective-permute-start | bytes 12296 | tf_op jit(solution)/shard_map/ppermute | solution.py:288
  114.0 5.5 %collective-permute-start.7 = (f32[8,128]{1,0:T(8,128)S(1)}, f32[8,128]{1,0:T(8,128)S(1)}, u32[]{:S(2)}, u32[]{:S(2)}) collective-permute-start(f32[8,128]{1,0:T(8,128)S(1)} %add.14), channel_id=1, source_target_pairs={{0,32},{32,0},{64,96},{96,64},{128,160},{160,128},{192,224},{224,1... | collective-permute-start | bytes 12296 | tf_op jit(solution)/shard_map/ppermute | solution.py:288
  119.5 26.2 %collective-permute-start.10 = (bf16[2,3,32,1536]{3,2,1,0:T(8,128)(2,1)S(1)}, bf16[2,3,32,1536]{3,2,1,0:T(8,128)(2,1)S(1)}, u32[]{:S(2)}, u32[]{:S(2)}) collective-permute-start(bf16[2,3,32,1536]{3,2,1,0:T(8,128)(2,1)S(1)} %forward_back_pack.1), channel_id=1, source_target_pairs={{0,8},{1,9},{2,10},{3,11},{4,12},{5,13},{6,14},{7,15},{8,0},{9,1},... | collective-permute-start | bytes 1769480 | tf_op jit(solution)/shard_map/ppermute | solution.py:288
  123.2 9.4 %collective-permute-start.8 = (f32[8,128]{1,0:T(8,128)S(1)}, f32[8,128]{1,0:T(8,128)S(1)}, u32[]{:S(2)}, u32[]{:S(2)}) collective-permute-start(f32[8,128]{1,0:T(8,128)S(1)} %add.15), channel_id=1, source_target_pairs={{0,256},{32,288},{64,320},{96,352},{128,384},{160,416},{192,448},{... | collective-permute-start | bytes 12296 | tf_op jit(solution)/shard_map/ppermute | solution.py:288
  133.2 16.8 %all-to-all-start.2 = ((f32[32,8,128]{2,1,0:T(8,128)}), f32[32,8,128]{2,1,0:T(8,128)S(1)}, u32[]{:S(2)}, u32[]{:S(2)}) async-start(f32[32,8,128]{2,1,0:T(8,128)} %broadcast_in_dim.30), calls=%async_computation.2 | async-start | bytes 262144 | tf_op jit(solution)/shard_map/all_to_all | solution.py:297
